TPU v7x, 512 devices: a whole 4x4x16 slice. The times are simulated.
512 devices in a mesh: space: 32 (over z, core), member: 16 (over y, x).
Axes of the slice: x: 4, y: 4, z: 16, core: 2. Of those that a mesh axis runs over, the one named last changes fastest.
Arguments:
- ensemble: bfloat16 [524288, 256], P('space', 'member'), may hold values from -20 to 20
- operator_blocks: bfloat16 [2048, 8, 128, 128], P('space')
- block_columns: int32 [2048, 8], P('space'), may hold values from 0 to 4095, as said below
- observed: float32 [262144], P('space')
- error_scale: float32 [262144], P('space'), as said below
Outputs:
- analysis: bfloat16 [524288, 256], P('space', 'member')
Inputs may be any that keep to these rules, and one draw needn't show every extreme that they name: `block_columns`: block row r reads state blocks 128 * (r // 64) - 1 + j modulo 4096, 0 <= j <= 129; its first entry has j = 0 and its second j = 129. `error_scale`: Positive.
All inputs are finite; a program needn't handle non-finite values.
Results may differ from a plain program's by a relative error of at most 0.0059.
Values may be sent and summed in bfloat16 or wider, within the bound.
No kernel may reach another device: no remote copies, remote signals or barrier semaphores. Data moves between devices by JAX's collectives and lax.ppermute only.
A program may use at most 128 MiB of HBM per device.

v0:
```python
import math

import jax
import jax.numpy as jnp
from jax import lax
from jax.sharding import PartitionSpec as P


def padded_2(cells, sides, width):
    for axis, dim in sides:
        count = lax.axis_size(axis)
        head = lax.slice_in_dim(cells, 0, width, axis=dim)
        tail = lax.slice_in_dim(cells, cells.shape[dim] - width, cells.shape[dim], axis=dim)
        cells = jnp.concatenate(
            [
                lax.ppermute(tail, axis, [(i, (i + 1) % count) for i in range(count)]),
                cells,
                lax.ppermute(head, axis, [((i + 1) % count, i) for i in range(count)]),
            ],
            axis=dim,
        )
    return cells


def local(ensemble, operator_blocks, block_columns, observed, error_scale):
    row_count, member_local = ensemble.shape
    block_size = operator_blocks.shape[2]
    space_count = lax.axis_size("space")
    member_count = lax.axis_size("member")
    member_total = member_local * member_count
    member_index = lax.axis_index("member")
    padded = padded_2(ensemble, (("space", 0),), block_size)
    state_local = row_count // block_size
    local_cols = jnp.mod(
        block_columns - lax.axis_index("space") * state_local + 1, state_local * space_count
    )
    grouped = padded.reshape(state_local + 2, block_size, member_local)
    picked = grouped[local_cols]
    predicted = jnp.einsum(
        "okij,okjm->oim", operator_blocks, picked, preferred_element_type=jnp.float32
    ).reshape(-1, member_local)
    totals = lax.psum(
        (jnp.sum(ensemble, axis=1, dtype=jnp.float32), jnp.sum(predicted, axis=1)), "member"
    )
    mean_state = totals[0] / member_total
    mean_pred = totals[1] / member_total
    root_scale = math.sqrt(member_total - 1)
    whitened = (predicted - mean_pred[:, None]) / (error_scale * root_scale)[:, None]
    departure = (observed - mean_pred) / (error_scale * root_scale)
    panel_all = lax.all_gather(whitened, "member", axis=1, tiled=True)
    gram_part = jnp.dot(panel_all.T, panel_all, precision=lax.Precision.HIGHEST)
    cross_part = jnp.dot(departure, panel_all, precision=lax.Precision.HIGHEST)
    identity = jnp.eye(member_total, dtype=jnp.float32)
    gram_sum, cross_term = lax.psum((gram_part, cross_part), "space")
    lower_factor = jnp.linalg.cholesky(identity + gram_sum)
    weight_mean = jax.scipy.linalg.cho_solve((lower_factor, True), cross_term)
    inverse_lower = jax.scipy.linalg.solve_triangular(lower_factor, identity, lower=True)
    transform = (inverse_lower.T + weight_mean[:, None]).astype(jnp.bfloat16)
    anomalies = (ensemble.astype(jnp.float32) - mean_state[:, None]).astype(jnp.bfloat16)
    my_cols = lax.dynamic_slice_in_dim(transform, member_index * member_local, member_local, 1)
    update = jnp.dot(
        lax.all_gather(anomalies, "member", axis=1, tiled=True),
        my_cols,
        preferred_element_type=jnp.float32,
    )
    return (mean_state[:, None] + update).astype(jnp.bfloat16)


def solution(mesh):
    in_specs = (
        P("space", "member"),
        P("space", None, None, None),
        P("space", None),
        P("space"),
        P("space"),
    )
    out_specs = P("space", "member")
    return jax.shard_map(local, mesh=mesh, in_specs=in_specs, out_specs=out_specs, check_vma=False)
```

profile of v0, /device:TPU:1, one launch (start us, length us, event | category | flops | bytes accessed | tf_op | source)
XLA Modules:
  0.0 536.4 jit_solution(817467369546225089)
XLA Ops:
  7.2 3.0 collective-permute-start
  10.3 3.9 collective-permute-start.1
  14.1 1.8 convert_reduce_fusion
  17.0 1.1 copy_bitcast_fusion
  18.1 2.0 gather_fusion
  20.2 8.1 %bitcast_reduce_fusion = (f32[64,128]{1,0:T(8,128)S(1)}, f32[64,16,128,1]{2,1,3,0:T(8,128)S(1)}) fusion(bf16[64,8,128,16]{2,3,1,0:T(8,128)(2,1)S(1)} %bitcast.102, bf16[64,8,128,128]{3,2,1,0:T(8,128)(2,1)} %param.6), kind=kOutput, calls=%fused_computation.23 | convolution fusion | flops 268558336 | bytes 19431424 | tf_op jit(solution)/shard_map/okij,okjm->oim/dot_general | solution.py:39
  28.3 57.3 %psum.29 = f32[8192]{0:T(1024)S(1)} all-reduce(f32[8192]{0:T(1024)S(1)} %bitcast.103), channel_id=1, replica_groups=mesh['space'=32,'member'=16] {'member'}, use_global_device_ids=true, to_apply=%region_3.4 | all-reduce | flops 8192 | bytes 65536 | tf_op jit(solution)/shard_map/psum | solution.py:42
  86.5 41.1 %all-reduce.4.cloned.1.call-done = f32[16384]{0:T(1024)} async-done(((f32[16384]{0:T(1024)}), f32[16384]{0:T(1024)}) %all-reduce.4.cloned.1.call-update) | async-done | bytes 65552 | tf_op jit(solution)/shard_map/psum | solution.py:42
  128.5 89.7 %all-gather.5.cloned.1.call-done = f32[8192,256]{0,1:T(8,128)} async-done(((f32[8192,16]{0,1:T(8,128)}), f32[8192,256]{0,1:T(8,128)}) %all-gather.5.cloned.1.call-update) | async-done | bytes 8388624 | tf_op jit(solution)/shard_map/all_gather | solution.py:50
  218.2 11.2 %fusion.29 = f32[256,256]{0,1:T(8,128)} fusion(f32[8192,256]{0,1:T(8,128)} %all-gather.5.cloned.1.call-done), kind=kOutput, calls=%fused_computation.76 | convolution fusion | flops 6442450944 | bytes 8650752 | tf_op jit(solution)/shard_map/dot_general | solution.py:51
  230.5 8.9 %fusion.30 = f32[1,256]{1,0:T(1,128)S(1)} fusion(f32[8192,1]{0,1:T(1,128)S(1)} %bitcast.104, f32[8192,256]{0,1:T(8,128)} %all-gather.5.cloned.1.call-done), kind=kOutput, calls=%fused_computation.77 | convolution fusion | flops 25165824 | bytes 8422400 | tf_op jit(solution)/shard_map/dot_general | solution.py:52
  239.4 47.2 %psum.31 = f32[256]{0:T(256)S(1)} all-reduce(f32[256]{0:T(256)S(1)} %bitcast.106), channel_id=1, replica_groups=mesh['space'=32,'member'=16] {'space'}, use_global_device_ids=true, to_apply=%region_9.10 | all-reduce | flops 256 | bytes 2048 | tf_op jit(solution)/shard_map/psum | solution.py:54
  286.7 149.0 %all-reduce.6.cloned.1.call-done = f32[256,256]{0,1:T(8,128)} async-done(((f32[256,256]{0,1:T(8,128)}), f32[256,256]{0,1:T(8,128)}) %all-reduce.6.cloned.1.call-update) | async-done | bytes 262160 | tf_op jit(solution)/shard_map/psum | solution.py:54
  435.6 1.0 convert_add_fusion
  436.8 1.0 fusion.7
  437.8 11.7 %cholesky.50 = f32[128,128]{1,0:T(8,128)S(1)} custom-call(f32[128,128]{1,0:T(8,128)S(1)} %cholesky.118), custom_call_target="Cholesky" | custom-call | tf_op jit(solution)/shard_map/jit(cholesky)/cholesky | solution.py:55
  449.5 9.8 %custom-call.21 = f32[1,128,128]{1,2,0:T(8,128)S(1)} custom-call(f32[1,128,128]{2,1,0:T(8,128)S(1)} %get-tuple-element.28), custom_call_target="InvertDiagBlocksLowerTriangular" | custom-call | tf_op jit(solution)/shard_map/jit(cholesky)/cholesky | solution.py:55
  459.8 11.7 %cholesky.105 = f32[128,128]{1,0:T(8,128)S(1)} custom-call(f32[128,128]{1,0:T(8,128)S(1)} %convolution_subtract_fusion.1), custom_call_target="Cholesky" | custom-call | tf_op jit(solution)/shard_map/jit(cholesky)/cholesky | solution.py:55
  473.6 3.7 while.1
  474.1 1.3 bitcast_dynamic-update-slice_fusion.2
  476.0 1.3 bitcast_dynamic-update-slice_fusion.2
  477.3 19.9 %custom-call.22 = f32[2,128,128]{1,2,0:T(8,128)S(1)} custom-call(f32[2,128,128]{2,1,0:T(8,128)S(1)} %get-tuple-element.12), custom_call_target="InvertDiagBlocksLowerTriangular" | custom-call | tf_op jit(solution)/shard_map/jit(_solve_triangular)/triangular_solve | solution.py:57
  499.4 25.1 %all-gather.3.cloned.1.call-done = bf16[16384,256]{0,1:T(8,128)(2,1)} async-done(((bf16[16384,16]{0,1:T(8,128)(2,1)}), bf16[16384,256]{0,1:T(8,128)(2,1)}) %all-gather.3.cloned.1.call-update) | async-done | bytes 8388624 | tf_op jit(solution)/shard_map/all_gather | solution.py:62
  524.5 5.4 %fusion = bf16[16384,16]{0,1:T(8,128)(2,1)} fusion(bf16[16384,256]{0,1:T(8,128)(2,1)} %all-gather.3.cloned.1.call-done, f32[16384]{0:T(1024)S(1)} %broadcast_multiply_fusion, s32[]{:T(128)S(6)} %select_n.20, f32[128,256]{1,0:T(8,128)S(1)} %fusion.15, f32[128,256]{1,0:T(8,128)S(1)} %fusion.8, f32[256]{0:T(256)S(1)} %bitcast.105), kind=kOutput, calls=%fused_computation.4 | convolution fusion | flops 134754304 | bytes 9241604 | tf_op jit(solution)/shard_map/dot_general | solution.py:61
  (53 shorter events, 9.2 us)
Async XLA Ops:
  6.5 121.1 %all-reduce.4.cloned.1.call-start = ((), (), s32[]{:S(2)}) async-start(), calls=%async_computation | async-start | bytes 131072 | tf_op jit(solution)/shard_map/psum | solution.py:42
  7.2 9.7 %collective-permute-start = (bf16[128,16]{0,1:T(8,128)(2,1)S(1)}, bf16[128,16]{0,1:T(8,128)(2,1)S(1)}, u32[]{:S(2)}, u32[]{:S(2)}) collective-permute-start(bf16[128,16]{0,1:T(8,128)(2,1)S(1)} %get-tuple-element.23), channel_id=1, source_target_pairs={{0,16},{16,32},{32,48},{48,64},{64,80},{80,96},{96,112},{112,128},... | collective-permute-start | bytes 12296 | tf_op jit(solution)/shard_map/ppermute | solution.py:16
  10.3 6.7 %collective-permute-start.1 = (bf16[128,16]{0,1:T(8,128)(2,1)S(1)}, bf16[128,16]{0,1:T(8,128)(2,1)S(1)}, u32[]{:S(2)}, u32[]{:S(2)}) collective-permute-start(bf16[128,16]{0,1:T(8,128)(2,1)S(1)} %get-tuple-element.24), channel_id=1, source_target_pairs={{16,0},{32,16},{48,32},{64,48},{80,64},{96,80},{112,96},{128,112},... | collective-permute-start | bytes 12296 | tf_op jit(solution)/shard_map/ppermute | solution.py:18
  16.0 202.3 %all-gather.5.cloned.1.call-start = ((), (), s32[]{:S(2)}) async-start(), calls=%async_computation.2 | async-start | bytes 8912896 | tf_op jit(solution)/shard_map/all_gather | solution.py:50
  20.1 65.4 %copy-start.1 = (f32[8192]{0:T(1024)S(1)}, f32[8192]{0:T(1024)}, u32[]{:S(2)}) copy-start(f32[8192]{0:T(1024)} %param.8) | copy-start | bytes 98308
  20.1 65.4 %copy-start.2 = (f32[8192]{0:T(1024)S(1)}, f32[8192]{0:T(1024)}, u32[]{:S(2)}) copy-start(f32[8192]{0:T(1024)} %param.9) | copy-start | bytes 98308
  86.5 349.2 %all-reduce.6.cloned.1.call-start = ((), (), s32[]{:S(2)}) async-start(), calls=%async_computation.3 | async-start | bytes 524288 | tf_op jit(solution)/shard_map/psum | solution.py:54
  128.5 101.0 %copy-start = (bf16[16384,16]{0,1:T(8,128)(2,1)S(1)}, bf16[16384,16]{0,1:T(8,128)(2,1)}, u32[]{:S(2)}) copy-start(bf16[16384,16]{0,1:T(8,128)(2,1)} %param.5) | copy-start | bytes 1572868
  229.5 295.0 %all-gather.3.cloned.1.call-start = ((), (), s32[]{:S(2)}) async-start(), calls=%async_computation.1 | async-start | bytes 8912896 | tf_op jit(solution)/shard_map/all_gather | solution.py:62
Sparse Core Ops, SparseCore 0:
  16.1 111.4 all-reduce.3
  131.1 87.0 all-gather.4
  229.6 205.9 all-reduce.5
  438.5 85.9 all-gather.2
where the time goes:
time: 537 us; the launch traced here: 536 us
  waiting for transfers between devices  305 us (57%)
  blocking collectives  105 us (20%)
  other arithmetic  62.2 us (12%)
  matrix products  36.2 us (7%)
  between operations  14.5 us (3%)
  starting transfers between devices  7.01 us (1%)
  local copies, waits for them, and re-layouts  6.85 us (1%)
    psum x1, waiting for transfers between devices, local(): gram_sum, cross_term = lax.psum((gram_part, cross_part), 'space')  149 us
    all_gather x1, waiting for transfers between devices, local(): panel_all = lax.all_gather(whitened, 'member', axis=1, tiled=True)  89.7 us
    psum x1, blocking collectives, local(): lax.psum((jnp.sum(ensemble, axis=1, dtype=jnp.float32), jnp.sum(predicted...  57.3 us
    psum x1, blocking collectives, local(): gram_sum, cross_term = lax.psum((gram_part, cross_part), 'space')  47.2 us
    psum x1, waiting for transfers between devices, local(): lax.psum((jnp.sum(ensemble, axis=1, dtype=jnp.float32), jnp.sum(predicted...  41.1 us
    another operation x6, other arithmetic, local(): lower_factor = jnp.linalg.cholesky(identity + gram_sum)  34 us
    all_gather x1, waiting for transfers between devices, local(): lax.all_gather(anomalies, 'member', axis=1, tiled=True)  25.1 us
    another operation x3, other arithmetic, local(): jax.scipy.linalg.solve_triangular(lower_factor, identity, lower=True)  19.9 us
  transfers between devices with their start and end apart: 6, of which 4 were waited for; matrix products, arithmetic and copies ran while one was open for 16% of the time, Pallas kernels for 0%

commit v1 on v0

v1 whole, which is shorter than its diff:
```python
import functools
import math

import jax
import jax.numpy as jnp
from jax import lax
from jax.experimental import pallas as pl
from jax.experimental.pallas import tpu as pltpu
from jax.sharding import Mesh
from jax.sharding import PartitionSpec as P

F32, BF16 = jnp.float32, jnp.bfloat16
HIGHEST = lax.Precision.HIGHEST
NT = (((1,), (1,)), ((), ()))
TN = (((0,), (0,)), ((), ()))
PLANE = ("core", "y", "x")
MEMBER = ("y", "x")
SPACE = ("z", "core")


def predict_kernel(group, cols_ref, ens_ref, left_ref, right_ref, ops_ref, out_ref, blocks):
    step = pl.program_id(0)
    count = ens_ref.shape[1] // 128

    @pl.when(step == 0)
    def _():
        blocks[0] = left_ref[...]
        blocks[count + 1] = right_ref[...]
        for j in range(count):
            blocks[j + 1] = ens_ref[:, 128 * j : 128 * (j + 1)]

    for o in range(group):
        picked = jnp.concatenate([blocks[cols_ref[step * group + o, k]] for k in range(8)], axis=1)
        weights = jnp.concatenate([ops_ref[o, k] for k in range(8)], axis=1)
        part = lax.dot_general(weights, picked, NT, preferred_element_type=F32)
        out_ref[:, 128 * o : 128 * (o + 1)] = part.T


def predict(cols, ens_t, left, right, ops, group=8):
    members, rows = ens_t.shape
    oblocks = ops.shape[0]
    whole = lambda shape: pl.BlockSpec(shape, lambda i, c: (0, 0))
    return pl.pallas_call(
        functools.partial(predict_kernel, group),
        out_shape=jax.ShapeDtypeStruct((members, oblocks * 128), F32),
        grid_spec=pltpu.PrefetchScalarGridSpec(
            num_scalar_prefetch=1,
            grid=(oblocks // group,),
            in_specs=[
                whole(ens_t.shape),
                whole(left.shape),
                whole(right.shape),
                pl.BlockSpec((group, 8, 128, 128), lambda i, c: (i, 0, 0, 0)),
            ],
            out_specs=pl.BlockSpec((members, group * 128), lambda i, c: (0, i)),
            scratch_shapes=[pltpu.VMEM((rows // 128 + 2, members, 128), BF16)],
        ),
        compiler_params=pltpu.CompilerParams(vmem_limit_bytes=24 * 2**20),
        cost_estimate=pl.CostEstimate(flops=2 * ops.size * members, bytes_accessed=2 * ops.size, transcendentals=0),
    )(cols, ens_t, left, right, ops)


def gram_kernel(pred_ref, obs_ref, err_ref, out_ref):
    total, half = pred_ref.shape[0], pred_ref.shape[0] // 2
    pred = pred_ref[...]
    mean = jnp.sum(pred, axis=0, keepdims=True) / total
    scale = err_ref[...] * math.sqrt(total - 1)
    white = (pred - mean) / scale
    departure = (obs_ref[...] - mean) / scale
    row = lax.broadcasted_iota(jnp.int32, (half, white.shape[1]), 0)
    first = jnp.where(row == 0, departure, 0.0)
    second = jnp.where(row == 1, departure, 0.0)
    top, low = white[:half], white[half:]
    dot = functools.partial(lax.dot_general, dimension_numbers=NT, precision=HIGHEST, preferred_element_type=F32)
    out_ref[:half, :half] = dot(top, top)
    out_ref[:half, half:] = dot(top, first) + dot(low, second)
    out_ref[half:, :] = dot(low, white)


def gram(pred, obs, err):
    total = pred.shape[0]
    return pl.pallas_call(
        gram_kernel,
        out_shape=jax.ShapeDtypeStruct((total, total), F32),
        compiler_params=pltpu.CompilerParams(vmem_limit_bytes=24 * 2**20),
    )(pred, obs, err)


WIDE = 32


def spread(column):
    return jnp.broadcast_to(column, (8, 128))


def eliminate(panel, col0):
    groups = WIDE // 8
    sub = lax.broadcasted_iota(jnp.int32, (8, 128), 0)
    tile = col0 // 128
    lanes = lax.broadcasted_iota(jnp.int32, (8, 128), 1) + 128 * tile
    tiles = panel[0].shape[1] // 128
    panel = [[p[:, 128 * t : 128 * (t + 1)] for t in range(tiles)] for p in panel]
    out = []
    for q in range(groups):
        start = col0 + 8 * q
        at = start - 128 * tile
        coef = [[None if g < q else spread(panel[g][tile][:, at + c : at + c + 1]) for g in range(groups)] for c in range(8)]
        pivots = jnp.ones((8, 128), F32)
        for j in range(8):
            pivot = spread(coef[j][q][j : j + 1, :])
            pivots = jnp.where(sub == j, pivot, pivots)
            ratio = 1.0 / pivot
            ahead = [spread(coef[c][q][j : j + 1, :]) for c in range(8)]
            for g in range(q, groups):
                times = coef[j][g] * ratio
                if g == q:
                    times = jnp.where(sub > j, times, 0.0)
                for c in range(8):
                    if c == j:
                        coef[c][g] = jnp.where(sub == j, 1.0, -times) if g == q else -times
                    else:
                        coef[c][g] = coef[c][g] - times * ahead[c]
        inside = (lanes >= start) & (lanes < start + 8)
        unit = jnp.where(lanes - start == sub, 1.0, 0.0)
        base = [jnp.where(inside, unit, panel[q][t]) if t == tile else panel[q][t] for t in range(tiles)]
        root = lax.rsqrt(pivots)
        rows = [[spread(base[t][c : c + 1, :]) for t in range(tiles)] for c in range(8)]
        low = [jnp.where(sub >= c, coef[c][q], 0.0) for c in range(8)]
        out.append([sum(low[c] * rows[c][t] for c in range(8)) * root for t in range(tiles)])
        for g in range(q + 1, groups):
            for t in range(tiles):
                here = jnp.where(inside, 0.0, panel[g][t]) if t == tile else panel[g][t]
                panel[g][t] = here + sum(coef[c][g] * rows[c][t] for c in range(8))
    return jnp.concatenate([jnp.concatenate(o, axis=1) for o in out], axis=0)


def transform_kernel(mine_ref, gram_ref, out_ref, a):
    total = gram_ref.shape[0]
    half = total // 2
    row = lax.broadcasted_iota(jnp.int32, (total, total), 0)
    col = lax.broadcasted_iota(jnp.int32, (total, total), 1)
    given = gram_ref[...]
    extra = given[:half, half:]
    cross = jnp.concatenate([extra[:, 0:1], extra[:, 1:2]], axis=0)
    mirror = given[half:, :half].T
    full = jnp.concatenate([jnp.concatenate([given[:half, :half], mirror], axis=1), given[half:, :]], axis=0)
    a[...] = full + jnp.where(row == col, 1.0, 0.0)
    for s in range(total // WIDE):
        r0, r1 = WIDE * s, WIDE * (s + 1)
        done = eliminate([a[r0 + 8 * g : r0 + 8 * (g + 1), :] for g in range(WIDE // 8)], r0)
        a[r0:r1, :] = done
        if r1 < total:
            above = (col[r0:r1] < r1) & (col[r0:r1] > row[r0:r1])
            kept = jnp.where(above, 0.0, done)
            update = lax.dot_general(done, kept, TN, precision=HIGHEST, preferred_element_type=F32)
            block = (col[r1:] >= r0) & (col[r1:] < r1)
            a[r1:, :] = jnp.where(block, 0.0, a[r1:, :]) - update[r1:, :]
    inverse = jnp.where(col <= row, a[...], 0.0)
    a[...] = inverse
    solved = jnp.sum(inverse * cross.T, axis=1, keepdims=True)
    weight = jnp.sum(inverse * solved, axis=0, keepdims=True)
    mine = a[pl.ds(pl.multiple_of(mine_ref[0] * 16, 16), 16), :]
    rounded = (mine + weight).astype(BF16).astype(F32)
    centred = rounded - jnp.sum(rounded, axis=1, keepdims=True) / total + 1.0 / total
    high = centred.astype(BF16)
    out_ref[:16] = high
    out_ref[16:] = (centred - high.astype(F32)).astype(BF16)


def transform(mine, gram_sum):
    total = gram_sum.shape[0]
    return pl.pallas_call(
        transform_kernel,
        out_shape=jax.ShapeDtypeStruct((32, total), BF16),
        in_specs=[pl.BlockSpec(memory_space=pltpu.SMEM), pl.BlockSpec(memory_space=pltpu.VMEM)],
        out_specs=pl.BlockSpec(memory_space=pltpu.VMEM),
        scratch_shapes=[pltpu.VMEM((total, total), F32)],
        compiler_params=pltpu.CompilerParams(vmem_limit_bytes=24 * 2**20),
    )(mine, gram_sum)


def update_kernel(left_ref, all_ref, out_ref):
    both = jnp.dot(left_ref[...], all_ref[...], preferred_element_type=F32)
    out_ref[...] = (both[:16] + both[16:]).astype(BF16)


def update(left, everyone, width=2048):
    total, rows = everyone.shape
    return pl.pallas_call(
        update_kernel,
        out_shape=jax.ShapeDtypeStruct((16, rows), BF16),
        grid=(rows // width,),
        in_specs=[pl.BlockSpec(left.shape, lambda i: (0, 0)), pl.BlockSpec((total, width), lambda i: (0, i))],
        out_specs=pl.BlockSpec((16, width), lambda i: (0, i)),
        compiler_params=pltpu.CompilerParams(vmem_limit_bytes=24 * 2**20),
        cost_estimate=pl.CostEstimate(flops=64 * total * rows, bytes_accessed=2 * total * rows, transcendentals=0),
    )(left, everyone)


def to_all(x, axes, count):
    return lax.all_to_all(jnp.broadcast_to(x[None], (count,) + x.shape), axes, 0, 0, tiled=True)


def local(ensemble, operator_blocks, block_columns, observed, error_scale):
    ens_t = ensemble.T
    members, rows = ens_t.shape
    space_count = lax.axis_size(SPACE)
    member_count = lax.axis_size(MEMBER)
    plane_count = lax.axis_size(PLANE)
    z_count = lax.axis_size("z")
    total = members * member_count
    space_index = lax.axis_index(SPACE)
    member_index = lax.axis_index(MEMBER)
    everyone = lax.all_gather(ens_t, MEMBER, axis=0, tiled=True)
    left = lax.ppermute(ens_t[:, -128:], SPACE, [(i, (i + 1) % space_count) for i in range(space_count)])
    right = lax.ppermute(ens_t[:, :128], SPACE, [((i + 1) % space_count, i) for i in range(space_count)])
    state_local = rows // 128
    cols = jnp.mod(block_columns - space_index * state_local + 1, state_local * space_count)
    predicted = predict(cols, ens_t, left, right, operator_blocks)
    predicted = lax.all_to_all(predicted, MEMBER, 1, 0, tiled=True)
    width = predicted.shape[1]
    obs = lax.dynamic_slice_in_dim(observed, member_index * width, width)[None]
    err = lax.dynamic_slice_in_dim(error_scale, member_index * width, width)[None]
    part = gram(predicted, obs, err).reshape(plane_count, -1, total)
    part = jnp.sum(lax.all_to_all(part, PLANE, 0, 0, tiled=True), axis=0)
    part = jnp.sum(to_all(part, "z", z_count), axis=0)
    gram_sum = to_all(part, PLANE, plane_count).reshape(total, total)
    mine = transform(member_index.astype(jnp.int32).reshape(1), gram_sum)
    return update(mine, everyone).T


def solution(mesh):
    fine = Mesh(mesh.devices.reshape(16, 2, 4, 4), ("z", "core", "y", "x"))
    in_specs = (P(SPACE, MEMBER), P(SPACE, None, None, None), P(SPACE, None), P(SPACE), P(SPACE))
    return jax.shard_map(local, mesh=fine, in_specs=in_specs, out_specs=P(SPACE, MEMBER), check_vma=False)
```

time: 537 us -> 135 us (0.25)
  waiting for transfers between devices: 305 us -> 14.5 us
  other arithmetic: 62.2 us -> 0.76 us
  blocking collectives: 105 us -> 57 us
  matrix products: 36.2 us -> 0 us
  Pallas kernels: 0 us -> 23.3 us
  local copies, waits for them, and re-layouts: 6.85 us -> 13.4 us
    psum x2 -> x0, waiting for transfers between devices: 190 us -> none  [the longest x1 149 us: local(): gram_sum, cross_term = lax.psum((gram_part, cross_part), 'space')]
    all_gather x2 -> x1, waiting for transfers between devices: 115 us -> 0.01 us  [local(): everyone = lax.all_gather(ens_t, MEMBER, axis=0, tiled=True)]
    psum x2 -> x0, blocking collectives: 105 us -> none  [the longest x1 57.3 us: local(): lax.psum((jnp.sum(ensemble, axis=1, dtype=jnp.float32), jnp.sum(predicted...]
    all_to_all x0 -> x3, blocking collectives: none -> 57 us  [the longest x2 42.1 us: to_all(): lax.all_to_all(jnp.broadcast_to(x[None], (count,) + x.shape), axes, 0, 0,...]
    another operation x10 -> x0, other arithmetic: 53.9 us -> none  [the longest x6 34 us: local(): lower_factor = jnp.linalg.cholesky(identity + gram_sum)]
    dot_general x4 -> x0, matrix products: 33.6 us -> none  [the longest x1 11.2 us: local(): gram_part = jnp.dot(panel_all.T, panel_all, precision=lax.Precision.HIGHEST)]
    pallas_call x0 -> x4, Pallas kernels: none -> 23.3 us  [the longest x1 10.7 us: transform(): pl.pallas_call(transform_kernel, out_shape=jax.ShapeDtypeStruct((32, tota...]
    all_to_all x0 -> x1, waiting for transfers between devices: none -> 13.8 us  [local(): predicted = lax.all_to_all(predicted, MEMBER, 1, 0, tiled=True)]
  transfers between devices with their start and end apart: 6 -> 4, of which waited for: 4 -> 1; matrix products, arithmetic and copies ran while one was open for 16% -> 3% of each run, Pallas kernels for 0% -> 14%
where the time goes in v1:
time: 135 us; the launch traced here: 134 us
  blocking collectives  57 us (42%)
  Pallas kernels  23.3 us (17%)
  waiting for transfers between devices  14.5 us (11%)
  between operations  13.5 us (10%)
  local copies, waits for them, and re-layouts  13.4 us (10%)
  starting transfers between devices  12 us (9%)
    all_to_all x2, blocking collectives, to_all(): lax.all_to_all(jnp.broadcast_to(x[None], (count,) + x.shape), axes, 0, 0,...  42.1 us
    all_to_all x1, blocking collectives, local(): part = jnp.sum(lax.all_to_all(part, PLANE, 0, 0, tiled=True), axis=0)  14.9 us
    all_to_all x1, waiting for transfers between devices, local(): predicted = lax.all_to_all(predicted, MEMBER, 1, 0, tiled=True)  13.8 us
    pallas_call x1, Pallas kernels, transform(): pl.pallas_call(transform_kernel, out_shape=jax.ShapeDtypeStruct((32, tota...  10.7 us
    unnamed x6, local copies, waits for them, and re-layouts  10.2 us
    pallas_call x1, Pallas kernels, predict(): pl.pallas_call(functools.partial(predict_kernel, group), out_shape=jax.Sh...  7.01 us
    all_to_all x1, starting transfers between devices, local(): predicted = lax.all_to_all(predicted, MEMBER, 1, 0, tiled=True)  5.11 us
    pallas_call x1, Pallas kernels, update(): pl.pallas_call(update_kernel, out_shape=jax.ShapeDtypeStruct((16, rows),...  4.33 us
  transfers between devices with their start and end apart: 4, of which 1 were waited for; matrix products, arithmetic and copies ran while one was open for 3% of the time, Pallas kernels for 14%

profile of v1, /device:TPU:1, one launch (start us, length us, event | category | flops | bytes accessed | tf_op | source)
XLA Modules:
  0.0 134.4 jit_solution(6721690900619151379)
XLA Ops:
  6.5 0.0 all-gather.2.cloned.1.call-start
  6.5 0.7 all-gather.2.cloned.1.call-update
  7.3 0.7 fusion.1
  8.0 3.0 %collective-permute-start = (bf16[16,128]{1,0:T(8,128)(2,1)S(1)}, bf16[16,128]{1,0:T(8,128)(2,1)S(1)}, u32[]{:S(2)}, u32[]{:S(2)}) collective-permute-start(bf16[16,128]{1,0:T(8,128)(2,1)S(1)} %get-tuple-element.6), channel_id=1, source_target_pairs={{0,16},{16,32},{32,48},{48,64},{64,80},{80,96},{96,112},{112,128},... | collective-permute-start | bytes 12296 | tf_op jit(solution)/shard_map/ppermute | solution.py:215
  11.0 3.9 %collective-permute-start.1 = (bf16[16,128]{1,0:T(8,128)(2,1)S(1)}, bf16[16,128]{1,0:T(8,128)(2,1)S(1)}, u32[]{:S(2)}, u32[]{:S(2)}) collective-permute-start(bf16[16,128]{1,0:T(8,128)(2,1)S(1)} %get-tuple-element.5), channel_id=1, source_target_pairs={{16,0},{32,16},{48,32},{64,48},{80,64},{96,80},{112,96},{128,112},... | collective-permute-start | bytes 12296 | tf_op jit(solution)/shard_map/ppermute | solution.py:216
  14.8 0.7 broadcast_subtract_fusion
  15.5 0.1 copy.12
  15.6 0.0 collective-permute-done.left_ref
  15.7 0.0 collective-permute-done.1.right_ref
  15.7 5.8 %copy-done = bf16[64,8,128,128]{3,2,1,0:T(8,128)(2,1)S(1)} copy-done((bf16[64,8,128,128]{3,2,1,0:T(8,128)(2,1)S(1)}, bf16[64,8,128,128]{3,2,1,0:T(8,128)(2,1)}, u32[]{:S(2)}) %copy-start) | copy-done | bytes 16777240
  21.4 1.0 copy-done.2
  22.5 7.0 %shard_map.55 = f32[16,8192]{1,0:T(8,128)S(1)} custom-call(s32[64,8]{1,0:T(8,128)S(1)} %add_select_fusion.cols_ref, bf16[16,16384]{1,0:T(8,128)(2,1)S(1)} %bitcast.16, bf16[16,128]{1,0:T(8,128)(2,1)S(1)} %collective-permute-done.left_ref, bf16[16,128]{1,0:T(8,128)(2,1)S(1)} %collective-permute-done.1.right_ref, bf16[64,8,128,128]{3,2,1,0:T(8,128)(2,1)S(1)} %copy-done), custom_call_target="tpu_custom_call" | custom-call | flops 268435456 | bytes 16777216 | tf_op jit(solution)/shard_map/pallas_call | solution.py:43
  29.5 0.8 copy.16
  30.3 5.1 %all-to-all-start = ((f32[16,16,512]{2,0,1:T(8,128)}), f32[16,16,512]{2,0,1:T(8,128)S(1)}, u32[]{:S(2)}, u32[]{:S(2)}) async-start(f32[16,16,512]{2,0,1:T(8,128)} %bitcast.13), calls=%async_computation | async-start | bytes 1048576 | tf_op jit(solution)/shard_map/all_to_all | solution.py:220
  35.5 0.8 dynamic_slice.6
  36.2 0.8 dynamic_slice.7
  37.0 13.8 %all-to-all-done = f32[16,16,512]{2,0,1:T(8,128)S(1)} async-done(((f32[16,16,512]{2,0,1:T(8,128)}), f32[16,16,512]{2,0,1:T(8,128)S(1)}, u32[]{:S(2)}, u32[]{:S(2)}) %all-to-all-start) | async-done | bytes 524320 | tf_op jit(solution)/shard_map/all_to_all | solution.py:220
  50.7 1.3 shard_map.56
  52.0 14.9 %all_to_all.34 = f32[32,8,256]{2,1,0:T(8,128)S(1)} all-to-all(f32[32,8,256]{2,1,0:T(8,128)S(1)} %bitcast.19), channel_id=1, replica_groups=mesh['z'=16,'core'=2,'y'=4,'x'=4] {'core','y','x'}, dimensions={0} | all-to-all | bytes 524288 | tf_op jit(solution)/shard_map/all_to_all | solution.py:225
  67.0 24.1 %all_to_all.35 = f32[16,8,256]{2,1,0:T(8,128)S(1)} all-to-all(f32[16,8,256]{2,1,0:T(8,128)S(1)} %broadcast_in_dim.20), channel_id=1, replica_groups=mesh['z'=16,'core'=2,'y'=4,'x'=4] {'z'}, dimensions={0} | all-to-all | bytes 262144 | tf_op jit(solution)/shard_map/all_to_all | solution.py:201
  91.1 18.0 %all_to_all.36 = f32[32,8,256]{2,1,0:T(8,128)S(1)} all-to-all(f32[32,8,256]{2,1,0:T(8,128)S(1)} %broadcast_in_dim.21), channel_id=1, replica_groups=mesh['z'=16,'core'=2,'y'=4,'x'=4] {'core','y','x'}, dimensions={0} | all-to-all | bytes 524288 | tf_op jit(solution)/shard_map/all_to_all | solution.py:201
  109.1 10.7 %shard_map.57.left_ref = bf16[32,256]{1,0:T(8,128)(2,1)S(1)} custom-call(s32[1]{0:T(128)} %bitcast.mine_ref, f32[256,256]{1,0:T(8,128)S(1)} %bitcast.20), custom_call_target="tpu_custom_call" | custom-call | tf_op jit(solution)/shard_map/pallas_call | solution.py:172
  119.8 3.4 %copy-done.1 = bf16[256,16384]{1,0:T(8,128)(2,1)S(1)} copy-done((bf16[256,16384]{1,0:T(8,128)(2,1)S(1)}, bf16[256,16384]{1,0:T(8,128)(2,1)}, u32[]{:S(2)}) %copy-start.1) | copy-done | bytes 8388632
  123.2 4.3 %shard_map.58 = bf16[16,16384]{1,0:T(8,128)(2,1)} custom-call(bf16[32,256]{1,0:T(8,128)(2,1)S(1)} %shard_map.57.left_ref, bf16[256,16384]{1,0:T(8,128)(2,1)S(1)} %copy-done.1), custom_call_target="tpu_custom_call" | custom-call | flops 268435456 | bytes 8388608 | tf_op jit(solution)/shard_map/pallas_call | solution.py:189
  (9 shorter events, 0.1 us)
Async XLA Ops:
  6.5 113.3 %all-gather.2.cloned.1.call-start = ((), (), s32[]{:S(2)}) async-start(), calls=%async_computation.4 | async-start | bytes 8912896 | tf_op jit(solution)/shard_map/all_gather | solution.py:214
  8.0 7.7 %collective-permute-start = (bf16[16,128]{1,0:T(8,128)(2,1)S(1)}, bf16[16,128]{1,0:T(8,128)(2,1)S(1)}, u32[]{:S(2)}, u32[]{:S(2)}) collective-permute-start(bf16[16,128]{1,0:T(8,128)(2,1)S(1)} %get-tuple-element.6), channel_id=1, source_target_pairs={{0,16},{16,32},{32,48},{48,64},{64,80},{80,96},{96,112},{112,128},... | collective-permute-start | bytes 12296 | tf_op jit(solution)/shard_map/ppermute | solution.py:215
  11.0 4.7 %collective-permute-start.1 = (bf16[16,128]{1,0:T(8,128)(2,1)S(1)}, bf16[16,128]{1,0:T(8,128)(2,1)S(1)}, u32[]{:S(2)}, u32[]{:S(2)}) collective-permute-start(bf16[16,128]{1,0:T(8,128)(2,1)S(1)} %get-tuple-element.5), channel_id=1, source_target_pairs={{16,0},{32,16},{48,32},{64,48},{80,64},{96,80},{112,96},{128,112},... | collective-permute-start | bytes 12296 | tf_op jit(solution)/shard_map/ppermute | solution.py:216
  15.7 5.8 %copy-start = (bf16[64,8,128,128]{3,2,1,0:T(8,128)(2,1)S(1)}, bf16[64,8,128,128]{3,2,1,0:T(8,128)(2,1)}, u32[]{:S(2)}) copy-start(bf16[64,8,128,128]{3,2,1,0:T(8,128)(2,1)} %ops_ref.1) | copy-start | bytes 50331652
  21.4 1.0 copy-start.2
  30.3 20.4 %all-to-all-start = ((f32[16,16,512]{2,0,1:T(8,128)}), f32[16,16,512]{2,0,1:T(8,128)S(1)}, u32[]{:S(2)}, u32[]{:S(2)}) async-start(f32[16,16,512]{2,0,1:T(8,128)} %bitcast.13), calls=%async_computation | async-start | bytes 1048576 | tf_op jit(solution)/shard_map/all_to_all | solution.py:220
  119.8 3.4 %copy-start.1 = (bf16[256,16384]{1,0:T(8,128)(2,1)S(1)}, bf16[256,16384]{1,0:T(8,128)(2,1)}, u32[]{:S(2)}) copy-start(bf16[256,16384]{1,0:T(8,128)(2,1)} %all-gather.2.cloned.1.call-done.all_ref) | copy-start | bytes 25165828
Sparse Core Ops, SparseCore 0:
  10.4 99.3 all-gather.1

commit v2 on v1

--- a/solution.py
+++ b/solution.py
@@ -18,44 +18,57 @@
 SPACE = ("z", "core")
 
 
-def predict_kernel(group, cols_ref, ens_ref, left_ref, right_ref, ops_ref, out_ref, blocks):
-    step = pl.program_id(0)
-    count = ens_ref.shape[1] // 128
-
-    @pl.when(step == 0)
-    def _():
-        blocks[0] = left_ref[...]
-        blocks[count + 1] = right_ref[...]
-        for j in range(count):
-            blocks[j + 1] = ens_ref[:, 128 * j : 128 * (j + 1)]
-
-    for o in range(group):
-        picked = jnp.concatenate([blocks[cols_ref[step * group + o, k]] for k in range(8)], axis=1)
-        weights = jnp.concatenate([ops_ref[o, k] for k in range(8)], axis=1)
-        part = lax.dot_general(weights, picked, NT, preferred_element_type=F32)
-        out_ref[:, 128 * o : 128 * (o + 1)] = part.T
-
-
-def predict(cols, ens_t, left, right, ops, group=8):
+def predict_kernel(cols_ref, ens_ref, left_ref, right_ref, ops_ref, out_ref, state, weights, state_sem, sems):
+    parts, members, width = out_ref.shape
+    group = width // 128
+    rows = ens_ref.shape[1]
+
+    def fetch(c):
+        return pltpu.make_async_copy(ops_ref.at[pl.ds(c * group, group)], weights.at[pl.ds(c * group, group)], sems.at[c])
+
+    inner = pltpu.make_async_copy(ens_ref, state.at[:, pl.ds(128, rows)], state_sem)
+    inner.start()
+    for c in range(4):
+        fetch(c).start()
+    state[:, :128] = left_ref[...]
+    state[:, rows + 128 :] = right_ref[...]
+    inner.wait()
+
+    def body(c, carry):
+        fetch(c).wait()
+
+        @pl.when(c + 4 < parts)
+        def _():
+            fetch(c + 4).start()
+
+        for o in range(group):
+            block = c * group + o
+            picked = [state[:, pl.ds(pl.multiple_of(cols_ref[block, k] * 128, 128), 128)] for k in range(8)]
+            rows_of = [weights[block, k] for k in range(8)]
+            out_ref[c, :, 128 * o : 128 * (o + 1)] = lax.dot_general(
+                jnp.concatenate(picked, axis=1), jnp.concatenate(rows_of, axis=1), NT, preferred_element_type=F32
+            )
+        return carry
+
+    lax.fori_loop(0, parts, body, 0)
+
+
+def predict(cols, ens_t, left, right, ops, parts):
     members, rows = ens_t.shape
     oblocks = ops.shape[0]
-    whole = lambda shape: pl.BlockSpec(shape, lambda i, c: (0, 0))
+    anywhere, inside = pl.BlockSpec(memory_space=pl.ANY), pl.BlockSpec(memory_space=pltpu.VMEM)
     return pl.pallas_call(
-        functools.partial(predict_kernel, group),
-        out_shape=jax.ShapeDtypeStruct((members, oblocks * 128), F32),
-        grid_spec=pltpu.PrefetchScalarGridSpec(
-            num_scalar_prefetch=1,
-            grid=(oblocks // group,),
-            in_specs=[
-                whole(ens_t.shape),
-                whole(left.shape),
-                whole(right.shape),
-                pl.BlockSpec((group, 8, 128, 128), lambda i, c: (i, 0, 0, 0)),
-            ],
-            out_specs=pl.BlockSpec((members, group * 128), lambda i, c: (0, i)),
-            scratch_shapes=[pltpu.VMEM((rows // 128 + 2, members, 128), BF16)],
-        ),
-        compiler_params=pltpu.CompilerParams(vmem_limit_bytes=24 * 2**20),
+        predict_kernel,
+        out_shape=jax.ShapeDtypeStruct((parts, members, oblocks * 128 // parts), F32),
+        in_specs=[pl.BlockSpec(memory_space=pltpu.SMEM), anywhere, inside, inside, anywhere],
+        out_specs=inside,
+        scratch_shapes=[
+            pltpu.VMEM((members, rows + 256), BF16),
+            pltpu.VMEM(ops.shape, BF16),
+            pltpu.SemaphoreType.DMA,
+            pltpu.SemaphoreType.DMA((parts,)),
+        ],
+        compiler_params=pltpu.CompilerParams(vmem_limit_bytes=50 * 2**20),
         cost_estimate=pl.CostEstimate(flops=2 * ops.size * members, bytes_accessed=2 * ops.size, transcendentals=0),
     )(cols, ens_t, left, right, ops)
 
@@ -82,7 +95,7 @@
     return pl.pallas_call(
         gram_kernel,
         out_shape=jax.ShapeDtypeStruct((total, total), F32),
-        compiler_params=pltpu.CompilerParams(vmem_limit_bytes=24 * 2**20),
+        compiler_params=pltpu.CompilerParams(vmem_limit_bytes=16 * 2**20),
     )(pred, obs, err)
 
 
@@ -134,7 +147,7 @@
     return jnp.concatenate([jnp.concatenate(o, axis=1) for o in out], axis=0)
 
 
-def transform_kernel(mine_ref, gram_ref, out_ref, a):
+def transform_kernel(gram_ref, ens_ref, out_ref, a):
     total = gram_ref.shape[0]
     half = total // 2
     row = lax.broadcasted_iota(jnp.int32, (total, total), 0)
@@ -159,42 +172,25 @@
     a[...] = inverse
     solved = jnp.sum(inverse * cross.T, axis=1, keepdims=True)
     weight = jnp.sum(inverse * solved, axis=0, keepdims=True)
-    mine = a[pl.ds(pl.multiple_of(mine_ref[0] * 16, 16), 16), :]
-    rounded = (mine + weight).astype(BF16).astype(F32)
+    rounded = (inverse + weight).astype(BF16).astype(F32)
     centred = rounded - jnp.sum(rounded, axis=1, keepdims=True) / total + 1.0 / total
     high = centred.astype(BF16)
-    out_ref[:16] = high
-    out_ref[16:] = (centred - high.astype(F32)).astype(BF16)
-
-
-def transform(mine, gram_sum):
+    rest = (centred - high.astype(F32)).astype(BF16)
+    states = ens_ref[...]
+    both = jnp.dot(high, states, preferred_element_type=F32) + jnp.dot(rest, states, preferred_element_type=F32)
+    out_ref[...] = both.astype(BF16)
+
+
+def transform(gram_sum, states):
     total = gram_sum.shape[0]
     return pl.pallas_call(
         transform_kernel,
-        out_shape=jax.ShapeDtypeStruct((32, total), BF16),
-        in_specs=[pl.BlockSpec(memory_space=pltpu.SMEM), pl.BlockSpec(memory_space=pltpu.VMEM)],
+        out_shape=jax.ShapeDtypeStruct(states.shape, BF16),
+        in_specs=[pl.BlockSpec(memory_space=pltpu.VMEM)] * 2,
         out_specs=pl.BlockSpec(memory_space=pltpu.VMEM),
         scratch_shapes=[pltpu.VMEM((total, total), F32)],
-        compiler_params=pltpu.CompilerParams(vmem_limit_bytes=24 * 2**20),
-    )(mine, gram_sum)
-
-
-def update_kernel(left_ref, all_ref, out_ref):
-    both = jnp.dot(left_ref[...], all_ref[...], preferred_element_type=F32)
-    out_ref[...] = (both[:16] + both[16:]).astype(BF16)
-
-
-def update(left, everyone, width=2048):
-    total, rows = everyone.shape
-    return pl.pallas_call(
-        update_kernel,
-        out_shape=jax.ShapeDtypeStruct((16, rows), BF16),
-        grid=(rows // width,),
-        in_specs=[pl.BlockSpec(left.shape, lambda i: (0, 0)), pl.BlockSpec((total, width), lambda i: (0, i))],
-        out_specs=pl.BlockSpec((16, width), lambda i: (0, i)),
-        compiler_params=pltpu.CompilerParams(vmem_limit_bytes=24 * 2**20),
-        cost_estimate=pl.CostEstimate(flops=64 * total * rows, bytes_accessed=2 * total * rows, transcendentals=0),
-    )(left, everyone)
+        compiler_params=pltpu.CompilerParams(vmem_limit_bytes=16 * 2**20),
+    )(gram_sum, states)
 
 
 def to_all(x, axes, count):
@@ -211,22 +207,26 @@
     total = members * member_count
     space_index = lax.axis_index(SPACE)
     member_index = lax.axis_index(MEMBER)
-    everyone = lax.all_gather(ens_t, MEMBER, axis=0, tiled=True)
+    width = rows // member_count
+    states = ens_t.reshape(members, member_count, width).transpose(1, 0, 2)
+    states = lax.all_to_all(states, MEMBER, 0, 0, tiled=True)
     left = lax.ppermute(ens_t[:, -128:], SPACE, [(i, (i + 1) % space_count) for i in range(space_count)])
     right = lax.ppermute(ens_t[:, :128], SPACE, [((i + 1) % space_count, i) for i in range(space_count)])
     state_local = rows // 128
     cols = jnp.mod(block_columns - space_index * state_local + 1, state_local * space_count)
-    predicted = predict(cols, ens_t, left, right, operator_blocks)
-    predicted = lax.all_to_all(predicted, MEMBER, 1, 0, tiled=True)
-    width = predicted.shape[1]
-    obs = lax.dynamic_slice_in_dim(observed, member_index * width, width)[None]
-    err = lax.dynamic_slice_in_dim(error_scale, member_index * width, width)[None]
+    predicted = predict(cols, ens_t, left, right, operator_blocks, member_count)
+    predicted, states = lax.optimization_barrier((predicted, states))
+    predicted = lax.all_to_all(predicted, MEMBER, 0, 0, tiled=True).reshape(total, -1)
+    count = predicted.shape[1]
+    obs = lax.dynamic_slice_in_dim(observed, member_index * count, count)[None]
+    err = lax.dynamic_slice_in_dim(error_scale, member_index * count, count)[None]
     part = gram(predicted, obs, err).reshape(plane_count, -1, total)
     part = jnp.sum(lax.all_to_all(part, PLANE, 0, 0, tiled=True), axis=0)
     part = jnp.sum(to_all(part, "z", z_count), axis=0)
     gram_sum = to_all(part, PLANE, plane_count).reshape(total, total)
-    mine = transform(member_index.astype(jnp.int32).reshape(1), gram_sum)
-    return update(mine, everyone).T
+    analysis = transform(gram_sum, states.reshape(total, width)).reshape(member_count, members, width)
+    analysis = lax.all_to_all(analysis, MEMBER, 0, 0, tiled=True)
+    return analysis.transpose(1, 0, 2).reshape(members, rows).T
 
 
 def solution(mesh):

time: 135 us -> 127 us (0.941)
  between operations: 13.5 us -> 0.1 us
  blocking collectives: 57 us -> 70.3 us
  local copies, waits for them, and re-layouts: 13.4 us -> 6.09 us
  starting transfers between devices: 12 us -> 17.7 us
  waiting for transfers between devices: 14.5 us -> 9.3 us
    all_to_all x0 -> x1, blocking collectives: none -> 14.2 us  [local(): analysis = lax.all_to_all(analysis, MEMBER, 0, 0, tiled=True)]
    all_to_all x1 -> x2, starting transfers between devices: 5.11 us -> 14.8 us  [the longest x1 7.58 us: local(): states = lax.all_to_all(states, MEMBER, 0, 0, tiled=True)]
    unnamed x6 -> x2, local copies, waits for them, and re-layouts: 10.2 us -> 1.04 us
    all_to_all x1 -> x2, waiting for transfers between devices: 13.8 us -> 7.46 us  [the longest x1 7.46 us: local(): lax.all_to_all(predicted, MEMBER, 0, 0, tiled=True).reshape(total, -1)]
    all_to_all x2, blocking collectives: 42.1 us -> 38.5 us  [to_all(): lax.all_to_all(jnp.broadcast_to(x[None], (count,) + x.shape), axes, 0, 0,...]
    ppermute x1, starting transfers between devices: 3.85 us -> 0.39 us  [local(): lax.ppermute(ens_t[:, :128], SPACE, [((i + 1) % space_count, i) for i in...]
    reshape x0 -> x2, local copies, waits for them, and re-layouts: none -> 2.71 us  [the longest x1 1.88 us: local(): states = ens_t.reshape(members, member_count, width).transpose(1, 0, 2)]
    all_to_all x1, blocking collectives: 14.9 us -> 17.6 us  [local(): part = jnp.sum(lax.all_to_all(part, PLANE, 0, 0, tiled=True), axis=0)]
  transfers between devices with their start and end apart: 4 -> 4, of which waited for: 1 -> 2; matrix products, arithmetic and copies ran while one was open for 3% -> 2% of each run, Pallas kernels for 14% -> 8%
where the time goes in v2:
time: 127 us; the launch traced here: 126 us
  blocking collectives  70.3 us (55%)
  Pallas kernels  22.3 us (18%)
  starting transfers between devices  17.7 us (14%)
  waiting for transfers between devices  9.3 us (7%)
  local copies, waits for them, and re-layouts  6.09 us (5%)
    all_to_all x2, blocking collectives, to_all(): lax.all_to_all(jnp.broadcast_to(x[None], (count,) + x.shape), axes, 0, 0,...  38.5 us
    all_to_all x1, blocking collectives, local(): part = jnp.sum(lax.all_to_all(part, PLANE, 0, 0, tiled=True), axis=0)  17.6 us
    all_to_all x1, blocking collectives, local(): analysis = lax.all_to_all(analysis, MEMBER, 0, 0, tiled=True)  14.2 us
    pallas_call x1, Pallas kernels, transform(): pl.pallas_call(transform_kernel, out_shape=jax.ShapeDtypeStruct(states.sh...  11.5 us
    pallas_call x1, Pallas kernels, predict(): pl.pallas_call(predict_kernel, out_shape=jax.ShapeDtypeStruct((parts, mem...  9.53 us
    all_to_all x1, starting transfers between devices, local(): states = lax.all_to_all(states, MEMBER, 0, 0, tiled=True)  7.58 us
    all_to_all x1, waiting for transfers between devices, local(): lax.all_to_all(predicted, MEMBER, 0, 0, tiled=True).reshape(total, -1)  7.46 us
    all_to_all x1, starting transfers between devices, local(): lax.all_to_all(predicted, MEMBER, 0, 0, tiled=True).reshape(total, -1)  7.24 us
  transfers between devices with their start and end apart: 4, of which 2 were waited for; matrix products, arithmetic and copies ran while one was open for 2% of the time, Pallas kernels for 8%

profile of v2, /device:TPU:1, one launch (start us, length us, event | category | flops | bytes accessed | tf_op | source)
XLA Modules:
  0.0 126.4 jit_solution(150087443679670544)
XLA Ops:
  0.0 1.9 %copy.20 = bf16[2,16,8,1024]{3,2,0,1:T(8,128)(2,1)} copy(bf16[2,16,8,1024]{3,2,1,0:T(8,128)(2,1)} %bitcast.20) | data formatting | bytes 1048576 | tf_op jit(solution)/shard_map/reshape | solution.py:211
  1.9 7.6 %all-to-all-start = ((bf16[16,16,1024]{2,1,0:T(8,128)(2,1)}), bf16[16,16,1024]{2,1,0:T(8,128)(2,1)S(1)}, u32[]{:S(2)}, u32[]{:S(2)}) async-start(bf16[16,16,1024]{2,1,0:T(8,128)(2,1)} %bitcast.19), calls=%async_computation | async-start | bytes 1048576 | tf_op jit(solution)/shard_map/all_to_all | solution.py:212
  9.5 0.7 fusion.1
  10.2 2.5 %collective-permute-start = (bf16[16,128]{1,0:T(8,128)(2,1)S(1)}, bf16[16,128]{1,0:T(8,128)(2,1)S(1)}, u32[]{:S(2)}, u32[]{:S(2)}) collective-permute-start(bf16[16,128]{1,0:T(8,128)(2,1)S(1)} %get-tuple-element.10), channel_id=1, source_target_pairs={{0,16},{16,32},{32,48},{48,64},{64,80},{80,96},{96,112},{112,128},... | collective-permute-start | bytes 12296 | tf_op jit(solution)/shard_map/ppermute | solution.py:213
  12.7 0.4 collective-permute-start.1
  13.0 0.7 broadcast_subtract_fusion
  13.7 0.1 copy.14
  13.8 0.0 collective-permute-done.left_ref
  13.9 1.8 %collective-permute-done.1.right_ref = bf16[16,128]{1,0:T(8,128)(2,1)S(1)} collective-permute-done((bf16[16,128]{1,0:T(8,128)(2,1)S(1)}, bf16[16,128]{1,0:T(8,128)(2,1)S(1)}, u32[]{:S(2)}, u32[]{:S(2)}) %collective-permute-start.1) | collective-permute-done | bytes 4128 | tf_op jit(solution)/shard_map/ppermute | solution.py:214
  15.7 0.0 copy-start
  15.7 1.0 copy-done
  16.7 9.5 %shard_map.55 = f32[16,16,512]{2,1,0:T(8,128)} custom-call(s32[64,8]{1,0:T(8,128)S(1)} %add_select_fusion.cols_ref, bf16[16,16384]{1,0:T(8,128)(2,1)S(1)} %bitcast.22, bf16[16,128]{1,0:T(8,128)(2,1)S(1)} %collective-permute-done.left_ref, bf16[16,128]{1,0:T(8,128)(2,1)S(1)} %collective-permute-done.1.right_ref, bf16[64,8,128,128]{3,2,1,0:T(8,128)(2,1)} %ops_ref.1), custom_call_target="tpu_custom_call" | custom-call | flops 268435456 | bytes 16777216 | tf_op jit(solution)/shard_map/pallas_call | solution.py:60
  26.3 0.0 all-to-all-done
  26.3 7.2 %all-to-all-start.1 = ((f32[16,16,512]{2,1,0:T(8,128)}), f32[16,16,512]{2,1,0:T(8,128)S(1)}, u32[]{:S(2)}, u32[]{:S(2)}) async-start(f32[16,16,512]{2,1,0:T(8,128)} %shard_map.55), calls=%async_computation.1 | async-start | bytes 1048576 | tf_op jit(solution)/shard_map/all_to_all | solution.py:219
  33.5 0.8 dynamic_slice.6
  34.3 0.8 dynamic_slice.7
  35.1 7.5 %all-to-all-done.1 = f32[16,16,512]{2,1,0:T(8,128)S(1)} async-done(((f32[16,16,512]{2,1,0:T(8,128)}), f32[16,16,512]{2,1,0:T(8,128)S(1)}, u32[]{:S(2)}, u32[]{:S(2)}) %all-to-all-start.1) | async-done | bytes 524320 | tf_op jit(solution)/shard_map/all_to_all | solution.py:219
  42.5 1.2 shard_map.56
  43.8 17.6 %all_to_all.30 = f32[32,8,256]{2,1,0:T(8,128)S(1)} all-to-all(f32[32,8,256]{2,1,0:T(8,128)S(1)} %bitcast.26), channel_id=1, replica_groups=mesh['z'=16,'core'=2,'y'=4,'x'=4] {'core','y','x'}, dimensions={0} | all-to-all | bytes 524288 | tf_op jit(solution)/shard_map/all_to_all | solution.py:224
  61.4 23.0 %all_to_all.31 = f32[16,8,256]{2,1,0:T(8,128)S(1)} all-to-all(f32[16,8,256]{2,1,0:T(8,128)S(1)} %broadcast_in_dim.20), channel_id=1, replica_groups=mesh['z'=16,'core'=2,'y'=4,'x'=4] {'z'}, dimensions={0} | all-to-all | bytes 262144 | tf_op jit(solution)/shard_map/all_to_all | solution.py:197
  84.5 15.5 %all_to_all.32 = f32[32,8,256]{2,1,0:T(8,128)S(1)} all-to-all(f32[32,8,256]{2,1,0:T(8,128)S(1)} %broadcast_in_dim.21), channel_id=1, replica_groups=mesh['z'=16,'core'=2,'y'=4,'x'=4] {'core','y','x'}, dimensions={0} | all-to-all | bytes 524288 | tf_op jit(solution)/shard_map/all_to_all | solution.py:197
  99.9 11.5 %shard_map.57 = bf16[256,1024]{1,0:T(8,128)(2,1)S(1)} custom-call(f32[256,256]{1,0:T(8,128)S(1)} %bitcast.27, bf16[256,1024]{1,0:T(8,128)(2,1)S(1)} %bitcast.23), custom_call_target="tpu_custom_call" | custom-call | tf_op jit(solution)/shard_map/pallas_call | solution.py:186
  111.4 14.2 %all_to_all.33 = bf16[16,16,1024]{2,1,0:T(8,128)(2,1)S(1)} all-to-all(bf16[16,16,1024]{2,1,0:T(8,128)(2,1)S(1)} %bitcast.25), channel_id=1, replica_groups=mesh['z'=16,'core'=2,'y'=4,'x'=4] {'y','x'}, dimensions={0} | all-to-all | bytes 1048576 | tf_op jit(solution)/shard_map/all_to_all | solution.py:228
  125.6 0.8 copy.18
  (5 shorter events, 0.1 us)
Async XLA Ops:
  1.9 24.4 %all-to-all-start = ((bf16[16,16,1024]{2,1,0:T(8,128)(2,1)}), bf16[16,16,1024]{2,1,0:T(8,128)(2,1)S(1)}, u32[]{:S(2)}, u32[]{:S(2)}) async-start(bf16[16,16,1024]{2,1,0:T(8,128)(2,1)} %bitcast.19), calls=%async_computation | async-start | bytes 1048576 | tf_op jit(solution)/shard_map/all_to_all | solution.py:212
  10.2 3.7 %collective-permute-start = (bf16[16,128]{1,0:T(8,128)(2,1)S(1)}, bf16[16,128]{1,0:T(8,128)(2,1)S(1)}, u32[]{:S(2)}, u32[]{:S(2)}) collective-permute-start(bf16[16,128]{1,0:T(8,128)(2,1)S(1)} %get-tuple-element.10), channel_id=1, source_target_pairs={{0,16},{16,32},{32,48},{48,64},{64,80},{80,96},{96,112},{112,128},... | collective-permute-start | bytes 12296 | tf_op jit(solution)/shard_map/ppermute | solution.py:213
  12.7 3.0 %collective-permute-start.1 = (bf16[16,128]{1,0:T(8,128)(2,1)S(1)}, bf16[16,128]{1,0:T(8,128)(2,1)S(1)}, u32[]{:S(2)}, u32[]{:S(2)}) collective-permute-start(bf16[16,128]{1,0:T(8,128)(2,1)S(1)} %get-tuple-element.9), channel_id=1, source_target_pairs={{16,0},{32,16},{48,32},{64,48},{80,64},{96,80},{112,96},{128,112},... | collective-permute-start | bytes 12296 | tf_op jit(solution)/shard_map/ppermute | solution.py:214
  15.7 1.0 copy-start
  26.3 16.2 %all-to-all-start.1 = ((f32[16,16,512]{2,1,0:T(8,128)}), f32[16,16,512]{2,1,0:T(8,128)S(1)}, u32[]{:S(2)}, u32[]{:S(2)}) async-start(f32[16,16,512]{2,1,0:T(8,128)} %shard_map.55), calls=%async_computation.1 | async-start | bytes 1048576 | tf_op jit(solution)/shard_map/all_to_all | solution.py:219

commit v3 on v2

--- a/solution.py
+++ b/solution.py
@@ -19,9 +19,10 @@
 
 
 def predict_kernel(cols_ref, ens_ref, left_ref, right_ref, ops_ref, out_ref, state, weights, state_sem, sems):
-    parts, members, width = out_ref.shape
-    group = width // 128
+    parts = out_ref.shape[0]
     rows = ens_ref.shape[1]
+    group = ops_ref.shape[0] // parts
+    width, share = 128 * group, rows // parts
 
     def fetch(c):
         return pltpu.make_async_copy(ops_ref.at[pl.ds(c * group, group)], weights.at[pl.ds(c * group, group)], sems.at[c])
@@ -45,9 +46,13 @@
             block = c * group + o
             picked = [state[:, pl.ds(pl.multiple_of(cols_ref[block, k] * 128, 128), 128)] for k in range(8)]
             rows_of = [weights[block, k] for k in range(8)]
-            out_ref[c, :, 128 * o : 128 * (o + 1)] = lax.dot_general(
+            value = lax.dot_general(
                 jnp.concatenate(picked, axis=1), jnp.concatenate(rows_of, axis=1), NT, preferred_element_type=F32
             )
+            high = value.astype(BF16)
+            out_ref[c, :, 128 * o : 128 * (o + 1)] = high
+            out_ref[c, :, width + 128 * o : width + 128 * (o + 1)] = (value - high.astype(F32)).astype(BF16)
+        out_ref[c, :, 2 * width :] = state[:, pl.ds(pl.multiple_of(128 + c * share, 128), share)]
         return carry
 
     lax.fori_loop(0, parts, body, 0)
@@ -56,11 +61,11 @@
 def predict(cols, ens_t, left, right, ops, parts):
     members, rows = ens_t.shape
     oblocks = ops.shape[0]
-    anywhere, inside = pl.BlockSpec(memory_space=pl.ANY), pl.BlockSpec(memory_space=pltpu.VMEM)
+    outside, inside = pl.BlockSpec(memory_space=pltpu.HBM), pl.BlockSpec(memory_space=pltpu.VMEM)
     return pl.pallas_call(
         predict_kernel,
-        out_shape=jax.ShapeDtypeStruct((parts, members, oblocks * 128 // parts), F32),
-        in_specs=[pl.BlockSpec(memory_space=pltpu.SMEM), anywhere, inside, inside, anywhere],
+        out_shape=jax.ShapeDtypeStruct((parts, members, (2 * oblocks * 128 + rows) // parts), BF16),
+        in_specs=[pl.BlockSpec(memory_space=pltpu.SMEM), outside, inside, inside, outside],
         out_specs=inside,
         scratch_shapes=[
             pltpu.VMEM((members, rows + 256), BF16),
@@ -68,14 +73,16 @@
             pltpu.SemaphoreType.DMA,
             pltpu.SemaphoreType.DMA((parts,)),
         ],
-        compiler_params=pltpu.CompilerParams(vmem_limit_bytes=50 * 2**20),
+        compiler_params=pltpu.CompilerParams(vmem_limit_bytes=58 * 2**20),
         cost_estimate=pl.CostEstimate(flops=2 * ops.size * members, bytes_accessed=2 * ops.size, transcendentals=0),
     )(cols, ens_t, left, right, ops)
 
 
 def gram_kernel(pred_ref, obs_ref, err_ref, out_ref):
-    total, half = pred_ref.shape[0], pred_ref.shape[0] // 2
-    pred = pred_ref[...]
+    total = out_ref.shape[0]
+    half = total // 2
+    width = obs_ref.shape[1]
+    pred = (pred_ref[:, :, :width].astype(F32) + pred_ref[:, :, width:].astype(F32)).reshape(total, width)
     mean = jnp.sum(pred, axis=0, keepdims=True) / total
     scale = err_ref[...] * math.sqrt(total - 1)
     white = (pred - mean) / scale
@@ -90,13 +97,18 @@
     out_ref[half:, :] = dot(low, white)
 
 
-def gram(pred, obs, err):
-    total = pred.shape[0]
+def gram(shared, obs, err):
+    sources, members = shared.shape[:2]
+    total, width = sources * members, obs.shape[1]
+    row = pl.BlockSpec((1, width), lambda i: (0, 0))
     return pl.pallas_call(
         gram_kernel,
         out_shape=jax.ShapeDtypeStruct((total, total), F32),
+        grid=(1,),
+        in_specs=[pl.BlockSpec((sources, members, 2 * width), lambda i: (0, 0, 0)), row, row],
+        out_specs=pl.BlockSpec((total, total), lambda i: (0, 0)),
         compiler_params=pltpu.CompilerParams(vmem_limit_bytes=16 * 2**20),
-    )(pred, obs, err)
+    )(shared, obs, err)
 
 
 WIDE = 32
@@ -147,7 +159,7 @@
     return jnp.concatenate([jnp.concatenate(o, axis=1) for o in out], axis=0)
 
 
-def transform_kernel(gram_ref, ens_ref, out_ref, a):
+def transform_kernel(gram_ref, ens_ref, out_ref):
     total = gram_ref.shape[0]
     half = total // 2
     row = lax.broadcasted_iota(jnp.int32, (total, total), 0)
@@ -157,40 +169,45 @@
     cross = jnp.concatenate([extra[:, 0:1], extra[:, 1:2]], axis=0)
     mirror = given[half:, :half].T
     full = jnp.concatenate([jnp.concatenate([given[:half, :half], mirror], axis=1), given[half:, :]], axis=0)
-    a[...] = full + jnp.where(row == col, 1.0, 0.0)
-    for s in range(total // WIDE):
+    full = full + jnp.where(row == col, 1.0, 0.0)
+    count = total // WIDE
+    blocks = [full[WIDE * t : WIDE * (t + 1), :] for t in range(count)]
+    for s in range(count):
         r0, r1 = WIDE * s, WIDE * (s + 1)
-        done = eliminate([a[r0 + 8 * g : r0 + 8 * (g + 1), :] for g in range(WIDE // 8)], r0)
-        a[r0:r1, :] = done
+        done = eliminate([blocks[s][8 * g : 8 * (g + 1), :] for g in range(WIDE // 8)], r0)
+        here = col[r0:r1]
+        blocks[s] = jnp.where(here <= row[r0:r1], done, 0.0)
         if r1 < total:
-            above = (col[r0:r1] < r1) & (col[r0:r1] > row[r0:r1])
-            kept = jnp.where(above, 0.0, done)
-            update = lax.dot_general(done, kept, TN, precision=HIGHEST, preferred_element_type=F32)
-            block = (col[r1:] >= r0) & (col[r1:] < r1)
-            a[r1:, :] = jnp.where(block, 0.0, a[r1:, :]) - update[r1:, :]
-    inverse = jnp.where(col <= row, a[...], 0.0)
-    a[...] = inverse
+            kept = jnp.where((here < r1) & (here > row[r0:r1]), 0.0, done)
+            turned = done.T
+            inside = (here >= r0) & (here < r1)
+            for t in range(s + 1, count):
+                change = jnp.dot(turned[WIDE * t : WIDE * (t + 1), :], kept, precision=HIGHEST, preferred_element_type=F32)
+                blocks[t] = jnp.where(inside, 0.0, blocks[t]) - change
+    inverse = jnp.concatenate(blocks, axis=0)
     solved = jnp.sum(inverse * cross.T, axis=1, keepdims=True)
     weight = jnp.sum(inverse * solved, axis=0, keepdims=True)
     rounded = (inverse + weight).astype(BF16).astype(F32)
     centred = rounded - jnp.sum(rounded, axis=1, keepdims=True) / total + 1.0 / total
     high = centred.astype(BF16)
     rest = (centred - high.astype(F32)).astype(BF16)
-    states = ens_ref[...]
+    states = ens_ref[...].reshape(total, -1)
     both = jnp.dot(high, states, preferred_element_type=F32) + jnp.dot(rest, states, preferred_element_type=F32)
-    out_ref[...] = both.astype(BF16)
-
-
-def transform(gram_sum, states):
+    out_ref[...] = both.astype(BF16).reshape(out_ref.shape)
+
+
+def transform(gram_sum, shared):
     total = gram_sum.shape[0]
+    sources, members, width = shared.shape
+    block = (sources, members, width // 2)
     return pl.pallas_call(
         transform_kernel,
-        out_shape=jax.ShapeDtypeStruct(states.shape, BF16),
-        in_specs=[pl.BlockSpec(memory_space=pltpu.VMEM)] * 2,
-        out_specs=pl.BlockSpec(memory_space=pltpu.VMEM),
-        scratch_shapes=[pltpu.VMEM((total, total), F32)],
+        out_shape=jax.ShapeDtypeStruct(block, BF16),
+        grid=(1,),
+        in_specs=[pl.BlockSpec((total, total), lambda i: (0, 0)), pl.BlockSpec(block, lambda i: (0, 0, 1))],
+        out_specs=pl.BlockSpec(block, lambda i: (0, 0, 0)),
         compiler_params=pltpu.CompilerParams(vmem_limit_bytes=16 * 2**20),
-    )(gram_sum, states)
+    )(gram_sum, shared)
 
 
 def to_all(x, axes, count):
@@ -207,25 +224,20 @@
     total = members * member_count
     space_index = lax.axis_index(SPACE)
     member_index = lax.axis_index(MEMBER)
-    width = rows // member_count
-    states = ens_t.reshape(members, member_count, width).transpose(1, 0, 2)
-    states = lax.all_to_all(states, MEMBER, 0, 0, tiled=True)
     left = lax.ppermute(ens_t[:, -128:], SPACE, [(i, (i + 1) % space_count) for i in range(space_count)])
     right = lax.ppermute(ens_t[:, :128], SPACE, [((i + 1) % space_count, i) for i in range(space_count)])
     state_local = rows // 128
     cols = jnp.mod(block_columns - space_index * state_local + 1, state_local * space_count)
-    predicted = predict(cols, ens_t, left, right, operator_blocks, member_count)
-    predicted, states = lax.optimization_barrier((predicted, states))
-    predicted = lax.all_to_all(predicted, MEMBER, 0, 0, tiled=True).reshape(total, -1)
-    count = predicted.shape[1]
+    shared = predict(cols, ens_t, left, right, operator_blocks, member_count)
+    shared = lax.all_to_all(shared, MEMBER, 0, 0, tiled=True)
+    count = observed.shape[0] // member_count
     obs = lax.dynamic_slice_in_dim(observed, member_index * count, count)[None]
     err = lax.dynamic_slice_in_dim(error_scale, member_index * count, count)[None]
-    part = gram(predicted, obs, err).reshape(plane_count, -1, total)
+    part = gram(shared, obs, err).reshape(plane_count, -1, total)
     part = jnp.sum(lax.all_to_all(part, PLANE, 0, 0, tiled=True), axis=0)
     part = jnp.sum(to_all(part, "z", z_count), axis=0)
     gram_sum = to_all(part, PLANE, plane_count).reshape(total, total)
-    analysis = transform(gram_sum, states.reshape(total, width)).reshape(member_count, members, width)
-    analysis = lax.all_to_all(analysis, MEMBER, 0, 0, tiled=True)
+    analysis = lax.all_to_all(transform(gram_sum, shared), MEMBER, 0, 0, tiled=True)
     return analysis.transpose(1, 0, 2).reshape(members, rows).T
 
 

time: 127 us -> 123 us (0.969)
  starting transfers between devices: 17.7 us -> 10.8 us
  blocking collectives: 70.3 us -> 73.9 us
  local copies, waits for them, and re-layouts: 6.09 us -> 4.35 us
  waiting for transfers between devices: 9.3 us -> 10.8 us
  Pallas kernels: 22.3 us -> 21 us
    all_to_all x2 -> x1, starting transfers between devices: 14.8 us -> 3.95 us  [local(): shared = lax.all_to_all(shared, MEMBER, 0, 0, tiled=True)]
    ppermute x1, starting transfers between devices: 0.39 us -> 3.85 us  [local(): lax.ppermute(ens_t[:, :128], SPACE, [((i + 1) % space_count, i) for i in...]
    all_to_all x2 -> x1, waiting for transfers between devices: 7.46 us -> 10.8 us  [local(): shared = lax.all_to_all(shared, MEMBER, 0, 0, tiled=True)]
    all_to_all x2, blocking collectives: 38.5 us -> 40.8 us  [to_all(): lax.all_to_all(jnp.broadcast_to(x[None], (count,) + x.shape), axes, 0, 0,...]
    pallas_call x1, Pallas kernels: 11.5 us -> 9.28 us  [transform(): pl.pallas_call(transform_kernel, out_shape=jax.ShapeDtypeStruct(block, BF...]
    reshape x1 -> x0, local copies, waits for them, and re-layouts: 1.88 us -> none  [local(): states = ens_t.reshape(members, member_count, width).transpose(1, 0, 2)]
    ppermute x1, waiting for transfers between devices: 1.83 us -> 0.01 us  [local(): lax.ppermute(ens_t[:, :128], SPACE, [((i + 1) % space_count, i) for i in...]
    all_to_all x1, blocking collectives: 17.6 us -> 18.9 us  [local(): part = jnp.sum(lax.all_to_all(part, PLANE, 0, 0, tiled=True), axis=0)]
  transfers between devices with their start and end apart: 4 -> 3, of which waited for: 2 -> 1; matrix products, arithmetic and copies ran while one was open for 2% -> 2% of each run, Pallas kernels for 8% -> 0%
where the time goes in v3:
time: 123 us; the launch traced here: 122 us
  blocking collectives  73.9 us (60%)
  Pallas kernels  21 us (17%)
  starting transfers between devices  10.8 us (9%)
  waiting for transfers between devices  10.8 us (9%)
  local copies, waits for them, and re-layouts  4.35 us (4%)
  other arithmetic  1.38 us (1%)
    all_to_all x2, blocking collectives, to_all(): lax.all_to_all(jnp.broadcast_to(x[None], (count,) + x.shape), axes, 0, 0,...  40.8 us
    all_to_all x1, blocking collectives, local(): part = jnp.sum(lax.all_to_all(part, PLANE, 0, 0, tiled=True), axis=0)  18.9 us
    all_to_all x1, blocking collectives, local(): lax.all_to_all(transform(gram_sum, shared), MEMBER, 0, 0, tiled=True)  14.2 us
    all_to_all x1, waiting for transfers between devices, local(): shared = lax.all_to_all(shared, MEMBER, 0, 0, tiled=True)  10.8 us
    pallas_call x1, Pallas kernels, predict(): pl.pallas_call(predict_kernel, out_shape=jax.ShapeDtypeStruct((parts, mem...  10.3 us
    pallas_call x1, Pallas kernels, transform(): pl.pallas_call(transform_kernel, out_shape=jax.ShapeDtypeStruct(block, BF...  9.28 us
    all_to_all x1, starting transfers between devices, local(): shared = lax.all_to_all(shared, MEMBER, 0, 0, tiled=True)  3.95 us
    ppermute x1, starting transfers between devices, local(): lax.ppermute(ens_t[:, :128], SPACE, [((i + 1) % space_count, i) for i in...  3.85 us
  transfers between devices with their start and end apart: 3, of which 1 were waited for; matrix products, arithmetic and copies ran while one was open for 2% of the time, Pallas kernels for 0%

profile of v3, /device:TPU:1, one launch (start us, length us, event | category | flops | bytes accessed | tf_op | source)
XLA Modules:
  0.0 122.2 jit_solution(11635039812205889161)
XLA Ops:
  0.0 0.7 fusion.1
  0.7 3.0 %collective-permute-start = (bf16[16,128]{1,0:T(8,128)(2,1)S(1)}, bf16[16,128]{1,0:T(8,128)(2,1)S(1)}, u32[]{:S(2)}, u32[]{:S(2)}) collective-permute-start(bf16[16,128]{1,0:T(8,128)(2,1)S(1)} %get-tuple-element.6), channel_id=1, source_target_pairs={{0,16},{16,32},{32,48},{48,64},{64,80},{80,96},{96,112},{112,128},... | collective-permute-start | bytes 12296 | tf_op jit(solution)/shard_map/ppermute | solution.py:227
  3.7 3.9 %collective-permute-start.1 = (bf16[16,128]{1,0:T(8,128)(2,1)S(1)}, bf16[16,128]{1,0:T(8,128)(2,1)S(1)}, u32[]{:S(2)}, u32[]{:S(2)}) collective-permute-start(bf16[16,128]{1,0:T(8,128)(2,1)S(1)} %get-tuple-element.5), channel_id=1, source_target_pairs={{16,0},{32,16},{48,32},{64,48},{80,64},{96,80},{112,96},{128,112},... | collective-permute-start | bytes 12296 | tf_op jit(solution)/shard_map/ppermute | solution.py:228
  7.6 0.7 broadcast_subtract_fusion
  8.3 0.1 copy.14
  8.4 0.6 add_select_fusion.cols_ref
  9.0 0.0 collective-permute-done.left_ref
  9.0 0.0 copy-start
  9.0 0.0 collective-permute-done.1.right_ref
  9.0 0.6 copy-done
  9.6 0.0 copy-start.1
  9.6 0.6 copy-done.1
  10.2 10.3 %shard_map.55 = bf16[16,16,2048]{2,1,0:T(8,128)(2,1)} custom-call(s32[64,8]{1,0:T(8,128)} %add_select_fusion.cols_ref, bf16[16,16384]{1,0:T(8,128)(2,1)} %bitcast.16, bf16[16,128]{1,0:T(8,128)(2,1)} %copy-done, bf16[16,128]{1,0:T(8,128)(2,1)} %copy-done.1, bf16[64,8,128,128]{3,2,1,0:T(8,128)(2,1)} %ops_ref.1), custom_call_target="tpu_custom_call" | custom-call | flops 268435456 | bytes 16777216 | tf_op jit(solution)/shard_map/pallas_call | solution.py:65
  20.5 3.9 %all-to-all-start = ((bf16[16,16,2048]{2,1,0:T(8,128)(2,1)}), bf16[16,16,2048]{2,1,0:T(8,128)(2,1)S(1)}, u32[]{:S(2)}, u32[]{:S(2)}) async-start(bf16[16,16,2048]{2,1,0:T(8,128)(2,1)} %shard_map.55), calls=%async_computation | async-start | bytes 2097152 | tf_op jit(solution)/shard_map/all_to_all | solution.py:232
  24.5 0.8 dynamic_slice.6
  25.2 0.8 dynamic_slice.7
  26.0 10.8 %all-to-all-done.pred_ref.ens_ref = bf16[16,16,2048]{2,1,0:T(8,128)(2,1)S(1)} async-done(((bf16[16,16,2048]{2,1,0:T(8,128)(2,1)}), bf16[16,16,2048]{2,1,0:T(8,128)(2,1)S(1)}, u32[]{:S(2)}, u32[]{:S(2)}) %all-to-all-start) | async-done | bytes 1048608 | tf_op jit(solution)/shard_map/all_to_all | solution.py:232
  36.8 1.4 %shard_map.56 = f32[256,256]{1,0:T(8,128)S(1)} custom-call(bf16[16,16,2048]{2,1,0:T(8,128)(2,1)S(1)} %all-to-all-done.pred_ref.ens_ref, f32[1,512]{1,0:T(1,128)S(1)} %bitcast.12, f32[1,512]{1,0:T(1,128)S(1)} %bitcast.13), custom_call_target="tpu_custom_call" | custom-call | tf_op jit(solution)/shard_map/pallas_call | solution.py:104
  38.1 18.9 %all_to_all.25 = f32[32,8,256]{2,1,0:T(8,128)S(1)} all-to-all(f32[32,8,256]{2,1,0:T(8,128)S(1)} %bitcast.10), channel_id=1, replica_groups=mesh['z'=16,'core'=2,'y'=4,'x'=4] {'core','y','x'}, dimensions={0} | all-to-all | bytes 524288 | tf_op jit(solution)/shard_map/all_to_all | solution.py:237
  57.1 25.3 %all_to_all.26 = f32[16,8,256]{2,1,0:T(8,128)S(1)} all-to-all(f32[16,8,256]{2,1,0:T(8,128)S(1)} %broadcast_in_dim.20), channel_id=1, replica_groups=mesh['z'=16,'core'=2,'y'=4,'x'=4] {'z'}, dimensions={0} | all-to-all | bytes 262144 | tf_op jit(solution)/shard_map/all_to_all | solution.py:214
  82.5 15.5 %all_to_all.27 = f32[32,8,256]{2,1,0:T(8,128)S(1)} all-to-all(f32[32,8,256]{2,1,0:T(8,128)S(1)} %broadcast_in_dim.21), channel_id=1, replica_groups=mesh['z'=16,'core'=2,'y'=4,'x'=4] {'core','y','x'}, dimensions={0} | all-to-all | bytes 524288 | tf_op jit(solution)/shard_map/all_to_all | solution.py:214
  97.9 9.3 %shard_map.57 = bf16[16,16,1024]{2,1,0:T(8,128)(2,1)S(1)} custom-call(f32[256,256]{1,0:T(8,128)S(1)} %bitcast.11, bf16[16,16,2048]{2,1,0:T(8,128)(2,1)S(1)} %all-to-all-done.pred_ref.ens_ref), custom_call_target="tpu_custom_call" | custom-call | tf_op jit(solution)/shard_map/pallas_call | solution.py:203
  107.2 14.2 %all_to_all.28 = bf16[16,16,1024]{2,1,0:T(8,128)(2,1)S(1)} all-to-all(bf16[16,16,1024]{2,1,0:T(8,128)(2,1)S(1)} %shard_map.57), channel_id=1, replica_groups=mesh['z'=16,'core'=2,'y'=4,'x'=4] {'y','x'}, dimensions={0} | all-to-all | bytes 1048576 | tf_op jit(solution)/shard_map/all_to_all | solution.py:240
  121.4 0.8 copy.16
  (4 shorter events, 0.1 us)
Async XLA Ops:
  0.7 8.3 %collective-permute-start = (bf16[16,128]{1,0:T(8,128)(2,1)S(1)}, bf16[16,128]{1,0:T(8,128)(2,1)S(1)}, u32[]{:S(2)}, u32[]{:S(2)}) collective-permute-start(bf16[16,128]{1,0:T(8,128)(2,1)S(1)} %get-tuple-element.6), channel_id=1, source_target_pairs={{0,16},{16,32},{32,48},{48,64},{64,80},{80,96},{96,112},{112,128},... | collective-permute-start | bytes 12296 | tf_op jit(solution)/shard_map/ppermute | solution.py:227
  3.7 5.3 %collective-permute-start.1 = (bf16[16,128]{1,0:T(8,128)(2,1)S(1)}, bf16[16,128]{1,0:T(8,128)(2,1)S(1)}, u32[]{:S(2)}, u32[]{:S(2)}) collective-permute-start(bf16[16,128]{1,0:T(8,128)(2,1)S(1)} %get-tuple-element.5), channel_id=1, source_target_pairs={{16,0},{32,16},{48,32},{64,48},{80,64},{96,80},{112,96},{128,112},... | collective-permute-start | bytes 12296 | tf_op jit(solution)/shard_map/ppermute | solution.py:228
  9.0 0.6 copy-start
  9.6 0.6 copy-start.1
  20.5 16.3 %all-to-all-start = ((bf16[16,16,2048]{2,1,0:T(8,128)(2,1)}), bf16[16,16,2048]{2,1,0:T(8,128)(2,1)S(1)}, u32[]{:S(2)}, u32[]{:S(2)}) async-start(bf16[16,16,2048]{2,1,0:T(8,128)(2,1)} %shard_map.55), calls=%async_computation | async-start | bytes 2097152 | tf_op jit(solution)/shard_map/all_to_all | solution.py:232

commit v4 on v3

--- a/solution.py
+++ b/solution.py
@@ -18,22 +18,30 @@
 SPACE = ("z", "core")
 
 
-def predict_kernel(cols_ref, ens_ref, left_ref, right_ref, ops_ref, out_ref, state, weights, state_sem, sems):
+def predict_kernel(cols_ref, state, left_ref, right_ref, ops_ref, out_ref, weights, staged, sems, out_sems, ens_sems):
     parts = out_ref.shape[0]
-    rows = ens_ref.shape[1]
+    rows = state.shape[1] - 256
     group = ops_ref.shape[0] // parts
     width, share = 128 * group, rows // parts
 
     def fetch(c):
         return pltpu.make_async_copy(ops_ref.at[pl.ds(c * group, group)], weights.at[pl.ds(c * group, group)], sems.at[c])
 
-    inner = pltpu.make_async_copy(ens_ref, state.at[:, pl.ds(128, rows)], state_sem)
-    inner.start()
     for c in range(4):
         fetch(c).start()
-    state[:, :128] = left_ref[...]
-    state[:, rows + 128 :] = right_ref[...]
-    inner.wait()
+    def deliver(c):
+        return pltpu.make_async_copy(staged.at[c], out_ref.at[c, :, pl.ds(0, 2 * width)], out_sems.at[c])
+
+    def pass_on(c):
+        chunk = state.at[:, pl.ds(128 + c * share, share)]
+        return pltpu.make_async_copy(chunk, out_ref.at[c, :, pl.ds(2 * width, share)], ens_sems.at[c])
+
+    def pick(at):
+        inner = state[:, pl.ds(pl.multiple_of(at * 128, 128), 128)]
+        return jnp.where(at == 0, left_ref[...], jnp.where(at == rows // 128 + 1, right_ref[...], inner))
+
+    for c in range(parts):
+        pass_on(c).start()
 
     def body(c, carry):
         fetch(c).wait()
@@ -44,38 +52,42 @@
 
         for o in range(group):
             block = c * group + o
-            picked = [state[:, pl.ds(pl.multiple_of(cols_ref[block, k] * 128, 128), 128)] for k in range(8)]
+            picked = [pick(cols_ref[block, k]) for k in range(8)]
             rows_of = [weights[block, k] for k in range(8)]
             value = lax.dot_general(
                 jnp.concatenate(picked, axis=1), jnp.concatenate(rows_of, axis=1), NT, preferred_element_type=F32
             )
             high = value.astype(BF16)
-            out_ref[c, :, 128 * o : 128 * (o + 1)] = high
-            out_ref[c, :, width + 128 * o : width + 128 * (o + 1)] = (value - high.astype(F32)).astype(BF16)
-        out_ref[c, :, 2 * width :] = state[:, pl.ds(pl.multiple_of(128 + c * share, 128), share)]
+            staged[c, :, 128 * o : 128 * (o + 1)] = high
+            staged[c, :, width + 128 * o : width + 128 * (o + 1)] = (value - high.astype(F32)).astype(BF16)
+        deliver(c).start()
         return carry
 
     lax.fori_loop(0, parts, body, 0)
-
-
-def predict(cols, ens_t, left, right, ops, parts):
-    members, rows = ens_t.shape
+    for c in range(parts):
+        pass_on(c).wait()
+        deliver(c).wait()
+
+
+def predict(cols, state, left, right, ops, parts):
+    members, rows = state.shape[0], state.shape[1] - 256
     oblocks = ops.shape[0]
     outside, inside = pl.BlockSpec(memory_space=pltpu.HBM), pl.BlockSpec(memory_space=pltpu.VMEM)
     return pl.pallas_call(
         predict_kernel,
         out_shape=jax.ShapeDtypeStruct((parts, members, (2 * oblocks * 128 + rows) // parts), BF16),
-        in_specs=[pl.BlockSpec(memory_space=pltpu.SMEM), outside, inside, inside, outside],
-        out_specs=inside,
+        in_specs=[pl.BlockSpec(memory_space=pltpu.SMEM), inside, inside, inside, outside],
+        out_specs=outside,
         scratch_shapes=[
-            pltpu.VMEM((members, rows + 256), BF16),
             pltpu.VMEM(ops.shape, BF16),
-            pltpu.SemaphoreType.DMA,
+            pltpu.VMEM((parts, members, 2 * oblocks * 128 // parts), BF16),
+            pltpu.SemaphoreType.DMA((parts,)),
+            pltpu.SemaphoreType.DMA((parts,)),
             pltpu.SemaphoreType.DMA((parts,)),
         ],
-        compiler_params=pltpu.CompilerParams(vmem_limit_bytes=58 * 2**20),
+        compiler_params=pltpu.CompilerParams(vmem_limit_bytes=50 * 2**20),
         cost_estimate=pl.CostEstimate(flops=2 * ops.size * members, bytes_accessed=2 * ops.size, transcendentals=0),
-    )(cols, ens_t, left, right, ops)
+    )(cols, state, left, right, ops)
 
 
 def gram_kernel(pred_ref, obs_ref, err_ref, out_ref):
@@ -112,66 +124,82 @@
 
 
 WIDE = 32
+STEP = 16
 
 
 def spread(column):
     return jnp.broadcast_to(column, (8, 128))
 
 
+def total_of(terms):
+    while len(terms) > 1:
+        terms = [a + b for a, b in zip(terms[::2], terms[1::2])] + terms[len(terms) & ~1 :]
+    return terms[0]
+
+
 def eliminate(panel, col0):
-    groups = WIDE // 8
+    groups, span = WIDE // 8, STEP // 8
     sub = lax.broadcasted_iota(jnp.int32, (8, 128), 0)
     tile = col0 // 128
     lanes = lax.broadcasted_iota(jnp.int32, (8, 128), 1) + 128 * tile
     tiles = panel[0].shape[1] // 128
+    order = [tile] + [t for t in range(tiles) if t != tile]
     panel = [[p[:, 128 * t : 128 * (t + 1)] for t in range(tiles)] for p in panel]
     out = []
-    for q in range(groups):
+    for q in range(0, groups, span):
         start = col0 + 8 * q
         at = start - 128 * tile
-        coef = [[None if g < q else spread(panel[g][tile][:, at + c : at + c + 1]) for g in range(groups)] for c in range(8)]
-        pivots = jnp.ones((8, 128), F32)
-        for j in range(8):
-            pivot = spread(coef[j][q][j : j + 1, :])
-            pivots = jnp.where(sub == j, pivot, pivots)
+        coef = [[None if g < q else spread(panel[g][tile][:, at + c : at + c + 1]) for g in range(groups)] for c in range(STEP)]
+        pivots = [jnp.ones((8, 128), F32) for _ in range(span)]
+        for j in range(STEP):
+            own, r = q + j // 8, j % 8
+            pivot = spread(coef[j][own][r : r + 1, :])
+            pivots[j // 8] = jnp.where(sub == r, pivot, pivots[j // 8])
             ratio = 1.0 / pivot
-            ahead = [spread(coef[c][q][j : j + 1, :]) for c in range(8)]
-            for g in range(q, groups):
+            ahead = [spread(coef[c][own][r : r + 1, :]) for c in range(STEP)]
+            for g in range(own, groups):
                 times = coef[j][g] * ratio
-                if g == q:
-                    times = jnp.where(sub > j, times, 0.0)
-                for c in range(8):
+                if g == own:
+                    times = jnp.where(sub > r, times, 0.0)
+                for c in [c for c in range(j + 1, STEP)] + [c for c in range(j + 1)]:
                     if c == j:
-                        coef[c][g] = jnp.where(sub == j, 1.0, -times) if g == q else -times
+                        coef[c][g] = jnp.where(sub == r, 1.0, -times) if g == own else -times
                     else:
                         coef[c][g] = coef[c][g] - times * ahead[c]
-        inside = (lanes >= start) & (lanes < start + 8)
-        unit = jnp.where(lanes - start == sub, 1.0, 0.0)
-        base = [jnp.where(inside, unit, panel[q][t]) if t == tile else panel[q][t] for t in range(tiles)]
-        root = lax.rsqrt(pivots)
-        rows = [[spread(base[t][c : c + 1, :]) for t in range(tiles)] for c in range(8)]
-        low = [jnp.where(sub >= c, coef[c][q], 0.0) for c in range(8)]
-        out.append([sum(low[c] * rows[c][t] for c in range(8)) * root for t in range(tiles)])
-        for g in range(q + 1, groups):
-            for t in range(tiles):
+        inside = (lanes >= start) & (lanes < start + STEP)
+        base = []
+        for h in range(span):
+            unit = jnp.where(lanes - start == sub + 8 * h, 1.0, 0.0)
+            base.append([jnp.where(inside, unit, panel[q + h][t]) if t == tile else panel[q + h][t] for t in range(tiles)])
+        rows = [[spread(base[c // 8][t][c % 8 : c % 8 + 1, :]) for t in range(tiles)] for c in range(STEP)]
+        for g in range(q + span, groups):
+            for t in order:
                 here = jnp.where(inside, 0.0, panel[g][t]) if t == tile else panel[g][t]
-                panel[g][t] = here + sum(coef[c][g] * rows[c][t] for c in range(8))
+                panel[g][t] = here + total_of([coef[c][g] * rows[c][t] for c in range(STEP)])
+        for h in range(span):
+            root = lax.rsqrt(pivots[h])
+            low = [jnp.where(sub + 8 * h >= c, coef[c][q + h], 0.0) for c in range(min(STEP, 8 * h + 8))]
+            out.append([total_of([low[c] * rows[c][t] for c in range(len(low))]) * root for t in range(tiles)])
     return jnp.concatenate([jnp.concatenate(o, axis=1) for o in out], axis=0)
 
 
 def transform_kernel(gram_ref, ens_ref, out_ref):
     total = gram_ref.shape[0]
     half = total // 2
+    states = ens_ref[...].astype(F32).reshape(total, -1)
+    mean_state = jnp.sum(states, axis=0, keepdims=True) / total
+    anomalies = (states - mean_state).astype(BF16)
     row = lax.broadcasted_iota(jnp.int32, (total, total), 0)
     col = lax.broadcasted_iota(jnp.int32, (total, total), 1)
     given = gram_ref[...]
     extra = given[:half, half:]
-    cross = jnp.concatenate([extra[:, 0:1], extra[:, 1:2]], axis=0)
+    cross = jnp.concatenate([extra[:, 0:1], extra[:, 1:2]], axis=0).T
     mirror = given[half:, :half].T
     full = jnp.concatenate([jnp.concatenate([given[:half, :half], mirror], axis=1), given[half:, :]], axis=0)
     full = full + jnp.where(row == col, 1.0, 0.0)
     count = total // WIDE
     blocks = [full[WIDE * t : WIDE * (t + 1), :] for t in range(count)]
+    weight = jnp.zeros((1, total), F32)
     for s in range(count):
         r0, r1 = WIDE * s, WIDE * (s + 1)
         done = eliminate([blocks[s][8 * g : 8 * (g + 1), :] for g in range(WIDE // 8)], r0)
@@ -184,16 +212,11 @@
             for t in range(s + 1, count):
                 change = jnp.dot(turned[WIDE * t : WIDE * (t + 1), :], kept, precision=HIGHEST, preferred_element_type=F32)
                 blocks[t] = jnp.where(inside, 0.0, blocks[t]) - change
-    inverse = jnp.concatenate(blocks, axis=0)
-    solved = jnp.sum(inverse * cross.T, axis=1, keepdims=True)
-    weight = jnp.sum(inverse * solved, axis=0, keepdims=True)
-    rounded = (inverse + weight).astype(BF16).astype(F32)
-    centred = rounded - jnp.sum(rounded, axis=1, keepdims=True) / total + 1.0 / total
-    high = centred.astype(BF16)
-    rest = (centred - high.astype(F32)).astype(BF16)
-    states = ens_ref[...].reshape(total, -1)
-    both = jnp.dot(high, states, preferred_element_type=F32) + jnp.dot(rest, states, preferred_element_type=F32)
-    out_ref[...] = both.astype(BF16).reshape(out_ref.shape)
+        solved = jnp.sum(blocks[s] * cross, axis=1, keepdims=True)
+        weight = weight + jnp.sum(blocks[s] * solved, axis=0, keepdims=True)
+    turned = (jnp.concatenate(blocks, axis=0) + weight).astype(BF16)
+    change = jnp.dot(turned, anomalies, preferred_element_type=F32)
+    out_ref[...] = (mean_state + change).astype(BF16).reshape(out_ref.shape)
 
 
 def transform(gram_sum, shared):
@@ -226,9 +249,10 @@
     member_index = lax.axis_index(MEMBER)
     left = lax.ppermute(ens_t[:, -128:], SPACE, [(i, (i + 1) % space_count) for i in range(space_count)])
     right = lax.ppermute(ens_t[:, :128], SPACE, [((i + 1) % space_count, i) for i in range(space_count)])
+    state = jnp.pad(ens_t, ((0, 0), (128, 128)))
     state_local = rows // 128
     cols = jnp.mod(block_columns - space_index * state_local + 1, state_local * space_count)
-    shared = predict(cols, ens_t, left, right, operator_blocks, member_count)
+    shared = predict(cols, state, left, right, operator_blocks, member_count)
     shared = lax.all_to_all(shared, MEMBER, 0, 0, tiled=True)
     count = observed.shape[0] // member_count
     obs = lax.dynamic_slice_in_dim(observed, member_index * count, count)[None]

time: 123 us -> 120 us (0.976)
  Pallas kernels: 21 us -> 19.6 us
  transfers between devices with their start and end apart: 3 -> 3, of which waited for: 1 -> 1; matrix products, arithmetic and copies ran while one was open for 2% -> 3% of each run, Pallas kernels for 0% -> 0%
where the time goes in v4:
time: 120 us
  blocking collectives  73.3 us (61%)
  Pallas kernels  19.6 us (16%)
  starting transfers between devices  10.9 us (9%)
  waiting for transfers between devices  10.8 us (9%)
  local copies, waits for them, and re-layouts  4.26 us (4%)
    all_to_all x2, blocking collectives, to_all(): lax.all_to_all(jnp.broadcast_to(x[None], (count,) + x.shape), axes, 0, 0,...  40.3 us
    all_to_all x1, blocking collectives, local(): part = jnp.sum(lax.all_to_all(part, PLANE, 0, 0, tiled=True), axis=0)  18.8 us
    all_to_all x1, blocking collectives, local(): lax.all_to_all(transform(gram_sum, shared), MEMBER, 0, 0, tiled=True)  14.2 us
    all_to_all x1, waiting for transfers between devices, local(): shared = lax.all_to_all(shared, MEMBER, 0, 0, tiled=True)  10.8 us
    pallas_call x1, Pallas kernels, predict(): pl.pallas_call(predict_kernel, out_shape=jax.ShapeDtypeStruct((parts, mem...  9.87 us
    pallas_call x1, Pallas kernels, transform(): pl.pallas_call(transform_kernel, out_shape=jax.ShapeDtypeStruct(block, BF...  8.42 us
    all_to_all x1, starting transfers between devices, local(): shared = lax.all_to_all(shared, MEMBER, 0, 0, tiled=True)  4.04 us
    ppermute x1, starting transfers between devices, local(): lax.ppermute(ens_t[:, :128], SPACE, [((i + 1) % space_count, i) for i in...  3.85 us
  transfers between devices with their start and end apart: 3, of which 1 were waited for; matrix products, arithmetic and copies ran while one was open for 3% of the time, Pallas kernels for 0%

profile of v4, /device:TPU:1, one launch (start us, length us, event | category | flops | bytes accessed | tf_op | source)
XLA Modules:
  0.0 119.8 jit_solution(12276628802283312482)
XLA Ops:
  0.0 0.7 fusion.1
  0.7 3.0 %collective-permute-start = (bf16[16,128]{1,0:T(8,128)(2,1)S(1)}, bf16[16,128]{1,0:T(8,128)(2,1)S(1)}, u32[]{:S(2)}, u32[]{:S(2)}) collective-permute-start(bf16[16,128]{1,0:T(8,128)(2,1)S(1)} %get-tuple-element.6), channel_id=1, source_target_pairs={{0,16},{16,32},{32,48},{48,64},{64,80},{80,96},{96,112},{112,128},... | collective-permute-start | bytes 12296 | tf_op jit(solution)/shard_map/ppermute | solution.py:250
  3.7 3.9 %collective-permute-start.1 = (bf16[16,128]{1,0:T(8,128)(2,1)S(1)}, bf16[16,128]{1,0:T(8,128)(2,1)S(1)}, u32[]{:S(2)}, u32[]{:S(2)}) collective-permute-start(bf16[16,128]{1,0:T(8,128)(2,1)S(1)} %get-tuple-element.5), channel_id=1, source_target_pairs={{16,0},{32,16},{48,32},{64,48},{80,64},{96,80},{112,96},{128,112},... | collective-permute-start | bytes 12296 | tf_op jit(solution)/shard_map/ppermute | solution.py:251
  7.6 0.7 broadcast_subtract_fusion
  8.3 0.1 copy.14
  8.4 1.1 pad.4.state
  9.5 0.0 collective-permute-done.left_ref
  9.5 0.0 collective-permute-done.1.right_ref
  9.5 9.9 %shard_map.55 = bf16[16,16,2048]{2,1,0:T(8,128)(2,1)} custom-call(s32[64,8]{1,0:T(8,128)S(1)} %add_select_fusion.cols_ref, bf16[16,16640]{1,0:T(8,128)(2,1)S(1)} %pad.4.state, bf16[16,128]{1,0:T(8,128)(2,1)S(1)} %collective-permute-done.left_ref, bf16[16,128]{1,0:T(8,128)(2,1)S(1)} %collective-permute-done.1.right_ref, bf16[64,8,128,128]{3,2,1,0:T(8,128)(2,1)} %ops_ref.1), custom_call_target="tpu_custom_call" | custom-call | flops 268435456 | bytes 16777216 | tf_op jit(solution)/shard_map/pallas_call | solution.py:76
  19.4 4.0 %all-to-all-start = ((bf16[16,16,2048]{2,1,0:T(8,128)(2,1)}), bf16[16,16,2048]{2,1,0:T(8,128)(2,1)S(1)}, u32[]{:S(2)}, u32[]{:S(2)}) async-start(bf16[16,16,2048]{2,1,0:T(8,128)(2,1)} %shard_map.55), calls=%async_computation | async-start | bytes 2097152 | tf_op jit(solution)/shard_map/all_to_all | solution.py:256
  23.4 0.8 dynamic_slice.6
  24.2 0.8 dynamic_slice.7
  25.0 10.8 %all-to-all-done.pred_ref.ens_ref = bf16[16,16,2048]{2,1,0:T(8,128)(2,1)S(1)} async-done(((bf16[16,16,2048]{2,1,0:T(8,128)(2,1)}), bf16[16,16,2048]{2,1,0:T(8,128)(2,1)S(1)}, u32[]{:S(2)}, u32[]{:S(2)}) %all-to-all-start) | async-done | bytes 1048608 | tf_op jit(solution)/shard_map/all_to_all | solution.py:256
  35.7 1.4 %shard_map.56 = f32[256,256]{1,0:T(8,128)S(1)} custom-call(bf16[16,16,2048]{2,1,0:T(8,128)(2,1)S(1)} %all-to-all-done.pred_ref.ens_ref, f32[1,512]{1,0:T(1,128)S(1)} %bitcast.12, f32[1,512]{1,0:T(1,128)S(1)} %bitcast.13), custom_call_target="tpu_custom_call" | custom-call | tf_op jit(solution)/shard_map/pallas_call | solution.py:116
  37.1 18.8 %all_to_all.25 = f32[32,8,256]{2,1,0:T(8,128)S(1)} all-to-all(f32[32,8,256]{2,1,0:T(8,128)S(1)} %bitcast.10), channel_id=1, replica_groups=mesh['z'=16,'core'=2,'y'=4,'x'=4] {'core','y','x'}, dimensions={0} | all-to-all | bytes 524288 | tf_op jit(solution)/shard_map/all_to_all | solution.py:261
  56.0 24.8 %all_to_all.26 = f32[16,8,256]{2,1,0:T(8,128)S(1)} all-to-all(f32[16,8,256]{2,1,0:T(8,128)S(1)} %broadcast_in_dim.20), channel_id=1, replica_groups=mesh['z'=16,'core'=2,'y'=4,'x'=4] {'z'}, dimensions={0} | all-to-all | bytes 262144 | tf_op jit(solution)/shard_map/all_to_all | solution.py:237
  80.8 15.5 %all_to_all.27 = f32[32,8,256]{2,1,0:T(8,128)S(1)} all-to-all(f32[32,8,256]{2,1,0:T(8,128)S(1)} %broadcast_in_dim.21), channel_id=1, replica_groups=mesh['z'=16,'core'=2,'y'=4,'x'=4] {'core','y','x'}, dimensions={0} | all-to-all | bytes 524288 | tf_op jit(solution)/shard_map/all_to_all | solution.py:237
  96.3 8.4 %shard_map.57 = bf16[16,16,1024]{2,1,0:T(8,128)(2,1)S(1)} custom-call(f32[256,256]{1,0:T(8,128)S(1)} %bitcast.11, bf16[16,16,2048]{2,1,0:T(8,128)(2,1)S(1)} %all-to-all-done.pred_ref.ens_ref), custom_call_target="tpu_custom_call" | custom-call | tf_op jit(solution)/shard_map/pallas_call | solution.py:226
  104.8 14.2 %all_to_all.28 = bf16[16,16,1024]{2,1,0:T(8,128)(2,1)S(1)} all-to-all(bf16[16,16,1024]{2,1,0:T(8,128)(2,1)S(1)} %shard_map.57), channel_id=1, replica_groups=mesh['z'=16,'core'=2,'y'=4,'x'=4] {'y','x'}, dimensions={0} | all-to-all | bytes 1048576 | tf_op jit(solution)/shard_map/all_to_all | solution.py:264
  118.9 0.8 copy.16
  (5 shorter events, 0.1 us)
Async XLA Ops:
  0.7 8.8 %collective-permute-start = (bf16[16,128]{1,0:T(8,128)(2,1)S(1)}, bf16[16,128]{1,0:T(8,128)(2,1)S(1)}, u32[]{:S(2)}, u32[]{:S(2)}) collective-permute-start(bf16[16,128]{1,0:T(8,128)(2,1)S(1)} %get-tuple-element.6), channel_id=1, source_target_pairs={{0,16},{16,32},{32,48},{48,64},{64,80},{80,96},{96,112},{112,128},... | collective-permute-start | bytes 12296 | tf_op jit(solution)/shard_map/ppermute | solution.py:250
  3.7 5.8 %collective-permute-start.1 = (bf16[16,128]{1,0:T(8,128)(2,1)S(1)}, bf16[16,128]{1,0:T(8,128)(2,1)S(1)}, u32[]{:S(2)}, u32[]{:S(2)}) collective-permute-start(bf16[16,128]{1,0:T(8,128)(2,1)S(1)} %get-tuple-element.5), channel_id=1, source_target_pairs={{16,0},{32,16},{48,32},{64,48},{80,64},{96,80},{112,96},{128,112},... | collective-permute-start | bytes 12296 | tf_op jit(solution)/shard_map/ppermute | solution.py:251
  19.4 16.4 %all-to-all-start = ((bf16[16,16,2048]{2,1,0:T(8,128)(2,1)}), bf16[16,16,2048]{2,1,0:T(8,128)(2,1)S(1)}, u32[]{:S(2)}, u32[]{:S(2)}) async-start(bf16[16,16,2048]{2,1,0:T(8,128)(2,1)} %shard_map.55), calls=%async_computation | async-start | bytes 2097152 | tf_op jit(solution)/shard_map/all_to_all | solution.py:256

commit v5 on v4

--- a/solution.py
+++ b/solution.py
@@ -91,7 +91,7 @@
 
 
 def gram_kernel(pred_ref, obs_ref, err_ref, out_ref):
-    total = out_ref.shape[0]
+    total = pred_ref.shape[0] * pred_ref.shape[1]
     half = total // 2
     width = obs_ref.shape[1]
     pred = (pred_ref[:, :, :width].astype(F32) + pred_ref[:, :, width:].astype(F32)).reshape(total, width)
@@ -99,14 +99,22 @@
     scale = err_ref[...] * math.sqrt(total - 1)
     white = (pred - mean) / scale
     departure = (obs_ref[...] - mean) / scale
-    row = lax.broadcasted_iota(jnp.int32, (half, white.shape[1]), 0)
-    first = jnp.where(row == 0, departure, 0.0)
-    second = jnp.where(row == 1, departure, 0.0)
+    edge = lax.broadcasted_iota(jnp.int32, (8, width), 0)
     top, low = white[:half], white[half:]
     dot = functools.partial(lax.dot_general, dimension_numbers=NT, precision=HIGHEST, preferred_element_type=F32)
-    out_ref[:half, :half] = dot(top, top)
-    out_ref[:half, half:] = dot(top, first) + dot(low, second)
-    out_ref[half:, :] = dot(low, white)
+    cross = dot(jnp.where(edge == 0, departure, 0.0), white)[:1]
+    first, second = dot(top, top), dot(low, low)
+    row = lax.broadcasted_iota(jnp.int32, (half, half), 0)
+    col = lax.broadcasted_iota(jnp.int32, (half, half), 1)
+    diagonal = jnp.sum(jnp.where(row == col, second, 0.0), axis=0, keepdims=True)
+    halves = [dot(low, top), jnp.where(row >= col, first, second)]
+    extra = [diagonal, cross[:, :half], cross[:, half:]]
+    for i in range(out_ref.shape[0]):
+        part = halves[8 * i // half]
+        for r in range(8):
+            at = (8 * i + r) % half
+            out_ref[i, :, 128 * r : 128 * (r + 1)] = part[at : at + 1, :]
+        out_ref[i, :, 1024:] = extra[i] if i < len(extra) else jnp.zeros((1, 128), F32)
 
 
 def gram(shared, obs, err):
@@ -115,10 +123,10 @@
     row = pl.BlockSpec((1, width), lambda i: (0, 0))
     return pl.pallas_call(
         gram_kernel,
-        out_shape=jax.ShapeDtypeStruct((total, total), F32),
+        out_shape=jax.ShapeDtypeStruct((total // 8, 1, 1152), F32),
         grid=(1,),
         in_specs=[pl.BlockSpec((sources, members, 2 * width), lambda i: (0, 0, 0)), row, row],
-        out_specs=pl.BlockSpec((total, total), lambda i: (0, 0)),
+        out_specs=pl.BlockSpec((total // 8, 1, 1152), lambda i: (0, 0, 0)),
         compiler_params=pltpu.CompilerParams(vmem_limit_bytes=16 * 2**20),
     )(shared, obs, err)
 
@@ -183,19 +191,28 @@
     return jnp.concatenate([jnp.concatenate(o, axis=1) for o in out], axis=0)
 
 
-def transform_kernel(gram_ref, ens_ref, out_ref):
-    total = gram_ref.shape[0]
+def transform_kernel(gram_ref, ens_ref, out_ref, packed):
+    total = 8 * gram_ref.shape[0]
     half = total // 2
     states = ens_ref[...].astype(F32).reshape(total, -1)
     mean_state = jnp.sum(states, axis=0, keepdims=True) / total
     anomalies = (states - mean_state).astype(BF16)
     row = lax.broadcasted_iota(jnp.int32, (total, total), 0)
     col = lax.broadcasted_iota(jnp.int32, (total, total), 1)
-    given = gram_ref[...]
-    extra = given[:half, half:]
-    cross = jnp.concatenate([extra[:, 0:1], extra[:, 1:2]], axis=0).T
-    mirror = given[half:, :half].T
-    full = jnp.concatenate([jnp.concatenate([given[:half, :half], mirror], axis=1), given[half:, :]], axis=0)
+    for i in range(total // 8):
+        for r in range(8):
+            packed[8 * i + r : 8 * i + r + 1, :] = gram_ref[i, :, 128 * r : 128 * (r + 1)]
+    diagonal, *cross = [gram_ref[i, :, 1024:] for i in range(3)]
+    cross = jnp.concatenate(cross, axis=1)
+    block, mixed = packed[:half], packed[half:]
+    flipped = mixed.T
+    above = (row < col)[:half, :half]
+    below = (row > col)[:half, :half]
+    first = jnp.where(above, flipped, mixed)
+    second = jnp.where(above, mixed, jnp.where(below, flipped, diagonal))
+    full = jnp.concatenate(
+        [jnp.concatenate([first, block.T], axis=1), jnp.concatenate([block, second], axis=1)], axis=0
+    )
     full = full + jnp.where(row == col, 1.0, 0.0)
     count = total // WIDE
     blocks = [full[WIDE * t : WIDE * (t + 1), :] for t in range(count)]
@@ -220,15 +237,15 @@
 
 
 def transform(gram_sum, shared):
-    total = gram_sum.shape[0]
     sources, members, width = shared.shape
     block = (sources, members, width // 2)
     return pl.pallas_call(
         transform_kernel,
         out_shape=jax.ShapeDtypeStruct(block, BF16),
         grid=(1,),
-        in_specs=[pl.BlockSpec((total, total), lambda i: (0, 0)), pl.BlockSpec(block, lambda i: (0, 0, 1))],
+        in_specs=[pl.BlockSpec(gram_sum.shape, lambda i: (0, 0, 0)), pl.BlockSpec(block, lambda i: (0, 0, 1))],
         out_specs=pl.BlockSpec(block, lambda i: (0, 0, 0)),
+        scratch_shapes=[pltpu.VMEM((sources * members, sources * members // 2), F32)],
         compiler_params=pltpu.CompilerParams(vmem_limit_bytes=16 * 2**20),
     )(gram_sum, shared)
 
@@ -257,10 +274,10 @@
     count = observed.shape[0] // member_count
     obs = lax.dynamic_slice_in_dim(observed, member_index * count, count)[None]
     err = lax.dynamic_slice_in_dim(error_scale, member_index * count, count)[None]
-    part = gram(shared, obs, err).reshape(plane_count, -1, total)
+    part = gram(shared, obs, err)
     part = jnp.sum(lax.all_to_all(part, PLANE, 0, 0, tiled=True), axis=0)
     part = jnp.sum(to_all(part, "z", z_count), axis=0)
-    gram_sum = to_all(part, PLANE, plane_count).reshape(total, total)
+    gram_sum = to_all(part, PLANE, plane_count).reshape(plane_count, 1, -1)
     analysis = lax.all_to_all(transform(gram_sum, shared), MEMBER, 0, 0, tiled=True)
     return analysis.transpose(1, 0, 2).reshape(members, rows).T
 

time: 120 us -> 117 us (0.975)
  blocking collectives: 73.3 us -> 69.4 us
    all_to_all x2, blocking collectives: 40.3 us -> 37.6 us  [to_all(): lax.all_to_all(jnp.broadcast_to(x[None], (count,) + x.shape), axes, 0, 0,...]
where the time goes in v5:
time: 117 us; the launch traced here: 116 us
  blocking collectives  69.4 us (59%)
  Pallas kernels  19.6 us (17%)
  starting transfers between devices  10.9 us (9%)
  waiting for transfers between devices  10.8 us (9%)
  local copies, waits for them, and re-layouts  4.34 us (4%)
    all_to_all x2, blocking collectives, to_all(): lax.all_to_all(jnp.broadcast_to(x[None], (count,) + x.shape), axes, 0, 0,...  37.6 us
    all_to_all x1, blocking collectives, local(): part = jnp.sum(lax.all_to_all(part, PLANE, 0, 0, tiled=True), axis=0)  18.2 us
    all_to_all x1, blocking collectives, local(): lax.all_to_all(transform(gram_sum, shared), MEMBER, 0, 0, tiled=True)  13.7 us
    all_to_all x1, waiting for transfers between devices, local(): shared = lax.all_to_all(shared, MEMBER, 0, 0, tiled=True)  10.8 us
    pallas_call x1, Pallas kernels, predict(): pl.pallas_call(predict_kernel, out_shape=jax.ShapeDtypeStruct((parts, mem...  9.87 us
    pallas_call x1, Pallas kernels, transform(): pl.pallas_call(transform_kernel, out_shape=jax.ShapeDtypeStruct(block, BF...  8.49 us
    all_to_all x1, starting transfers between devices, local(): shared = lax.all_to_all(shared, MEMBER, 0, 0, tiled=True)  4.04 us
    ppermute x1, starting transfers between devices, local(): lax.ppermute(ens_t[:, :128], SPACE, [((i + 1) % space_count, i) for i in...  3.85 us
  transfers between devices with their start and end apart: 3, of which 1 were waited for; matrix products, arithmetic and copies ran while one was open for 3% of the time, Pallas kernels for 0%

profile of v5, /device:TPU:1, one launch (start us, length us, event | category | flops | bytes accessed | tf_op | source)
XLA Modules:
  0.0 116.0 jit_solution(3674824915218916925)
XLA Ops:
  0.0 0.7 fusion.1
  0.7 3.0 %collective-permute-start = (bf16[16,128]{1,0:T(8,128)(2,1)S(1)}, bf16[16,128]{1,0:T(8,128)(2,1)S(1)}, u32[]{:S(2)}, u32[]{:S(2)}) collective-permute-start(bf16[16,128]{1,0:T(8,128)(2,1)S(1)} %get-tuple-element.6), channel_id=1, source_target_pairs={{0,16},{16,32},{32,48},{48,64},{64,80},{80,96},{96,112},{112,128},... | collective-permute-start | bytes 12296 | tf_op jit(solution)/shard_map/ppermute | solution.py:267
  3.7 3.9 %collective-permute-start.1 = (bf16[16,128]{1,0:T(8,128)(2,1)S(1)}, bf16[16,128]{1,0:T(8,128)(2,1)S(1)}, u32[]{:S(2)}, u32[]{:S(2)}) collective-permute-start(bf16[16,128]{1,0:T(8,128)(2,1)S(1)} %get-tuple-element.5), channel_id=1, source_target_pairs={{16,0},{32,16},{48,32},{64,48},{80,64},{96,80},{112,96},{128,112},... | collective-permute-start | bytes 12296 | tf_op jit(solution)/shard_map/ppermute | solution.py:268
  7.6 0.7 broadcast_subtract_fusion
  8.3 0.1 copy.18
  8.4 1.1 pad.4.state
  9.5 0.0 collective-permute-done.left_ref
  9.5 0.0 collective-permute-done.1.right_ref
  9.5 9.9 %shard_map.55 = bf16[16,16,2048]{2,1,0:T(8,128)(2,1)} custom-call(s32[64,8]{1,0:T(8,128)S(1)} %add_select_fusion.cols_ref, bf16[16,16640]{1,0:T(8,128)(2,1)S(1)} %pad.4.state, bf16[16,128]{1,0:T(8,128)(2,1)S(1)} %collective-permute-done.left_ref, bf16[16,128]{1,0:T(8,128)(2,1)S(1)} %collective-permute-done.1.right_ref, bf16[64,8,128,128]{3,2,1,0:T(8,128)(2,1)} %ops_ref.1), custom_call_target="tpu_custom_call" | custom-call | flops 268435456 | bytes 16777216 | tf_op jit(solution)/shard_map/pallas_call | solution.py:76
  19.4 4.0 %all-to-all-start = ((bf16[16,16,2048]{2,1,0:T(8,128)(2,1)}), bf16[16,16,2048]{2,1,0:T(8,128)(2,1)S(1)}, u32[]{:S(2)}, u32[]{:S(2)}) async-start(bf16[16,16,2048]{2,1,0:T(8,128)(2,1)} %shard_map.55), calls=%async_computation | async-start | bytes 2097152 | tf_op jit(solution)/shard_map/all_to_all | solution.py:273
  23.4 0.8 dynamic_slice.6
  24.2 0.8 dynamic_slice.7
  25.0 10.8 %all-to-all-done.pred_ref.ens_ref = bf16[16,16,2048]{2,1,0:T(8,128)(2,1)S(1)} async-done(((bf16[16,16,2048]{2,1,0:T(8,128)(2,1)}), bf16[16,16,2048]{2,1,0:T(8,128)(2,1)S(1)}, u32[]{:S(2)}, u32[]{:S(2)}) %all-to-all-start) | async-done | bytes 1048608 | tf_op jit(solution)/shard_map/all_to_all | solution.py:273
  35.7 1.3 %shard_map.56 = f32[32,1,1152]{2,1,0:T(1,128)S(1)} custom-call(bf16[16,16,2048]{2,1,0:T(8,128)(2,1)S(1)} %all-to-all-done.pred_ref.ens_ref, f32[1,512]{1,0:T(1,128)S(1)} %bitcast.8, f32[1,512]{1,0:T(1,128)S(1)} %bitcast.9), custom_call_target="tpu_custom_call" | custom-call | tf_op jit(solution)/shard_map/pallas_call | solution.py:124
  37.0 18.2 %all_to_all.25 = f32[32,1,1152]{2,1,0:T(1,128)S(1)} all-to-all(f32[32,1,1152]{2,1,0:T(1,128)S(1)} %shard_map.56), channel_id=1, replica_groups=mesh['z'=16,'core'=2,'y'=4,'x'=4] {'core','y','x'}, dimensions={0} | all-to-all | bytes 294912 | tf_op jit(solution)/shard_map/all_to_all | solution.py:278
  55.2 0.1 reduce_sum.18
  55.3 24.6 %all_to_all.26 = f32[16,1,1152]{2,1,0:T(1,128)S(1)} all-to-all(f32[16,1,1152]{2,1,0:T(1,128)S(1)} %broadcast_in_dim.20), channel_id=1, replica_groups=mesh['z'=16,'core'=2,'y'=4,'x'=4] {'z'}, dimensions={0} | all-to-all | bytes 147456 | tf_op jit(solution)/shard_map/all_to_all | solution.py:254
  79.9 0.1 reduce_sum.19
  80.0 0.1 broadcast_in_dim.21
  80.0 13.0 %all_to_all.27.gram_ref = f32[32,1,1152]{2,1,0:T(1,128)S(1)} all-to-all(f32[32,1,1152]{2,1,0:T(1,128)S(1)} %broadcast_in_dim.21), channel_id=1, replica_groups=mesh['z'=16,'core'=2,'y'=4,'x'=4] {'core','y','x'}, dimensions={0} | all-to-all | bytes 294912 | tf_op jit(solution)/shard_map/all_to_all | solution.py:254
  93.1 8.5 %shard_map.57 = bf16[16,16,1024]{2,1,0:T(8,128)(2,1)S(1)} custom-call(f32[32,1,1152]{2,1,0:T(1,128)S(1)} %all_to_all.27.gram_ref, bf16[16,16,2048]{2,1,0:T(8,128)(2,1)S(1)} %all-to-all-done.pred_ref.ens_ref), custom_call_target="tpu_custom_call" | custom-call | tf_op jit(solution)/shard_map/pallas_call | solution.py:242
  101.6 13.7 %all_to_all.28 = bf16[16,16,1024]{2,1,0:T(8,128)(2,1)S(1)} all-to-all(bf16[16,16,1024]{2,1,0:T(8,128)(2,1)S(1)} %shard_map.57), channel_id=1, replica_groups=mesh['z'=16,'core'=2,'y'=4,'x'=4] {'y','x'}, dimensions={0} | all-to-all | bytes 1048576 | tf_op jit(solution)/shard_map/all_to_all | solution.py:281
  115.2 0.8 copy.22
  (2 shorter events, 0.1 us)
Async XLA Ops:
  0.7 8.8 %collective-permute-start = (bf16[16,128]{1,0:T(8,128)(2,1)S(1)}, bf16[16,128]{1,0:T(8,128)(2,1)S(1)}, u32[]{:S(2)}, u32[]{:S(2)}) collective-permute-start(bf16[16,128]{1,0:T(8,128)(2,1)S(1)} %get-tuple-element.6), channel_id=1, source_target_pairs={{0,16},{16,32},{32,48},{48,64},{64,80},{80,96},{96,112},{112,128},... | collective-permute-start | bytes 12296 | tf_op jit(solution)/shard_map/ppermute | solution.py:267
  3.7 5.8 %collective-permute-start.1 = (bf16[16,128]{1,0:T(8,128)(2,1)S(1)}, bf16[16,128]{1,0:T(8,128)(2,1)S(1)}, u32[]{:S(2)}, u32[]{:S(2)}) collective-permute-start(bf16[16,128]{1,0:T(8,128)(2,1)S(1)} %get-tuple-element.5), channel_id=1, source_target_pairs={{16,0},{32,16},{48,32},{64,48},{80,64},{96,80},{112,96},{128,112},... | collective-permute-start | bytes 12296 | tf_op jit(solution)/shard_map/ppermute | solution.py:268
  19.4 16.4 %all-to-all-start = ((bf16[16,16,2048]{2,1,0:T(8,128)(2,1)}), bf16[16,16,2048]{2,1,0:T(8,128)(2,1)S(1)}, u32[]{:S(2)}, u32[]{:S(2)}) async-start(bf16[16,16,2048]{2,1,0:T(8,128)(2,1)} %shard_map.55), calls=%async_computation | async-start | bytes 2097152 | tf_op jit(solution)/shard_map/all_to_all | solution.py:273

commit v6 on v5

--- a/solution.py
+++ b/solution.py
@@ -21,7 +21,9 @@
 def predict_kernel(cols_ref, state, left_ref, right_ref, ops_ref, out_ref, weights, staged, sems, out_sems, ens_sems):
     parts = out_ref.shape[0]
     rows = state.shape[1] - 256
+    members = state.shape[0]
     group = ops_ref.shape[0] // parts
+    sub = lax.broadcasted_iota(jnp.int32, (members, 128), 0)
     width, share = 128 * group, rows // parts
 
     def fetch(c):
@@ -30,11 +32,11 @@
     for c in range(4):
         fetch(c).start()
     def deliver(c):
-        return pltpu.make_async_copy(staged.at[c], out_ref.at[c, :, pl.ds(0, 2 * width)], out_sems.at[c])
+        return pltpu.make_async_copy(staged.at[c], out_ref.at[c, :, pl.ds(0, width + 128)], out_sems.at[c])
 
     def pass_on(c):
         chunk = state.at[:, pl.ds(128 + c * share, share)]
-        return pltpu.make_async_copy(chunk, out_ref.at[c, :, pl.ds(2 * width, share)], ens_sems.at[c])
+        return pltpu.make_async_copy(chunk, out_ref.at[c, :, pl.ds(width + 128, share)], ens_sems.at[c])
 
     def pick(at):
         inner = state[:, pl.ds(pl.multiple_of(at * 128, 128), 128)]
@@ -50,6 +52,7 @@
         def _():
             fetch(c + 4).start()
 
+        means = jnp.zeros((members, 128), F32)
         for o in range(group):
             block = c * group + o
             picked = [pick(cols_ref[block, k]) for k in range(8)]
@@ -57,9 +60,13 @@
             value = lax.dot_general(
                 jnp.concatenate(picked, axis=1), jnp.concatenate(rows_of, axis=1), NT, preferred_element_type=F32
             )
-            high = value.astype(BF16)
-            staged[c, :, 128 * o : 128 * (o + 1)] = high
-            staged[c, :, width + 128 * o : width + 128 * (o + 1)] = (value - high.astype(F32)).astype(BF16)
+            mean = jnp.sum(value, axis=0, keepdims=True) / members
+            staged[c, :, 128 * o : 128 * (o + 1)] = (value - mean).astype(BF16)
+            for part in range(3):
+                taken = mean.astype(BF16).astype(F32)
+                means = jnp.where(sub == group * part + o, taken, means)
+                mean = mean - taken
+        staged[c, :, width:] = means.astype(BF16)
         deliver(c).start()
         return carry
 
@@ -75,12 +82,12 @@
     outside, inside = pl.BlockSpec(memory_space=pltpu.HBM), pl.BlockSpec(memory_space=pltpu.VMEM)
     return pl.pallas_call(
         predict_kernel,
-        out_shape=jax.ShapeDtypeStruct((parts, members, (2 * oblocks * 128 + rows) // parts), BF16),
+        out_shape=jax.ShapeDtypeStruct((parts, members, (oblocks * 128 + rows) // parts + 128), BF16),
         in_specs=[pl.BlockSpec(memory_space=pltpu.SMEM), inside, inside, inside, outside],
         out_specs=outside,
         scratch_shapes=[
             pltpu.VMEM(ops.shape, BF16),
-            pltpu.VMEM((parts, members, 2 * oblocks * 128 // parts), BF16),
+            pltpu.VMEM((parts, members, oblocks * 128 // parts + 128), BF16),
             pltpu.SemaphoreType.DMA((parts,)),
             pltpu.SemaphoreType.DMA((parts,)),
             pltpu.SemaphoreType.DMA((parts,)),
@@ -94,7 +101,11 @@
     total = pred_ref.shape[0] * pred_ref.shape[1]
     half = total // 2
     width = obs_ref.shape[1]
-    pred = (pred_ref[:, :, :width].astype(F32) + pred_ref[:, :, width:].astype(F32)).reshape(total, width)
+    parts = pred_ref[:, :, width : width + 128].astype(F32)
+    group = width // 128
+    means = parts[:, :group] + parts[:, group : 2 * group] + parts[:, 2 * group : 3 * group]
+    means = jnp.concatenate([means[:, o : o + 1] for o in range(group)], axis=2)
+    pred = (pred_ref[:, :, :width].astype(F32) + means).reshape(total, width)
     mean = jnp.sum(pred, axis=0, keepdims=True) / total
     scale = err_ref[...] * math.sqrt(total - 1)
     white = (pred - mean) / scale
@@ -118,15 +129,10 @@
 
 
 def gram(shared, obs, err):
-    sources, members = shared.shape[:2]
-    total, width = sources * members, obs.shape[1]
-    row = pl.BlockSpec((1, width), lambda i: (0, 0))
+    total = shared.shape[0] * shared.shape[1]
     return pl.pallas_call(
         gram_kernel,
         out_shape=jax.ShapeDtypeStruct((total // 8, 1, 1152), F32),
-        grid=(1,),
-        in_specs=[pl.BlockSpec((sources, members, 2 * width), lambda i: (0, 0, 0)), row, row],
-        out_specs=pl.BlockSpec((total // 8, 1, 1152), lambda i: (0, 0, 0)),
         compiler_params=pltpu.CompilerParams(vmem_limit_bytes=16 * 2**20),
     )(shared, obs, err)
 
@@ -194,7 +200,7 @@
 def transform_kernel(gram_ref, ens_ref, out_ref, packed):
     total = 8 * gram_ref.shape[0]
     half = total // 2
-    states = ens_ref[...].astype(F32).reshape(total, -1)
+    states = ens_ref[:, :, ens_ref.shape[2] - out_ref.shape[2] :].astype(F32).reshape(total, -1)
     mean_state = jnp.sum(states, axis=0, keepdims=True) / total
     anomalies = (states - mean_state).astype(BF16)
     row = lax.broadcasted_iota(jnp.int32, (total, total), 0)
@@ -236,15 +242,11 @@
     out_ref[...] = (mean_state + change).astype(BF16).reshape(out_ref.shape)
 
 
-def transform(gram_sum, shared):
-    sources, members, width = shared.shape
-    block = (sources, members, width // 2)
+def transform(gram_sum, shared, width):
+    sources, members = shared.shape[:2]
     return pl.pallas_call(
         transform_kernel,
-        out_shape=jax.ShapeDtypeStruct(block, BF16),
-        grid=(1,),
-        in_specs=[pl.BlockSpec(gram_sum.shape, lambda i: (0, 0, 0)), pl.BlockSpec(block, lambda i: (0, 0, 1))],
-        out_specs=pl.BlockSpec(block, lambda i: (0, 0, 0)),
+        out_shape=jax.ShapeDtypeStruct((sources, members, width), BF16),
         scratch_shapes=[pltpu.VMEM((sources * members, sources * members // 2), F32)],
         compiler_params=pltpu.CompilerParams(vmem_limit_bytes=16 * 2**20),
     )(gram_sum, shared)
@@ -278,7 +280,7 @@
     part = jnp.sum(lax.all_to_all(part, PLANE, 0, 0, tiled=True), axis=0)
     part = jnp.sum(to_all(part, "z", z_count), axis=0)
     gram_sum = to_all(part, PLANE, plane_count).reshape(plane_count, 1, -1)
-    analysis = lax.all_to_all(transform(gram_sum, shared), MEMBER, 0, 0, tiled=True)
+    analysis = lax.all_to_all(transform(gram_sum, shared, rows // member_count), MEMBER, 0, 0, tiled=True)
     return analysis.transpose(1, 0, 2).reshape(members, rows).T
 
 

time: 117 us -> 114 us (0.974)
  waiting for transfers between devices: 10.8 us -> 9.36 us
  blocking collectives: 69.4 us -> 68.2 us
    all_to_all x2, blocking collectives: 37.6 us -> 36.1 us  [to_all(): lax.all_to_all(jnp.broadcast_to(x[None], (count,) + x.shape), axes, 0, 0,...]
    all_to_all x1, waiting for transfers between devices: 10.8 us -> 9.36 us  [local(): shared = lax.all_to_all(shared, MEMBER, 0, 0, tiled=True)]
where the time goes in v6:
time: 114 us
  blocking collectives  68.2 us (60%)
  Pallas kernels  19.8 us (17%)
  starting transfers between devices  10.9 us (10%)
  waiting for transfers between devices  9.36 us (8%)
  local copies, waits for them, and re-layouts  4.34 us (4%)
    all_to_all x2, blocking collectives, to_all(): lax.all_to_all(jnp.broadcast_to(x[None], (count,) + x.shape), axes, 0, 0,...  36.1 us
    all_to_all x1, blocking collectives, local(): part = jnp.sum(lax.all_to_all(part, PLANE, 0, 0, tiled=True), axis=0)  18.5 us
    all_to_all x1, blocking collectives, local(): lax.all_to_all(transform(gram_sum, shared, rows // member_count), MEMBER,...  13.7 us
    pallas_call x1, Pallas kernels, predict(): pl.pallas_call(predict_kernel, out_shape=jax.ShapeDtypeStruct((parts, mem...  10.1 us
    all_to_all x1, waiting for transfers between devices, local(): shared = lax.all_to_all(shared, MEMBER, 0, 0, tiled=True)  9.36 us
    pallas_call x1, Pallas kernels, transform(): pl.pallas_call(transform_kernel, out_shape=jax.ShapeDtypeStruct((sources,...  8.47 us
    all_to_all x1, starting transfers between devices, local(): shared = lax.all_to_all(shared, MEMBER, 0, 0, tiled=True)  4.04 us
    ppermute x1, starting transfers between devices, local(): lax.ppermute(ens_t[:, :128], SPACE, [((i + 1) % space_count, i) for i in...  3.85 us
  transfers between devices with their start and end apart: 3, of which 1 were waited for; matrix products, arithmetic and copies ran while one was open for 3% of the time, Pallas kernels for 0%

profile of v6, /device:TPU:1, one launch (start us, length us, event | category | flops | bytes accessed | tf_op | source)
XLA Modules:
  0.0 113.6 jit_solution(268495635590564579)
XLA Ops:
  0.0 0.7 fusion.1
  0.7 3.0 %collective-permute-start = (bf16[16,128]{1,0:T(8,128)(2,1)S(1)}, bf16[16,128]{1,0:T(8,128)(2,1)S(1)}, u32[]{:S(2)}, u32[]{:S(2)}) collective-permute-start(bf16[16,128]{1,0:T(8,128)(2,1)S(1)} %get-tuple-element.6), channel_id=1, source_target_pairs={{0,16},{16,32},{32,48},{48,64},{64,80},{80,96},{96,112},{112,128},... | collective-permute-start | bytes 12296 | tf_op jit(solution)/shard_map/ppermute | solution.py:269
  3.7 3.9 %collective-permute-start.1 = (bf16[16,128]{1,0:T(8,128)(2,1)S(1)}, bf16[16,128]{1,0:T(8,128)(2,1)S(1)}, u32[]{:S(2)}, u32[]{:S(2)}) collective-permute-start(bf16[16,128]{1,0:T(8,128)(2,1)S(1)} %get-tuple-element.5), channel_id=1, source_target_pairs={{16,0},{32,16},{48,32},{64,48},{80,64},{96,80},{112,96},{128,112},... | collective-permute-start | bytes 12296 | tf_op jit(solution)/shard_map/ppermute | solution.py:270
  7.6 0.7 broadcast_subtract_fusion
  8.3 0.1 copy.18
  8.4 1.1 pad.4.state
  9.5 0.0 collective-permute-done.left_ref
  9.5 0.0 collective-permute-done.1.right_ref
  9.5 10.1 %shard_map.55 = bf16[16,16,1664]{2,1,0:T(8,128)(2,1)} custom-call(s32[64,8]{1,0:T(8,128)S(1)} %add_select_fusion.cols_ref, bf16[16,16640]{1,0:T(8,128)(2,1)S(1)} %pad.4.state, bf16[16,128]{1,0:T(8,128)(2,1)S(1)} %collective-permute-done.left_ref, bf16[16,128]{1,0:T(8,128)(2,1)S(1)} %collective-permute-done.1.right_ref, bf16[64,8,128,128]{3,2,1,0:T(8,128)(2,1)} %ops_ref.1), custom_call_target="tpu_custom_call" | custom-call | flops 268435456 | bytes 16777216 | tf_op jit(solution)/shard_map/pallas_call | solution.py:83
  19.6 4.0 %all-to-all-start = ((bf16[16,16,1664]{2,1,0:T(8,128)(2,1)}), bf16[16,16,1664]{2,1,0:T(8,128)(2,1)S(1)}, u32[]{:S(2)}, u32[]{:S(2)}) async-start(bf16[16,16,1664]{2,1,0:T(8,128)(2,1)} %shard_map.55), calls=%async_computation | async-start | bytes 1703936 | tf_op jit(solution)/shard_map/all_to_all | solution.py:275
  23.6 0.8 dynamic_slice.6
  24.4 0.8 dynamic_slice.7
  25.1 9.4 %all-to-all-done.pred_ref.ens_ref = bf16[16,16,1664]{2,1,0:T(8,128)(2,1)S(1)} async-done(((bf16[16,16,1664]{2,1,0:T(8,128)(2,1)}), bf16[16,16,1664]{2,1,0:T(8,128)(2,1)S(1)}, u32[]{:S(2)}, u32[]{:S(2)}) %all-to-all-start) | async-done | bytes 852000 | tf_op jit(solution)/shard_map/all_to_all | solution.py:275
  34.5 1.3 %shard_map.56 = f32[32,1,1152]{2,1,0:T(1,128)S(1)} custom-call(bf16[16,16,1664]{2,1,0:T(8,128)(2,1)S(1)} %all-to-all-done.pred_ref.ens_ref, f32[1,512]{1,0:T(1,128)S(1)} %bitcast.8, f32[1,512]{1,0:T(1,128)S(1)} %bitcast.9), custom_call_target="tpu_custom_call" | custom-call | tf_op jit(solution)/shard_map/pallas_call | solution.py:133
  35.8 18.5 %all_to_all.25 = f32[32,1,1152]{2,1,0:T(1,128)S(1)} all-to-all(f32[32,1,1152]{2,1,0:T(1,128)S(1)} %shard_map.56), channel_id=1, replica_groups=mesh['z'=16,'core'=2,'y'=4,'x'=4] {'core','y','x'}, dimensions={0} | all-to-all | bytes 294912 | tf_op jit(solution)/shard_map/all_to_all | solution.py:280
  54.3 0.1 reduce_sum.18
  54.5 23.0 %all_to_all.26 = f32[16,1,1152]{2,1,0:T(1,128)S(1)} all-to-all(f32[16,1,1152]{2,1,0:T(1,128)S(1)} %broadcast_in_dim.20), channel_id=1, replica_groups=mesh['z'=16,'core'=2,'y'=4,'x'=4] {'z'}, dimensions={0} | all-to-all | bytes 147456 | tf_op jit(solution)/shard_map/all_to_all | solution.py:256
  77.5 0.1 reduce_sum.19
  77.6 0.1 broadcast_in_dim.21
  77.6 13.0 %all_to_all.27.gram_ref = f32[32,1,1152]{2,1,0:T(1,128)S(1)} all-to-all(f32[32,1,1152]{2,1,0:T(1,128)S(1)} %broadcast_in_dim.21), channel_id=1, replica_groups=mesh['z'=16,'core'=2,'y'=4,'x'=4] {'core','y','x'}, dimensions={0} | all-to-all | bytes 294912 | tf_op jit(solution)/shard_map/all_to_all | solution.py:256
  90.7 8.5 %shard_map.57 = bf16[16,16,1024]{2,1,0:T(8,128)(2,1)S(1)} custom-call(f32[32,1,1152]{2,1,0:T(1,128)S(1)} %all_to_all.27.gram_ref, bf16[16,16,1664]{2,1,0:T(8,128)(2,1)S(1)} %all-to-all-done.pred_ref.ens_ref), custom_call_target="tpu_custom_call" | custom-call | tf_op jit(solution)/shard_map/pallas_call | solution.py:247
  99.1 13.7 %all_to_all.28 = bf16[16,16,1024]{2,1,0:T(8,128)(2,1)S(1)} all-to-all(bf16[16,16,1024]{2,1,0:T(8,128)(2,1)S(1)} %shard_map.57), channel_id=1, replica_groups=mesh['z'=16,'core'=2,'y'=4,'x'=4] {'y','x'}, dimensions={0} | all-to-all | bytes 1048576 | tf_op jit(solution)/shard_map/all_to_all | solution.py:283
  112.8 0.8 copy.22
  (2 shorter events, 0.1 us)
Async XLA Ops:
  0.7 8.8 %collective-permute-start = (bf16[16,128]{1,0:T(8,128)(2,1)S(1)}, bf16[16,128]{1,0:T(8,128)(2,1)S(1)}, u32[]{:S(2)}, u32[]{:S(2)}) collective-permute-start(bf16[16,128]{1,0:T(8,128)(2,1)S(1)} %get-tuple-element.6), channel_id=1, source_target_pairs={{0,16},{16,32},{32,48},{48,64},{64,80},{80,96},{96,112},{112,128},... | collective-permute-start | bytes 12296 | tf_op jit(solution)/shard_map/ppermute | solution.py:269
  3.7 5.8 %collective-permute-start.1 = (bf16[16,128]{1,0:T(8,128)(2,1)S(1)}, bf16[16,128]{1,0:T(8,128)(2,1)S(1)}, u32[]{:S(2)}, u32[]{:S(2)}) collective-permute-start(bf16[16,128]{1,0:T(8,128)(2,1)S(1)} %get-tuple-element.5), channel_id=1, source_target_pairs={{16,0},{32,16},{48,32},{64,48},{80,64},{96,80},{112,96},{128,112},... | collective-permute-start | bytes 12296 | tf_op jit(solution)/shard_map/ppermute | solution.py:270
  19.6 14.9 %all-to-all-start = ((bf16[16,16,1664]{2,1,0:T(8,128)(2,1)}), bf16[16,16,1664]{2,1,0:T(8,128)(2,1)S(1)}, u32[]{:S(2)}, u32[]{:S(2)}) async-start(bf16[16,16,1664]{2,1,0:T(8,128)(2,1)} %shard_map.55), calls=%async_computation | async-start | bytes 1703936 | tf_op jit(solution)/shard_map/all_to_all | solution.py:275

commit v7 on v6

--- a/solution.py
+++ b/solution.py
@@ -18,7 +18,9 @@
 SPACE = ("z", "core")
 
 
-def predict_kernel(cols_ref, state, left_ref, right_ref, ops_ref, out_ref, weights, staged, sems, out_sems, ens_sems):
+def predict_kernel(
+    cols_ref, state, left_ref, right_ref, scaled_ref, inverse_ref, ops_ref, out_ref, lost_ref, weights, raw, staged, sems, out_sems, ens_sems
+):
     parts = out_ref.shape[0]
     rows = state.shape[1] - 256
     members = state.shape[0]
@@ -35,58 +37,83 @@
         return pltpu.make_async_copy(staged.at[c], out_ref.at[c, :, pl.ds(0, width + 128)], out_sems.at[c])
 
     def pass_on(c):
-        chunk = state.at[:, pl.ds(128 + c * share, share)]
+        chunk = state.at[:, pl.ds(pl.multiple_of(128 + c * share, 128), share)]
         return pltpu.make_async_copy(chunk, out_ref.at[c, :, pl.ds(width + 128, share)], ens_sems.at[c])
 
     def pick(at):
         inner = state[:, pl.ds(pl.multiple_of(at * 128, 128), 128)]
         return jnp.where(at == 0, left_ref[...], jnp.where(at == rows // 128 + 1, right_ref[...], inner))
 
-    for c in range(parts):
-        pass_on(c).start()
-
-    def body(c, carry):
-        fetch(c).wait()
-
-        @pl.when(c + 4 < parts)
-        def _():
-            fetch(c + 4).start()
-
-        means = jnp.zeros((members, 128), F32)
+
+    def multiply(c):
+        values = []
         for o in range(group):
             block = c * group + o
             picked = [pick(cols_ref[block, k]) for k in range(8)]
             rows_of = [weights[block, k] for k in range(8)]
-            value = lax.dot_general(
-                jnp.concatenate(picked, axis=1), jnp.concatenate(rows_of, axis=1), NT, preferred_element_type=F32
+            values.append(
+                lax.dot_general(
+                    jnp.concatenate(picked, axis=1), jnp.concatenate(rows_of, axis=1), NT, preferred_element_type=F32
+                )
             )
+        raw[lax.rem(c, 2)] = jnp.concatenate(values, axis=1)
+
+    def split(c, values, lost):
+        means = jnp.zeros((members, 128), F32)
+        for o in range(group):
+            block = c * group + o
+            value = values[:, 128 * o : 128 * (o + 1)]
             mean = jnp.sum(value, axis=0, keepdims=True) / members
-            staged[c, :, 128 * o : 128 * (o + 1)] = (value - mean).astype(BF16)
+            rounded = (value - mean).astype(BF16)
+            staged[c, :, 128 * o : 128 * (o + 1)] = rounded
+            inverse = inverse_ref[pl.ds(block, 1), :]
+            departure = scaled_ref[pl.ds(block, 1), :] - mean * inverse
+            lost = lost + (value - mean - rounded.astype(F32)) * inverse * departure
             for part in range(3):
                 taken = mean.astype(BF16).astype(F32)
                 means = jnp.where(sub == group * part + o, taken, means)
                 mean = mean - taken
         staged[c, :, width:] = means.astype(BF16)
         deliver(c).start()
-        return carry
-
-    lax.fori_loop(0, parts, body, 0)
+        pass_on(c).start()
+        return lost
+
+    def body(c, lost):
+        fetch(c).wait()
+
+        @pl.when(c + 4 < parts)
+        def _():
+            fetch(c + 4).start()
+
+        values = raw[lax.rem(c - 1, 2)]
+        multiply(c)
+        return split(c - 1, values, lost)
+
+    fetch(0).wait()
+    fetch(4).start()
+    multiply(0)
+    lost = lax.fori_loop(1, parts, body, jnp.zeros((members, 128), F32))
+    lost_ref[...] = split(parts - 1, raw[(parts - 1) % 2], lost)
     for c in range(parts):
         pass_on(c).wait()
         deliver(c).wait()
 
 
-def predict(cols, state, left, right, ops, parts):
+def predict(cols, state, left, right, scaled, inverse, ops, parts):
     members, rows = state.shape[0], state.shape[1] - 256
     oblocks = ops.shape[0]
     outside, inside = pl.BlockSpec(memory_space=pltpu.HBM), pl.BlockSpec(memory_space=pltpu.VMEM)
     return pl.pallas_call(
         predict_kernel,
-        out_shape=jax.ShapeDtypeStruct((parts, members, (oblocks * 128 + rows) // parts + 128), BF16),
-        in_specs=[pl.BlockSpec(memory_space=pltpu.SMEM), inside, inside, inside, outside],
-        out_specs=outside,
+        out_shape=[
+            jax.ShapeDtypeStruct((parts, members, (oblocks * 128 + rows) // parts + 128), BF16),
+            jax.ShapeDtypeStruct((members, 128), F32),
+        ],
+        in_specs=[pl.BlockSpec(memory_space=pltpu.SMEM)] + [inside] * 5 + [outside],
+        out_specs=[outside, inside],
         scratch_shapes=[
             pltpu.VMEM(ops.shape, BF16),
+            pltpu.VMEM((2, members, oblocks * 128 // parts), F32),
             pltpu.VMEM((parts, members, oblocks * 128 // parts + 128), BF16),
             pltpu.SemaphoreType.DMA((parts,)),
             pltpu.SemaphoreType.DMA((parts,)),
@@ -94,10 +121,10 @@
         ],
         compiler_params=pltpu.CompilerParams(vmem_limit_bytes=50 * 2**20),
         cost_estimate=pl.CostEstimate(flops=2 * ops.size * members, bytes_accessed=2 * ops.size, transcendentals=0),
-    )(cols, state, left, right, ops)
-
-
-def gram_kernel(pred_ref, obs_ref, err_ref, out_ref):
+    )(cols, state, left, right, scaled, inverse, ops)
+
+
+def gram_kernel(mine_ref, lost_ref, pred_ref, obs_ref, err_ref, out_ref):
     total = pred_ref.shape[0] * pred_ref.shape[1]
     half = total // 2
     width = obs_ref.shape[1]
@@ -114,6 +141,11 @@
     top, low = white[:half], white[half:]
     dot = functools.partial(lax.dot_general, dimension_numbers=NT, precision=HIGHEST, preferred_element_type=F32)
     cross = dot(jnp.where(edge == 0, departure, 0.0), white)[:1]
+    members = lost_ref.shape[0]
+    member = lax.broadcasted_iota(jnp.int32, (members, total), 0) + mine_ref[0] * members
+    own = member == lax.broadcasted_iota(jnp.int32, (members, total), 1)
+    lost = jnp.sum(lost_ref[...], axis=1, keepdims=True)
+    cross = cross + jnp.sum(jnp.where(own, lost, 0.0), axis=0, keepdims=True)
     first, second = dot(top, top), dot(low, low)
     row = lax.broadcasted_iota(jnp.int32, (half, half), 0)
     col = lax.broadcasted_iota(jnp.int32, (half, half), 1)
@@ -128,13 +160,14 @@
         out_ref[i, :, 1024:] = extra[i] if i < len(extra) else jnp.zeros((1, 128), F32)
 
 
-def gram(shared, obs, err):
+def gram(mine, lost, shared, obs, err):
     total = shared.shape[0] * shared.shape[1]
     return pl.pallas_call(
         gram_kernel,
         out_shape=jax.ShapeDtypeStruct((total // 8, 1, 1152), F32),
+        in_specs=[pl.BlockSpec(memory_space=pltpu.SMEM)] + [pl.BlockSpec(memory_space=pltpu.VMEM)] * 4,
         compiler_params=pltpu.CompilerParams(vmem_limit_bytes=16 * 2**20),
-    )(shared, obs, err)
+    )(mine, lost, shared, obs, err)
 
 
 WIDE = 32
@@ -271,12 +304,14 @@
     state = jnp.pad(ens_t, ((0, 0), (128, 128)))
     state_local = rows // 128
     cols = jnp.mod(block_columns - space_index * state_local + 1, state_local * space_count)
-    shared = predict(cols, state, left, right, operator_blocks, member_count)
+    inverse = 1.0 / (error_scale * math.sqrt(total - 1))
+    scaled = (observed * inverse).reshape(-1, 128)
+    shared, lost = predict(cols, state, left, right, scaled, inverse.reshape(-1, 128), operator_blocks, member_count)
     shared = lax.all_to_all(shared, MEMBER, 0, 0, tiled=True)
     count = observed.shape[0] // member_count
     obs = lax.dynamic_slice_in_dim(observed, member_index * count, count)[None]
     err = lax.dynamic_slice_in_dim(error_scale, member_index * count, count)[None]
-    part = gram(shared, obs, err)
+    part = gram(member_index.astype(jnp.int32).reshape(1), lost, shared, obs, err)
     part = jnp.sum(lax.all_to_all(part, PLANE, 0, 0, tiled=True), axis=0)
     part = jnp.sum(to_all(part, "z", z_count), axis=0)
     gram_sum = to_all(part, PLANE, plane_count).reshape(plane_count, 1, -1)

time: 114 us -> 114 us (level)
  transfers between devices with their start and end apart: 3 -> 3, of which waited for: 1 -> 1; matrix products, arithmetic and copies ran while one was open for 3% -> 4% of each run, Pallas kernels for 0% -> 0%
where the time goes in v7:
time: 114 us
  blocking collectives  68.4 us (60%)
  Pallas kernels  19.4 us (17%)
  starting transfers between devices  10.5 us (9%)
  waiting for transfers between devices  9.31 us (8%)
  local copies, waits for them, and re-layouts  4.34 us (4%)
  other arithmetic  1.65 us (1%)
    all_to_all x2, blocking collectives, to_all(): lax.all_to_all(jnp.broadcast_to(x[None], (count,) + x.shape), axes, 0, 0,...  35.8 us
    all_to_all x1, blocking collectives, local(): part = jnp.sum(lax.all_to_all(part, PLANE, 0, 0, tiled=True), axis=0)  19 us
    all_to_all x1, blocking collectives, local(): lax.all_to_all(transform(gram_sum, shared, rows // member_count), MEMBER,...  13.7 us
    pallas_call x1, Pallas kernels, predict(): pl.pallas_call(predict_kernel, out_shape=[jax.ShapeDtypeStruct((parts, me...  9.62 us
    all_to_all x1, waiting for transfers between devices, local(): shared = lax.all_to_all(shared, MEMBER, 0, 0, tiled=True)  9.31 us
    pallas_call x1, Pallas kernels, transform(): pl.pallas_call(transform_kernel, out_shape=jax.ShapeDtypeStruct((sources,...  8.48 us
    ppermute x1, starting transfers between devices, local(): lax.ppermute(ens_t[:, :128], SPACE, [((i + 1) % space_count, i) for i in...  3.85 us
    all_to_all x1, starting transfers between devices, local(): shared = lax.all_to_all(shared, MEMBER, 0, 0, tiled=True)  3.64 us
  transfers between devices with their start and end apart: 3, of which 1 were waited for; matrix products, arithmetic and copies ran while one was open for 4% of the time, Pallas kernels for 0%

profile of v7, /device:TPU:1, one launch (start us, length us, event | category | flops | bytes accessed | tf_op | source)
XLA Modules:
  0.0 113.7 jit_solution(11737399374256541080)
XLA Ops:
  0.0 0.7 fusion.2
  0.7 3.0 %collective-permute-start = (bf16[16,128]{1,0:T(8,128)(2,1)S(1)}, bf16[16,128]{1,0:T(8,128)(2,1)S(1)}, u32[]{:S(2)}, u32[]{:S(2)}) collective-permute-start(bf16[16,128]{1,0:T(8,128)(2,1)S(1)} %get-tuple-element.10), channel_id=1, source_target_pairs={{0,16},{16,32},{32,48},{48,64},{64,80},{80,96},{96,112},{112,128},... | collective-permute-start | bytes 12296 | tf_op jit(solution)/shard_map/ppermute | solution.py:302
  3.7 3.9 %collective-permute-start.1 = (bf16[16,128]{1,0:T(8,128)(2,1)S(1)}, bf16[16,128]{1,0:T(8,128)(2,1)S(1)}, u32[]{:S(2)}, u32[]{:S(2)}) collective-permute-start(bf16[16,128]{1,0:T(8,128)(2,1)S(1)} %get-tuple-element.9), channel_id=1, source_target_pairs={{16,0},{32,16},{48,32},{64,48},{80,64},{96,80},{112,96},{128,112},... | collective-permute-start | bytes 12296 | tf_op jit(solution)/shard_map/ppermute | solution.py:303
  7.6 0.7 broadcast_subtract_fusion
  8.3 0.1 copy.18
  8.4 0.8 fusion.1
  9.2 1.1 pad.4.state
  10.3 0.0 collective-permute-done.left_ref
  10.3 0.0 collective-permute-done.1.right_ref
  10.3 9.6 %shard_map.55 = (bf16[16,16,1664]{2,1,0:T(8,128)(2,1)}, f32[16,128]{1,0:T(8,128)S(1)}) custom-call(s32[64,8]{1,0:T(8,128)S(1)} %add_select_fusion.cols_ref, bf16[16,16640]{1,0:T(8,128)(2,1)S(1)} %pad.4.state, bf16[16,128]{1,0:T(8,128)(2,1)S(1)} %collective-permute-done.left_ref, bf16[16,128]{1,0:T(8,128)(2,1)S(1)} %collective-permute-done.1.right_ref, ...), custom_call_target="tpu_custom_call" | custom-call | flops 268435456 | bytes 16777216 | tf_op jit(solution)/shard_map/pallas_call | solution.py:106
  19.9 3.6 %all-to-all-start = ((bf16[16,16,1664]{2,1,0:T(8,128)(2,1)}), bf16[16,16,1664]{2,1,0:T(8,128)(2,1)S(1)}, u32[]{:S(2)}, u32[]{:S(2)}) async-start(bf16[16,16,1664]{2,1,0:T(8,128)(2,1)} %get-tuple-element.8), calls=%async_computation | async-start | bytes 1703936 | tf_op jit(solution)/shard_map/all_to_all | solution.py:310
  23.6 0.8 dynamic_slice.6
  24.3 0.8 dynamic_slice.7
  25.1 9.3 %all-to-all-done.pred_ref.ens_ref = bf16[16,16,1664]{2,1,0:T(8,128)(2,1)S(1)} async-done(((bf16[16,16,1664]{2,1,0:T(8,128)(2,1)}), bf16[16,16,1664]{2,1,0:T(8,128)(2,1)S(1)}, u32[]{:S(2)}, u32[]{:S(2)}) %all-to-all-start) | async-done | bytes 852000 | tf_op jit(solution)/shard_map/all_to_all | solution.py:310
  34.4 1.3 %shard_map.56 = f32[32,1,1152]{2,1,0:T(1,128)S(1)} custom-call(s32[1]{0:T(128)} %bitcast.mine_ref, f32[16,128]{1,0:T(8,128)S(1)} %get-tuple-element.7.lost_ref, bf16[16,16,1664]{2,1,0:T(8,128)(2,1)S(1)} %all-to-all-done.pred_ref.ens_ref, f32[1,512]{1,0:T(1,128)S(1)} %bitcast.13, f32[1,512]{1,0:T(1,128)S(1)} %bitcast.14), custom_call_target="tpu_custom_call" | custom-call | tf_op jit(solution)/shard_map/pallas_call | solution.py:165
  35.7 19.0 %all_to_all.25 = f32[32,1,1152]{2,1,0:T(1,128)S(1)} all-to-all(f32[32,1,1152]{2,1,0:T(1,128)S(1)} %shard_map.56), channel_id=1, replica_groups=mesh['z'=16,'core'=2,'y'=4,'x'=4] {'core','y','x'}, dimensions={0} | all-to-all | bytes 294912 | tf_op jit(solution)/shard_map/all_to_all | solution.py:315
  54.7 0.1 reduce_sum.18
  54.8 22.7 %all_to_all.26 = f32[16,1,1152]{2,1,0:T(1,128)S(1)} all-to-all(f32[16,1,1152]{2,1,0:T(1,128)S(1)} %broadcast_in_dim.20), channel_id=1, replica_groups=mesh['z'=16,'core'=2,'y'=4,'x'=4] {'z'}, dimensions={0} | all-to-all | bytes 147456 | tf_op jit(solution)/shard_map/all_to_all | solution.py:289
  77.6 0.1 reduce_sum.19
  77.6 0.1 broadcast_in_dim.21
  77.7 13.0 %all_to_all.27.gram_ref = f32[32,1,1152]{2,1,0:T(1,128)S(1)} all-to-all(f32[32,1,1152]{2,1,0:T(1,128)S(1)} %broadcast_in_dim.21), channel_id=1, replica_groups=mesh['z'=16,'core'=2,'y'=4,'x'=4] {'core','y','x'}, dimensions={0} | all-to-all | bytes 294912 | tf_op jit(solution)/shard_map/all_to_all | solution.py:289
  90.7 8.5 %shard_map.57 = bf16[16,16,1024]{2,1,0:T(8,128)(2,1)S(1)} custom-call(f32[32,1,1152]{2,1,0:T(1,128)S(1)} %all_to_all.27.gram_ref, bf16[16,16,1664]{2,1,0:T(8,128)(2,1)S(1)} %all-to-all-done.pred_ref.ens_ref), custom_call_target="tpu_custom_call" | custom-call | tf_op jit(solution)/shard_map/pallas_call | solution.py:280
  99.2 13.7 %all_to_all.28 = bf16[16,16,1024]{2,1,0:T(8,128)(2,1)S(1)} all-to-all(bf16[16,16,1024]{2,1,0:T(8,128)(2,1)S(1)} %shard_map.57), channel_id=1, replica_groups=mesh['z'=16,'core'=2,'y'=4,'x'=4] {'y','x'}, dimensions={0} | all-to-all | bytes 1048576 | tf_op jit(solution)/shard_map/all_to_all | solution.py:318
  112.9 0.8 copy.22
  (2 shorter events, 0.1 us)
Async XLA Ops:
  0.7 9.6 %collective-permute-start = (bf16[16,128]{1,0:T(8,128)(2,1)S(1)}, bf16[16,128]{1,0:T(8,128)(2,1)S(1)}, u32[]{:S(2)}, u32[]{:S(2)}) collective-permute-start(bf16[16,128]{1,0:T(8,128)(2,1)S(1)} %get-tuple-element.10), channel_id=1, source_target_pairs={{0,16},{16,32},{32,48},{48,64},{64,80},{80,96},{96,112},{112,128},... | collective-permute-start | bytes 12296 | tf_op jit(solution)/shard_map/ppermute | solution.py:302
  3.7 6.5 %collective-permute-start.1 = (bf16[16,128]{1,0:T(8,128)(2,1)S(1)}, bf16[16,128]{1,0:T(8,128)(2,1)S(1)}, u32[]{:S(2)}, u32[]{:S(2)}) collective-permute-start(bf16[16,128]{1,0:T(8,128)(2,1)S(1)} %get-tuple-element.9), channel_id=1, source_target_pairs={{16,0},{32,16},{48,32},{64,48},{80,64},{96,80},{112,96},{128,112},... | collective-permute-start | bytes 12296 | tf_op jit(solution)/shard_map/ppermute | solution.py:303
  19.9 14.5 %all-to-all-start = ((bf16[16,16,1664]{2,1,0:T(8,128)(2,1)}), bf16[16,16,1664]{2,1,0:T(8,128)(2,1)S(1)}, u32[]{:S(2)}, u32[]{:S(2)}) async-start(bf16[16,16,1664]{2,1,0:T(8,128)(2,1)} %get-tuple-element.8), calls=%async_computation | async-start | bytes 1703936 | tf_op jit(solution)/shard_map/all_to_all | solution.py:310

commit v8 on v7

--- a/solution.py
+++ b/solution.py
@@ -16,6 +16,12 @@
 PLANE = ("core", "y", "x")
 MEMBER = ("y", "x")
 SPACE = ("z", "core")
+EXCHANGE = ("x", "y")
+
+
+def turned(count):
+    side = math.isqrt(count)
+    return [i % side * side + i // side for i in range(count)]
 
 
 def predict_kernel(
@@ -128,11 +134,12 @@
     total = pred_ref.shape[0] * pred_ref.shape[1]
     half = total // 2
     width = obs_ref.shape[1]
-    parts = pred_ref[:, :, width : width + 128].astype(F32)
+    given = jnp.concatenate([pred_ref[s : s + 1, :, : width + 128] for s in turned(pred_ref.shape[0])], axis=0).astype(F32)
+    parts = given[:, :, width:]
     group = width // 128
     means = parts[:, :group] + parts[:, group : 2 * group] + parts[:, 2 * group : 3 * group]
     means = jnp.concatenate([means[:, o : o + 1] for o in range(group)], axis=2)
-    pred = (pred_ref[:, :, :width].astype(F32) + means).reshape(total, width)
+    pred = (given[:, :, :width] + means).reshape(total, width)
     mean = jnp.sum(pred, axis=0, keepdims=True) / total
     scale = err_ref[...] * math.sqrt(total - 1)
     white = (pred - mean) / scale
@@ -233,7 +240,9 @@
 def transform_kernel(gram_ref, ens_ref, out_ref, packed):
     total = 8 * gram_ref.shape[0]
     half = total // 2
-    states = ens_ref[:, :, ens_ref.shape[2] - out_ref.shape[2] :].astype(F32).reshape(total, -1)
+    places = turned(out_ref.shape[0])
+    first_row = ens_ref.shape[2] - out_ref.shape[2]
+    states = jnp.concatenate([ens_ref[s, :, first_row:] for s in places], axis=0).astype(F32)
     mean_state = jnp.sum(states, axis=0, keepdims=True) / total
     anomalies = (states - mean_state).astype(BF16)
     row = lax.broadcasted_iota(jnp.int32, (total, total), 0)
@@ -263,16 +272,19 @@
         blocks[s] = jnp.where(here <= row[r0:r1], done, 0.0)
         if r1 < total:
             kept = jnp.where((here < r1) & (here > row[r0:r1]), 0.0, done)
-            turned = done.T
+            flipped = done.T
             inside = (here >= r0) & (here < r1)
             for t in range(s + 1, count):
-                change = jnp.dot(turned[WIDE * t : WIDE * (t + 1), :], kept, precision=HIGHEST, preferred_element_type=F32)
+                change = jnp.dot(flipped[WIDE * t : WIDE * (t + 1), :], kept, precision=HIGHEST, preferred_element_type=F32)
                 blocks[t] = jnp.where(inside, 0.0, blocks[t]) - change
         solved = jnp.sum(blocks[s] * cross, axis=1, keepdims=True)
         weight = weight + jnp.sum(blocks[s] * solved, axis=0, keepdims=True)
-    turned = (jnp.concatenate(blocks, axis=0) + weight).astype(BF16)
-    change = jnp.dot(turned, anomalies, preferred_element_type=F32)
-    out_ref[...] = (mean_state + change).astype(BF16).reshape(out_ref.shape)
+    transposed = (jnp.concatenate(blocks, axis=0) + weight).astype(BF16)
+    change = jnp.dot(transposed, anomalies, preferred_element_type=F32)
+    result = (mean_state + change).astype(BF16)
+    members = out_ref.shape[1]
+    for i, s in enumerate(places):
+        out_ref[s] = result[members * i : members * (i + 1)]
 
 
 def transform(gram_sum, shared, width):
@@ -307,15 +319,16 @@
     inverse = 1.0 / (error_scale * math.sqrt(total - 1))
     scaled = (observed * inverse).reshape(-1, 128)
     shared, lost = predict(cols, state, left, right, scaled, inverse.reshape(-1, 128), operator_blocks, member_count)
-    shared = lax.all_to_all(shared, MEMBER, 0, 0, tiled=True)
+    shared = lax.all_to_all(shared, EXCHANGE, 0, 0, tiled=True)
+    place = lax.axis_index(EXCHANGE)
     count = observed.shape[0] // member_count
-    obs = lax.dynamic_slice_in_dim(observed, member_index * count, count)[None]
-    err = lax.dynamic_slice_in_dim(error_scale, member_index * count, count)[None]
+    obs = lax.dynamic_slice_in_dim(observed, place * count, count)[None]
+    err = lax.dynamic_slice_in_dim(error_scale, place * count, count)[None]
     part = gram(member_index.astype(jnp.int32).reshape(1), lost, shared, obs, err)
     part = jnp.sum(lax.all_to_all(part, PLANE, 0, 0, tiled=True), axis=0)
     part = jnp.sum(to_all(part, "z", z_count), axis=0)
     gram_sum = to_all(part, PLANE, plane_count).reshape(plane_count, 1, -1)
-    analysis = lax.all_to_all(transform(gram_sum, shared, rows // member_count), MEMBER, 0, 0, tiled=True)
+    analysis = lax.all_to_all(transform(gram_sum, shared, rows // member_count), EXCHANGE, 0, 0, tiled=True)
     return analysis.transpose(1, 0, 2).reshape(members, rows).T
 
 

time: 114 us -> 114 us (level)
  no operation moved by 1% of the time
where the time goes in v8:
time: 114 us; the launch traced here: 113 us
  blocking collectives  68.1 us (60%)
  Pallas kernels  19.4 us (17%)
  starting transfers between devices  10.5 us (9%)
  waiting for transfers between devices  9.14 us (8%)
  local copies, waits for them, and re-layouts  4.34 us (4%)
  other arithmetic  1.65 us (1%)
    all_to_all x2, blocking collectives, to_all(): lax.all_to_all(jnp.broadcast_to(x[None], (count,) + x.shape), axes, 0, 0,...  35.6 us
    all_to_all x1, blocking collectives, local(): part = jnp.sum(lax.all_to_all(part, PLANE, 0, 0, tiled=True), axis=0)  19.2 us
    all_to_all x1, blocking collectives, local(): lax.all_to_all(transform(gram_sum, shared, rows // member_count), EXCHANG...  13.3 us
    pallas_call x1, Pallas kernels, predict(): pl.pallas_call(predict_kernel, out_shape=[jax.ShapeDtypeStruct((parts, me...  9.62 us
    all_to_all x1, waiting for transfers between devices, local(): shared = lax.all_to_all(shared, EXCHANGE, 0, 0, tiled=True)  9.13 us
    pallas_call x1, Pallas kernels, transform(): pl.pallas_call(transform_kernel, out_shape=jax.ShapeDtypeStruct((sources,...  8.5 us
    ppermute x1, starting transfers between devices, local(): lax.ppermute(ens_t[:, :128], SPACE, [((i + 1) % space_count, i) for i in...  3.85 us
    all_to_all x1, starting transfers between devices, local(): shared = lax.all_to_all(shared, EXCHANGE, 0, 0, tiled=True)  3.64 us
  transfers between devices with their start and end apart: 3, of which 1 were waited for; matrix products, arithmetic and copies ran while one was open for 4% of the time, Pallas kernels for 0%

profile of v8, /device:TPU:1, one launch (start us, length us, event | category | flops | bytes accessed | tf_op | source)
XLA Modules:
  0.0 113.3 jit_solution(3116188880151189218)
XLA Ops:
  0.0 0.7 fusion.2
  0.7 3.0 %collective-permute-start = (bf16[16,128]{1,0:T(8,128)(2,1)S(1)}, bf16[16,128]{1,0:T(8,128)(2,1)S(1)}, u32[]{:S(2)}, u32[]{:S(2)}) collective-permute-start(bf16[16,128]{1,0:T(8,128)(2,1)S(1)} %get-tuple-element.10), channel_id=1, source_target_pairs={{0,16},{16,32},{32,48},{48,64},{64,80},{80,96},{96,112},{112,128},... | collective-permute-start | bytes 12296 | tf_op jit(solution)/shard_map/ppermute | solution.py:314
  3.7 3.9 %collective-permute-start.1 = (bf16[16,128]{1,0:T(8,128)(2,1)S(1)}, bf16[16,128]{1,0:T(8,128)(2,1)S(1)}, u32[]{:S(2)}, u32[]{:S(2)}) collective-permute-start(bf16[16,128]{1,0:T(8,128)(2,1)S(1)} %get-tuple-element.9), channel_id=1, source_target_pairs={{16,0},{32,16},{48,32},{64,48},{80,64},{96,80},{112,96},{128,112},... | collective-permute-start | bytes 12296 | tf_op jit(solution)/shard_map/ppermute | solution.py:315
  7.6 0.7 broadcast_subtract_fusion
  8.3 0.1 copy.18
  8.4 0.8 fusion.1
  9.2 1.1 pad.4.state
  10.3 0.0 collective-permute-done.left_ref
  10.3 0.0 collective-permute-done.1.right_ref
  10.3 9.6 %shard_map.55 = (bf16[16,16,1664]{2,1,0:T(8,128)(2,1)}, f32[16,128]{1,0:T(8,128)S(1)}) custom-call(s32[64,8]{1,0:T(8,128)S(1)} %add_select_fusion.cols_ref, bf16[16,16640]{1,0:T(8,128)(2,1)S(1)} %pad.4.state, bf16[16,128]{1,0:T(8,128)(2,1)S(1)} %collective-permute-done.left_ref, bf16[16,128]{1,0:T(8,128)(2,1)S(1)} %collective-permute-done.1.right_ref, ...), custom_call_target="tpu_custom_call" | custom-call | flops 268435456 | bytes 16777216 | tf_op jit(solution)/shard_map/pallas_call | solution.py:112
  19.9 3.6 %all-to-all-start = ((bf16[16,16,1664]{2,1,0:T(8,128)(2,1)}), bf16[16,16,1664]{2,1,0:T(8,128)(2,1)S(1)}, u32[]{:S(2)}, u32[]{:S(2)}) async-start(bf16[16,16,1664]{2,1,0:T(8,128)(2,1)} %get-tuple-element.8), calls=%async_computation | async-start | bytes 1703936 | tf_op jit(solution)/shard_map/all_to_all | solution.py:322
  23.6 0.8 dynamic_slice.6
  24.3 0.8 dynamic_slice.7
  25.1 9.1 %all-to-all-done.pred_ref.ens_ref = bf16[16,16,1664]{2,1,0:T(8,128)(2,1)S(1)} async-done(((bf16[16,16,1664]{2,1,0:T(8,128)(2,1)}), bf16[16,16,1664]{2,1,0:T(8,128)(2,1)S(1)}, u32[]{:S(2)}, u32[]{:S(2)}) %all-to-all-start) | async-done | bytes 852000 | tf_op jit(solution)/shard_map/all_to_all | solution.py:322
  34.2 1.3 %shard_map.56 = f32[32,1,1152]{2,1,0:T(1,128)S(1)} custom-call(s32[1]{0:T(128)} %bitcast.mine_ref, f32[16,128]{1,0:T(8,128)S(1)} %get-tuple-element.7.lost_ref, bf16[16,16,1664]{2,1,0:T(8,128)(2,1)S(1)} %all-to-all-done.pred_ref.ens_ref, f32[1,512]{1,0:T(1,128)S(1)} %bitcast.13, f32[1,512]{1,0:T(1,128)S(1)} %bitcast.14), custom_call_target="tpu_custom_call" | custom-call | tf_op jit(solution)/shard_map/pallas_call | solution.py:172
  35.5 19.2 %all_to_all.25 = f32[32,1,1152]{2,1,0:T(1,128)S(1)} all-to-all(f32[32,1,1152]{2,1,0:T(1,128)S(1)} %shard_map.56), channel_id=1, replica_groups=mesh['z'=16,'core'=2,'y'=4,'x'=4] {'core','y','x'}, dimensions={0} | all-to-all | bytes 294912 | tf_op jit(solution)/shard_map/all_to_all | solution.py:328
  54.8 0.1 reduce_sum.18
  54.9 22.6 %all_to_all.26 = f32[16,1,1152]{2,1,0:T(1,128)S(1)} all-to-all(f32[16,1,1152]{2,1,0:T(1,128)S(1)} %broadcast_in_dim.20), channel_id=1, replica_groups=mesh['z'=16,'core'=2,'y'=4,'x'=4] {'z'}, dimensions={0} | all-to-all | bytes 147456 | tf_op jit(solution)/shard_map/all_to_all | solution.py:301
  77.5 0.1 reduce_sum.19
  77.6 0.1 broadcast_in_dim.21
  77.6 13.0 %all_to_all.27.gram_ref = f32[32,1,1152]{2,1,0:T(1,128)S(1)} all-to-all(f32[32,1,1152]{2,1,0:T(1,128)S(1)} %broadcast_in_dim.21), channel_id=1, replica_groups=mesh['z'=16,'core'=2,'y'=4,'x'=4] {'core','y','x'}, dimensions={0} | all-to-all | bytes 294912 | tf_op jit(solution)/shard_map/all_to_all | solution.py:301
  90.7 8.5 %shard_map.57 = bf16[16,16,1024]{2,1,0:T(8,128)(2,1)S(1)} custom-call(f32[32,1,1152]{2,1,0:T(1,128)S(1)} %all_to_all.27.gram_ref, bf16[16,16,1664]{2,1,0:T(8,128)(2,1)S(1)} %all-to-all-done.pred_ref.ens_ref), custom_call_target="tpu_custom_call" | custom-call | tf_op jit(solution)/shard_map/pallas_call | solution.py:292
  99.2 13.3 %all_to_all.28 = bf16[16,16,1024]{2,1,0:T(8,128)(2,1)S(1)} all-to-all(bf16[16,16,1024]{2,1,0:T(8,128)(2,1)S(1)} %shard_map.57), channel_id=1, replica_groups=mesh['z'=16,'core'=2,'y'=4,'x'=4] {'x','y'}, dimensions={0} | all-to-all | bytes 1048576 | tf_op jit(solution)/shard_map/all_to_all | solution.py:331
  112.5 0.8 copy.22
  (2 shorter events, 0.1 us)
Async XLA Ops:
  0.7 9.6 %collective-permute-start = (bf16[16,128]{1,0:T(8,128)(2,1)S(1)}, bf16[16,128]{1,0:T(8,128)(2,1)S(1)}, u32[]{:S(2)}, u32[]{:S(2)}) collective-permute-start(bf16[16,128]{1,0:T(8,128)(2,1)S(1)} %get-tuple-element.10), channel_id=1, source_target_pairs={{0,16},{16,32},{32,48},{48,64},{64,80},{80,96},{96,112},{112,128},... | collective-permute-start | bytes 12296 | tf_op jit(solution)/shard_map/ppermute | solution.py:314
  3.7 6.5 %collective-permute-start.1 = (bf16[16,128]{1,0:T(8,128)(2,1)S(1)}, bf16[16,128]{1,0:T(8,128)(2,1)S(1)}, u32[]{:S(2)}, u32[]{:S(2)}) collective-permute-start(bf16[16,128]{1,0:T(8,128)(2,1)S(1)} %get-tuple-element.9), channel_id=1, source_target_pairs={{16,0},{32,16},{48,32},{64,48},{80,64},{96,80},{112,96},{128,112},... | collective-permute-start | bytes 12296 | tf_op jit(solution)/shard_map/ppermute | solution.py:315
  19.9 14.3 %all-to-all-start = ((bf16[16,16,1664]{2,1,0:T(8,128)(2,1)}), bf16[16,16,1664]{2,1,0:T(8,128)(2,1)S(1)}, u32[]{:S(2)}, u32[]{:S(2)}) async-start(bf16[16,16,1664]{2,1,0:T(8,128)(2,1)} %get-tuple-element.8), calls=%async_computation | async-start | bytes 1703936 | tf_op jit(solution)/shard_map/all_to_all | solution.py:322

commit v9 on v8

--- a/solution.py
+++ b/solution.py
@@ -25,7 +25,8 @@
 
 
 def predict_kernel(
-    cols_ref, state, left_ref, right_ref, scaled_ref, inverse_ref, ops_ref, out_ref, lost_ref, weights, raw, staged, sems, out_sems, ens_sems
+    place_ref, cols_ref, state, left_ref, right_ref, scaled_ref, inverse_ref, ops_ref, out_ref, side_ref,
+    weights, raw, staged, sems, out_sems, ens_sems,
 ):
     parts = out_ref.shape[0]
     rows = state.shape[1] - 256
@@ -99,13 +100,23 @@
     fetch(4).start()
     multiply(0)
     lost = lax.fori_loop(1, parts, body, jnp.zeros((members, 128), F32))
-    lost_ref[...] = split(parts - 1, raw[(parts - 1) % 2], lost)
+    lost = jnp.sum(split(parts - 1, raw[(parts - 1) % 2], lost), axis=1, keepdims=True)
+    place, edge = place_ref[0], math.isqrt(parts)
+    mine = lax.rem(place, edge) * edge + lax.div(place, edge)
+    member = lax.broadcasted_iota(jnp.int32, (members, width), 0) + mine * members
+    own = member == lax.broadcasted_iota(jnp.int32, (members, width), 1)
+    side_ref[...] = jnp.zeros(side_ref.shape, F32)
+    side_ref[2:3, :] = jnp.sum(jnp.where(own, lost, 0.0), axis=0, keepdims=True)
+    for o in range(group):
+        at = slice(128 * o, 128 * (o + 1))
+        side_ref[0:1, at] = scaled_ref[pl.ds(place * group + o, 1), :]
+        side_ref[1:2, at] = inverse_ref[pl.ds(place * group + o, 1), :]
     for c in range(parts):
         pass_on(c).wait()
         deliver(c).wait()
 
 
-def predict(cols, state, left, right, scaled, inverse, ops, parts):
+def predict(place, cols, state, left, right, scaled, inverse, ops, parts):
     members, rows = state.shape[0], state.shape[1] - 256
     oblocks = ops.shape[0]
     outside, inside = pl.BlockSpec(memory_space=pltpu.HBM), pl.BlockSpec(memory_space=pltpu.VMEM)
@@ -113,9 +124,9 @@
         predict_kernel,
         out_shape=[
             jax.ShapeDtypeStruct((parts, members, (oblocks * 128 + rows) // parts + 128), BF16),
-            jax.ShapeDtypeStruct((members, 128), F32),
+            jax.ShapeDtypeStruct((8, oblocks * 128 // parts), F32),
         ],
-        in_specs=[pl.BlockSpec(memory_space=pltpu.SMEM)] + [inside] * 5 + [outside],
+        in_specs=[pl.BlockSpec(memory_space=pltpu.SMEM)] * 2 + [inside] * 5 + [outside],
         out_specs=[outside, inside],
         scratch_shapes=[
             pltpu.VMEM(ops.shape, BF16),
@@ -127,32 +138,28 @@
         ],
         compiler_params=pltpu.CompilerParams(vmem_limit_bytes=50 * 2**20),
         cost_estimate=pl.CostEstimate(flops=2 * ops.size * members, bytes_accessed=2 * ops.size, transcendentals=0),
-    )(cols, state, left, right, scaled, inverse, ops)
-
-
-def gram_kernel(mine_ref, lost_ref, pred_ref, obs_ref, err_ref, out_ref):
+    )(place, cols, state, left, right, scaled, inverse, ops)
+
+
+def gram_kernel(side_ref, pred_ref, out_ref):
     total = pred_ref.shape[0] * pred_ref.shape[1]
     half = total // 2
-    width = obs_ref.shape[1]
+    width = side_ref.shape[1]
+    group = width // 128
     given = jnp.concatenate([pred_ref[s : s + 1, :, : width + 128] for s in turned(pred_ref.shape[0])], axis=0).astype(F32)
     parts = given[:, :, width:]
-    group = width // 128
     means = parts[:, :group] + parts[:, group : 2 * group] + parts[:, 2 * group : 3 * group]
     means = jnp.concatenate([means[:, o : o + 1] for o in range(group)], axis=2)
     pred = (given[:, :, :width] + means).reshape(total, width)
     mean = jnp.sum(pred, axis=0, keepdims=True) / total
-    scale = err_ref[...] * math.sqrt(total - 1)
-    white = (pred - mean) / scale
-    departure = (obs_ref[...] - mean) / scale
+    scaled, inverse = side_ref[0:1, :], side_ref[1:2, :]
+    white = (pred - mean) * inverse
+    departure = scaled - mean * inverse
     edge = lax.broadcasted_iota(jnp.int32, (8, width), 0)
     top, low = white[:half], white[half:]
     dot = functools.partial(lax.dot_general, dimension_numbers=NT, precision=HIGHEST, preferred_element_type=F32)
     cross = dot(jnp.where(edge == 0, departure, 0.0), white)[:1]
-    members = lost_ref.shape[0]
-    member = lax.broadcasted_iota(jnp.int32, (members, total), 0) + mine_ref[0] * members
-    own = member == lax.broadcasted_iota(jnp.int32, (members, total), 1)
-    lost = jnp.sum(lost_ref[...], axis=1, keepdims=True)
-    cross = cross + jnp.sum(jnp.where(own, lost, 0.0), axis=0, keepdims=True)
+    cross = cross + side_ref[2:3, :total]
     first, second = dot(top, top), dot(low, low)
     row = lax.broadcasted_iota(jnp.int32, (half, half), 0)
     col = lax.broadcasted_iota(jnp.int32, (half, half), 1)
@@ -167,14 +174,13 @@
         out_ref[i, :, 1024:] = extra[i] if i < len(extra) else jnp.zeros((1, 128), F32)
 
 
-def gram(mine, lost, shared, obs, err):
+def gram(side, shared):
     total = shared.shape[0] * shared.shape[1]
     return pl.pallas_call(
         gram_kernel,
         out_shape=jax.ShapeDtypeStruct((total // 8, 1, 1152), F32),
-        in_specs=[pl.BlockSpec(memory_space=pltpu.SMEM)] + [pl.BlockSpec(memory_space=pltpu.VMEM)] * 4,
         compiler_params=pltpu.CompilerParams(vmem_limit_bytes=16 * 2**20),
-    )(mine, lost, shared, obs, err)
+    )(side, shared)
 
 
 WIDE = 32
@@ -310,21 +316,17 @@
     z_count = lax.axis_size("z")
     total = members * member_count
     space_index = lax.axis_index(SPACE)
-    member_index = lax.axis_index(MEMBER)
     left = lax.ppermute(ens_t[:, -128:], SPACE, [(i, (i + 1) % space_count) for i in range(space_count)])
     right = lax.ppermute(ens_t[:, :128], SPACE, [((i + 1) % space_count, i) for i in range(space_count)])
     state = jnp.pad(ens_t, ((0, 0), (128, 128)))
     state_local = rows // 128
     cols = jnp.mod(block_columns - space_index * state_local + 1, state_local * space_count)
     inverse = 1.0 / (error_scale * math.sqrt(total - 1))
-    scaled = (observed * inverse).reshape(-1, 128)
-    shared, lost = predict(cols, state, left, right, scaled, inverse.reshape(-1, 128), operator_blocks, member_count)
+    scaled, inverse = (observed * inverse).reshape(-1, 128), inverse.reshape(-1, 128)
+    place = lax.axis_index(EXCHANGE).astype(jnp.int32).reshape(1)
+    shared, side = predict(place, cols, state, left, right, scaled, inverse, operator_blocks, member_count)
     shared = lax.all_to_all(shared, EXCHANGE, 0, 0, tiled=True)
-    place = lax.axis_index(EXCHANGE)
-    count = observed.shape[0] // member_count
-    obs = lax.dynamic_slice_in_dim(observed, place * count, count)[None]
-    err = lax.dynamic_slice_in_dim(error_scale, place * count, count)[None]
-    part = gram(member_index.astype(jnp.int32).reshape(1), lost, shared, obs, err)
+    part = gram(side, shared)
     part = jnp.sum(lax.all_to_all(part, PLANE, 0, 0, tiled=True), axis=0)
     part = jnp.sum(to_all(part, "z", z_count), axis=0)
     gram_sum = to_all(part, PLANE, plane_count).reshape(plane_count, 1, -1)

time: 114 us -> 113 us (level)
  blocking collectives: 68.1 us -> 80.4 us
  waiting for transfers between devices: 9.14 us -> 1.52 us
  starting transfers between devices: 10.5 us -> 6.88 us
  local copies, waits for them, and re-layouts: 4.34 us -> 2.82 us
    all_to_all x0 -> x1, blocking collectives: none -> 17.1 us  [local(): shared = lax.all_to_all(shared, EXCHANGE, 0, 0, tiled=True)]
    all_to_all x1 -> x0, waiting for transfers between devices: 9.13 us -> none  [local(): shared = lax.all_to_all(shared, EXCHANGE, 0, 0, tiled=True)]
    all_to_all x1 -> x0, starting transfers between devices: 3.64 us -> none  [local(): shared = lax.all_to_all(shared, EXCHANGE, 0, 0, tiled=True)]
    ppermute x1, starting transfers between devices: 3.85 us -> 6.88 us  [local(): lax.ppermute(ens_t[:, :128], SPACE, [((i + 1) % space_count, i) for i in...]
    ppermute x1, starting transfers between devices: 3.03 us -> 0.01 us  [local(): lax.ppermute(ens_t[:, -128:], SPACE, [(i, (i + 1) % space_count) for i in...]
    all_to_all x1, blocking collectives: 19.2 us -> 16.4 us  [local(): part = jnp.sum(lax.all_to_all(part, PLANE, 0, 0, tiled=True), axis=0)]
    all_to_all x2, blocking collectives: 35.6 us -> 33.6 us  [to_all(): lax.all_to_all(jnp.broadcast_to(x[None], (count,) + x.shape), axes, 0, 0,...]
    dynamic_slice x2 -> x0, local copies, waits for them, and re-layouts: 1.52 us -> none  [the longest x1 0.76 us: local(): obs = lax.dynamic_slice_in_dim(observed, place * count, count)[None]]
  transfers between devices with their start and end apart: 3 -> 2, of which waited for: 1 -> 1; matrix products, arithmetic and copies ran while one was open for 4% -> 2% of each run, Pallas kernels for 0% -> 0%
where the time goes in v9:
time: 113 us
  blocking collectives  80.4 us (71%)
  Pallas kernels  19.2 us (17%)
  starting transfers between devices  6.88 us (6%)
  local copies, waits for them, and re-layouts  2.82 us (2%)
  other arithmetic  1.65 us (1%)
  waiting for transfers between devices  1.52 us (1%)
    all_to_all x2, blocking collectives, to_all(): lax.all_to_all(jnp.broadcast_to(x[None], (count,) + x.shape), axes, 0, 0,...  33.6 us
    all_to_all x1, blocking collectives, local(): shared = lax.all_to_all(shared, EXCHANGE, 0, 0, tiled=True)  17.1 us
    all_to_all x1, blocking collectives, local(): part = jnp.sum(lax.all_to_all(part, PLANE, 0, 0, tiled=True), axis=0)  16.4 us
    all_to_all x1, blocking collectives, local(): lax.all_to_all(transform(gram_sum, shared, rows // member_count), EXCHANG...  13.3 us
    pallas_call x1, Pallas kernels, predict(): pl.pallas_call(predict_kernel, out_shape=[jax.ShapeDtypeStruct((parts, me...  9.4 us
    pallas_call x1, Pallas kernels, transform(): pl.pallas_call(transform_kernel, out_shape=jax.ShapeDtypeStruct((sources,...  8.5 us
    ppermute x1, starting transfers between devices, local(): lax.ppermute(ens_t[:, :128], SPACE, [((i + 1) % space_count, i) for i in...  6.88 us
  transfers between devices with their start and end apart: 2, of which 1 were waited for; matrix products, arithmetic and copies ran while one was open for 2% of the time, Pallas kernels for 0%

profile of v9, /device:TPU:1, one launch (start us, length us, event | category | flops | bytes accessed | tf_op | source)
XLA Modules:
  0.0 112.6 jit_solution(3498748579394090756)
XLA Ops:
  0.0 0.7 fusion.2
  0.7 6.9 %collective-permute-start.1 = (bf16[16,128]{1,0:T(8,128)(2,1)S(1)}, bf16[16,128]{1,0:T(8,128)(2,1)S(1)}, u32[]{:S(2)}, u32[]{:S(2)}) collective-permute-start(bf16[16,128]{1,0:T(8,128)(2,1)S(1)} %get-tuple-element.9), channel_id=1, source_target_pairs={{16,0},{32,16},{48,32},{64,48},{80,64},{96,80},{112,96},{128,112},... | collective-permute-start | bytes 12296 | tf_op jit(solution)/shard_map/ppermute | solution.py:320
  7.6 0.0 collective-permute-start
  7.6 0.7 broadcast_subtract_fusion
  8.3 0.1 copy.18
  8.4 0.8 fusion.1
  9.2 1.1 pad.4.state
  10.3 0.0 collective-permute-done.1.right_ref
  10.3 1.5 %collective-permute-done.left_ref = bf16[16,128]{1,0:T(8,128)(2,1)S(1)} collective-permute-done((bf16[16,128]{1,0:T(8,128)(2,1)S(1)}, bf16[16,128]{1,0:T(8,128)(2,1)S(1)}, u32[]{:S(2)}, u32[]{:S(2)}) %collective-permute-start) | collective-permute-done | bytes 4128 | tf_op jit(solution)/shard_map/ppermute | solution.py:319
  11.8 9.4 %shard_map.55 = (bf16[16,16,1664]{2,1,0:T(8,128)(2,1)S(1)}, f32[8,512]{1,0:T(8,128)S(1)}) custom-call(s32[1]{0:T(128)} %bitcast.place_ref, s32[64,8]{1,0:T(8,128)S(1)} %add_select_fusion.cols_ref, bf16[16,16640]{1,0:T(8,128)(2,1)S(1)} %pad.4.state, bf16[16,128]{1,0:T(8,128)(2,1)S(1)} %collective-permute-done.left_ref, ...), custom_call_target="tpu_custom_call" | custom-call | flops 268435456 | bytes 16777216 | tf_op jit(solution)/shard_map/pallas_call | solution.py:123
  21.2 17.1 %all_to_all.25.pred_ref.ens_ref = bf16[16,16,1664]{2,1,0:T(8,128)(2,1)S(1)} all-to-all(bf16[16,16,1664]{2,1,0:T(8,128)(2,1)S(1)} %get-tuple-element.8), channel_id=1, replica_groups=mesh['z'=16,'core'=2,'y'=4,'x'=4] {'x','y'}, dimensions={0} | all-to-all | bytes 1703936 | tf_op jit(solution)/shard_map/all_to_all | solution.py:328
  38.3 1.3 %shard_map.56 = f32[32,1,1152]{2,1,0:T(1,128)S(1)} custom-call(f32[8,512]{1,0:T(8,128)S(1)} %get-tuple-element.7.side_ref, bf16[16,16,1664]{2,1,0:T(8,128)(2,1)S(1)} %all_to_all.25.pred_ref.ens_ref), custom_call_target="tpu_custom_call" | custom-call | tf_op jit(solution)/shard_map/pallas_call | solution.py:179
  39.7 16.4 %all_to_all.26 = f32[32,1,1152]{2,1,0:T(1,128)S(1)} all-to-all(f32[32,1,1152]{2,1,0:T(1,128)S(1)} %shard_map.56), channel_id=1, replica_groups=mesh['z'=16,'core'=2,'y'=4,'x'=4] {'core','y','x'}, dimensions={0} | all-to-all | bytes 294912 | tf_op jit(solution)/shard_map/all_to_all | solution.py:330
  56.0 0.1 reduce_sum.18
  56.2 20.6 %all_to_all.27 = f32[16,1,1152]{2,1,0:T(1,128)S(1)} all-to-all(f32[16,1,1152]{2,1,0:T(1,128)S(1)} %broadcast_in_dim.4), channel_id=1, replica_groups=mesh['z'=16,'core'=2,'y'=4,'x'=4] {'z'}, dimensions={0} | all-to-all | bytes 147456 | tf_op jit(solution)/shard_map/all_to_all | solution.py:307
  76.8 0.1 reduce_sum.19
  76.9 0.1 broadcast_in_dim.5
  76.9 13.0 %all_to_all.28.gram_ref = f32[32,1,1152]{2,1,0:T(1,128)S(1)} all-to-all(f32[32,1,1152]{2,1,0:T(1,128)S(1)} %broadcast_in_dim.5), channel_id=1, replica_groups=mesh['z'=16,'core'=2,'y'=4,'x'=4] {'core','y','x'}, dimensions={0} | all-to-all | bytes 294912 | tf_op jit(solution)/shard_map/all_to_all | solution.py:307
  90.0 8.5 %shard_map.57 = bf16[16,16,1024]{2,1,0:T(8,128)(2,1)S(1)} custom-call(f32[32,1,1152]{2,1,0:T(1,128)S(1)} %all_to_all.28.gram_ref, bf16[16,16,1664]{2,1,0:T(8,128)(2,1)S(1)} %all_to_all.25.pred_ref.ens_ref), custom_call_target="tpu_custom_call" | custom-call | tf_op jit(solution)/shard_map/pallas_call | solution.py:298
  98.5 13.3 %all_to_all.29 = bf16[16,16,1024]{2,1,0:T(8,128)(2,1)S(1)} all-to-all(bf16[16,16,1024]{2,1,0:T(8,128)(2,1)S(1)} %shard_map.57), channel_id=1, replica_groups=mesh['z'=16,'core'=2,'y'=4,'x'=4] {'x','y'}, dimensions={0} | all-to-all | bytes 1048576 | tf_op jit(solution)/shard_map/all_to_all | solution.py:333
  111.8 0.8 copy.22
  (2 shorter events, 0.1 us)
Async XLA Ops:
  0.7 9.6 %collective-permute-start.1 = (bf16[16,128]{1,0:T(8,128)(2,1)S(1)}, bf16[16,128]{1,0:T(8,128)(2,1)S(1)}, u32[]{:S(2)}, u32[]{:S(2)}) collective-permute-start(bf16[16,128]{1,0:T(8,128)(2,1)S(1)} %get-tuple-element.9), channel_id=1, source_target_pairs={{16,0},{32,16},{48,32},{64,48},{80,64},{96,80},{112,96},{128,112},... | collective-permute-start | bytes 12296 | tf_op jit(solution)/shard_map/ppermute | solution.py:320
  7.6 4.2 %collective-permute-start = (bf16[16,128]{1,0:T(8,128)(2,1)S(1)}, bf16[16,128]{1,0:T(8,128)(2,1)S(1)}, u32[]{:S(2)}, u32[]{:S(2)}) collective-permute-start(bf16[16,128]{1,0:T(8,128)(2,1)S(1)} %get-tuple-element.10), channel_id=1, source_target_pairs={{0,16},{16,32},{32,48},{48,64},{64,80},{80,96},{96,112},{112,128},... | collective-permute-start | bytes 12296 | tf_op jit(solution)/shard_map/ppermute | solution.py:319

commit v10 on v9

--- a/solution.py
+++ b/solution.py
@@ -16,12 +16,6 @@
 PLANE = ("core", "y", "x")
 MEMBER = ("y", "x")
 SPACE = ("z", "core")
-EXCHANGE = ("x", "y")
-
-
-def turned(count):
-    side = math.isqrt(count)
-    return [i % side * side + i // side for i in range(count)]
 
 
 def predict_kernel(
@@ -101,9 +95,8 @@
     multiply(0)
     lost = lax.fori_loop(1, parts, body, jnp.zeros((members, 128), F32))
     lost = jnp.sum(split(parts - 1, raw[(parts - 1) % 2], lost), axis=1, keepdims=True)
-    place, edge = place_ref[0], math.isqrt(parts)
-    mine = lax.rem(place, edge) * edge + lax.div(place, edge)
-    member = lax.broadcasted_iota(jnp.int32, (members, width), 0) + mine * members
+    place = place_ref[0]
+    member = lax.broadcasted_iota(jnp.int32, (members, width), 0) + place * members
     own = member == lax.broadcasted_iota(jnp.int32, (members, width), 1)
     side_ref[...] = jnp.zeros(side_ref.shape, F32)
     side_ref[2:3, :] = jnp.sum(jnp.where(own, lost, 0.0), axis=0, keepdims=True)
@@ -146,7 +139,7 @@
     half = total // 2
     width = side_ref.shape[1]
     group = width // 128
-    given = jnp.concatenate([pred_ref[s : s + 1, :, : width + 128] for s in turned(pred_ref.shape[0])], axis=0).astype(F32)
+    given = pred_ref[:, :, : width + 128].astype(F32)
     parts = given[:, :, width:]
     means = parts[:, :group] + parts[:, group : 2 * group] + parts[:, 2 * group : 3 * group]
     means = jnp.concatenate([means[:, o : o + 1] for o in range(group)], axis=2)
@@ -246,9 +239,8 @@
 def transform_kernel(gram_ref, ens_ref, out_ref, packed):
     total = 8 * gram_ref.shape[0]
     half = total // 2
-    places = turned(out_ref.shape[0])
     first_row = ens_ref.shape[2] - out_ref.shape[2]
-    states = jnp.concatenate([ens_ref[s, :, first_row:] for s in places], axis=0).astype(F32)
+    states = ens_ref[:, :, first_row:].astype(F32).reshape(total, -1)
     mean_state = jnp.sum(states, axis=0, keepdims=True) / total
     anomalies = (states - mean_state).astype(BF16)
     row = lax.broadcasted_iota(jnp.int32, (total, total), 0)
@@ -287,10 +279,7 @@
         weight = weight + jnp.sum(blocks[s] * solved, axis=0, keepdims=True)
     transposed = (jnp.concatenate(blocks, axis=0) + weight).astype(BF16)
     change = jnp.dot(transposed, anomalies, preferred_element_type=F32)
-    result = (mean_state + change).astype(BF16)
-    members = out_ref.shape[1]
-    for i, s in enumerate(places):
-        out_ref[s] = result[members * i : members * (i + 1)]
+    out_ref[...] = (mean_state + change).astype(BF16).reshape(out_ref.shape)
 
 
 def transform(gram_sum, shared, width):
@@ -323,14 +312,14 @@
     cols = jnp.mod(block_columns - space_index * state_local + 1, state_local * space_count)
     inverse = 1.0 / (error_scale * math.sqrt(total - 1))
     scaled, inverse = (observed * inverse).reshape(-1, 128), inverse.reshape(-1, 128)
-    place = lax.axis_index(EXCHANGE).astype(jnp.int32).reshape(1)
+    place = lax.axis_index(MEMBER).astype(jnp.int32).reshape(1)
     shared, side = predict(place, cols, state, left, right, scaled, inverse, operator_blocks, member_count)
-    shared = lax.all_to_all(shared, EXCHANGE, 0, 0, tiled=True)
+    shared = lax.all_to_all(shared, MEMBER, 0, 0, tiled=True)
     part = gram(side, shared)
     part = jnp.sum(lax.all_to_all(part, PLANE, 0, 0, tiled=True), axis=0)
     part = jnp.sum(to_all(part, "z", z_count), axis=0)
     gram_sum = to_all(part, PLANE, plane_count).reshape(plane_count, 1, -1)
-    analysis = lax.all_to_all(transform(gram_sum, shared, rows // member_count), EXCHANGE, 0, 0, tiled=True)
+    analysis = lax.all_to_all(transform(gram_sum, shared, rows // member_count), MEMBER, 0, 0, tiled=True)
     return analysis.transpose(1, 0, 2).reshape(members, rows).T
 
 

time: 113 us -> 113 us (level)
    all_to_all x2, blocking collectives: 30.4 us -> 31.7 us  [the longest x1 18 us: local(): shared = lax.all_to_all(shared, MEMBER, 0, 0, tiled=True)]
    all_to_all x1, blocking collectives: 16.4 us -> 15.2 us  [local(): part = jnp.sum(lax.all_to_all(part, PLANE, 0, 0, tiled=True), axis=0)]
where the time goes in v10:
time: 113 us
  blocking collectives  80.4 us (71%)
  Pallas kernels  19.2 us (17%)
  starting transfers between devices  6.88 us (6%)
  local copies, waits for them, and re-layouts  2.82 us (2%)
  other arithmetic  1.65 us (1%)
  waiting for transfers between devices  1.52 us (1%)
    all_to_all x2, blocking collectives, to_all(): lax.all_to_all(jnp.broadcast_to(x[None], (count,) + x.shape), axes, 0, 0,...  33.5 us
    all_to_all x1, blocking collectives, local(): shared = lax.all_to_all(shared, MEMBER, 0, 0, tiled=True)  18 us
    all_to_all x1, blocking collectives, local(): part = jnp.sum(lax.all_to_all(part, PLANE, 0, 0, tiled=True), axis=0)  15.2 us
    all_to_all x1, blocking collectives, local(): lax.all_to_all(transform(gram_sum, shared, rows // member_count), MEMBER,...  13.7 us
    pallas_call x1, Pallas kernels, predict(): pl.pallas_call(predict_kernel, out_shape=[jax.ShapeDtypeStruct((parts, me...  9.4 us
    pallas_call x1, Pallas kernels, transform(): pl.pallas_call(transform_kernel, out_shape=jax.ShapeDtypeStruct((sources,...  8.48 us
    ppermute x1, starting transfers between devices, local(): lax.ppermute(ens_t[:, :128], SPACE, [((i + 1) % space_count, i) for i in...  6.88 us
  transfers between devices with their start and end apart: 2, of which 1 were waited for; matrix products, arithmetic and copies ran while one was open for 2% of the time, Pallas kernels for 0%

profile of v10, /device:TPU:1, one launch (start us, length us, event | category | flops | bytes accessed | tf_op | source)
XLA Modules:
  0.0 112.5 jit_solution(13146458557226742998)
XLA Ops:
  0.0 0.7 fusion.2
  0.7 6.9 %collective-permute-start.1 = (bf16[16,128]{1,0:T(8,128)(2,1)S(1)}, bf16[16,128]{1,0:T(8,128)(2,1)S(1)}, u32[]{:S(2)}, u32[]{:S(2)}) collective-permute-start(bf16[16,128]{1,0:T(8,128)(2,1)S(1)} %get-tuple-element.9), channel_id=1, source_target_pairs={{16,0},{32,16},{48,32},{64,48},{80,64},{96,80},{112,96},{128,112},... | collective-permute-start | bytes 12296 | tf_op jit(solution)/shard_map/ppermute | solution.py:309
  7.6 0.0 collective-permute-start
  7.6 0.7 broadcast_subtract_fusion
  8.3 0.1 copy.18
  8.4 0.8 fusion.1
  9.2 1.1 pad.4.state
  10.3 0.0 collective-permute-done.1.right_ref
  10.3 1.5 %collective-permute-done.left_ref = bf16[16,128]{1,0:T(8,128)(2,1)S(1)} collective-permute-done((bf16[16,128]{1,0:T(8,128)(2,1)S(1)}, bf16[16,128]{1,0:T(8,128)(2,1)S(1)}, u32[]{:S(2)}, u32[]{:S(2)}) %collective-permute-start) | collective-permute-done | bytes 4128 | tf_op jit(solution)/shard_map/ppermute | solution.py:308
  11.8 9.4 %shard_map.55 = (bf16[16,16,1664]{2,1,0:T(8,128)(2,1)S(1)}, f32[8,512]{1,0:T(8,128)S(1)}) custom-call(s32[1]{0:T(128)} %bitcast.place_ref, s32[64,8]{1,0:T(8,128)S(1)} %add_select_fusion.cols_ref, bf16[16,16640]{1,0:T(8,128)(2,1)S(1)} %pad.4.state, bf16[16,128]{1,0:T(8,128)(2,1)S(1)} %collective-permute-done.left_ref, ...), custom_call_target="tpu_custom_call" | custom-call | flops 268435456 | bytes 16777216 | tf_op jit(solution)/shard_map/pallas_call | solution.py:116
  21.2 18.0 %all_to_all.25.pred_ref.ens_ref = bf16[16,16,1664]{2,1,0:T(8,128)(2,1)S(1)} all-to-all(bf16[16,16,1664]{2,1,0:T(8,128)(2,1)S(1)} %get-tuple-element.8), channel_id=1, replica_groups=mesh['z'=16,'core'=2,'y'=4,'x'=4] {'y','x'}, dimensions={0} | all-to-all | bytes 1703936 | tf_op jit(solution)/shard_map/all_to_all | solution.py:317
  39.2 1.3 %shard_map.56 = f32[32,1,1152]{2,1,0:T(1,128)S(1)} custom-call(f32[8,512]{1,0:T(8,128)S(1)} %get-tuple-element.7.side_ref, bf16[16,16,1664]{2,1,0:T(8,128)(2,1)S(1)} %all_to_all.25.pred_ref.ens_ref), custom_call_target="tpu_custom_call" | custom-call | tf_op jit(solution)/shard_map/pallas_call | solution.py:172
  40.6 15.2 %all_to_all.26 = f32[32,1,1152]{2,1,0:T(1,128)S(1)} all-to-all(f32[32,1,1152]{2,1,0:T(1,128)S(1)} %shard_map.56), channel_id=1, replica_groups=mesh['z'=16,'core'=2,'y'=4,'x'=4] {'core','y','x'}, dimensions={0} | all-to-all | bytes 294912 | tf_op jit(solution)/shard_map/all_to_all | solution.py:319
  55.8 0.1 reduce_sum.18
  55.9 20.5 %all_to_all.27 = f32[16,1,1152]{2,1,0:T(1,128)S(1)} all-to-all(f32[16,1,1152]{2,1,0:T(1,128)S(1)} %broadcast_in_dim.4), channel_id=1, replica_groups=mesh['z'=16,'core'=2,'y'=4,'x'=4] {'z'}, dimensions={0} | all-to-all | bytes 147456 | tf_op jit(solution)/shard_map/all_to_all | solution.py:296
  76.4 0.1 reduce_sum.19
  76.5 0.1 broadcast_in_dim.5
  76.5 13.0 %all_to_all.28.gram_ref = f32[32,1,1152]{2,1,0:T(1,128)S(1)} all-to-all(f32[32,1,1152]{2,1,0:T(1,128)S(1)} %broadcast_in_dim.5), channel_id=1, replica_groups=mesh['z'=16,'core'=2,'y'=4,'x'=4] {'core','y','x'}, dimensions={0} | all-to-all | bytes 294912 | tf_op jit(solution)/shard_map/all_to_all | solution.py:296
  89.6 8.5 %shard_map.57 = bf16[16,16,1024]{2,1,0:T(8,128)(2,1)S(1)} custom-call(f32[32,1,1152]{2,1,0:T(1,128)S(1)} %all_to_all.28.gram_ref, bf16[16,16,1664]{2,1,0:T(8,128)(2,1)S(1)} %all_to_all.25.pred_ref.ens_ref), custom_call_target="tpu_custom_call" | custom-call | tf_op jit(solution)/shard_map/pallas_call | solution.py:287
  98.1 13.7 %all_to_all.29 = bf16[16,16,1024]{2,1,0:T(8,128)(2,1)S(1)} all-to-all(bf16[16,16,1024]{2,1,0:T(8,128)(2,1)S(1)} %shard_map.57), channel_id=1, replica_groups=mesh['z'=16,'core'=2,'y'=4,'x'=4] {'y','x'}, dimensions={0} | all-to-all | bytes 1048576 | tf_op jit(solution)/shard_map/all_to_all | solution.py:322
  111.7 0.8 copy.22
  (2 shorter events, 0.1 us)
Async XLA Ops:
  0.7 9.6 %collective-permute-start.1 = (bf16[16,128]{1,0:T(8,128)(2,1)S(1)}, bf16[16,128]{1,0:T(8,128)(2,1)S(1)}, u32[]{:S(2)}, u32[]{:S(2)}) collective-permute-start(bf16[16,128]{1,0:T(8,128)(2,1)S(1)} %get-tuple-element.9), channel_id=1, source_target_pairs={{16,0},{32,16},{48,32},{64,48},{80,64},{96,80},{112,96},{128,112},... | collective-permute-start | bytes 12296 | tf_op jit(solution)/shard_map/ppermute | solution.py:309
  7.6 4.2 %collective-permute-start = (bf16[16,128]{1,0:T(8,128)(2,1)S(1)}, bf16[16,128]{1,0:T(8,128)(2,1)S(1)}, u32[]{:S(2)}, u32[]{:S(2)}) collective-permute-start(bf16[16,128]{1,0:T(8,128)(2,1)S(1)} %get-tuple-element.10), channel_id=1, source_target_pairs={{0,16},{16,32},{32,48},{48,64},{64,80},{80,96},{96,112},{112,128},... | collective-permute-start | bytes 12296 | tf_op jit(solution)/shard_map/ppermute | solution.py:308

commit v11 on v9

--- a/solution.py
+++ b/solution.py
@@ -25,7 +25,7 @@
 
 
 def predict_kernel(
-    place_ref, cols_ref, state, left_ref, right_ref, scaled_ref, inverse_ref, ops_ref, out_ref, side_ref,
+    place_ref, cols_ref, state, right_ref, left_ref, scaled_ref, inverse_ref, ops_ref, out_ref, side_ref,
     weights, raw, staged, sems, out_sems, ens_sems,
 ):
     parts = out_ref.shape[0]
@@ -138,7 +138,7 @@
         ],
         compiler_params=pltpu.CompilerParams(vmem_limit_bytes=50 * 2**20),
         cost_estimate=pl.CostEstimate(flops=2 * ops.size * members, bytes_accessed=2 * ops.size, transcendentals=0),
-    )(place, cols, state, left, right, scaled, inverse, ops)
+    )(place, cols, state, right, left, scaled, inverse, ops)
 
 
 def gram_kernel(side_ref, pred_ref, out_ref):

time: 113 us -> 113 us (level)
  blocking collectives: 80.4 us -> 82 us
  waiting for transfers between devices: 1.52 us -> 0.01 us
    all_to_all x1, blocking collectives: 17.1 us -> 13.5 us  [local(): shared = lax.all_to_all(shared, EXCHANGE, 0, 0, tiled=True)]
    all_to_all x1, blocking collectives: 16.4 us -> 19.7 us  [local(): part = jnp.sum(lax.all_to_all(part, PLANE, 0, 0, tiled=True), axis=0)]
    ppermute x1, starting transfers between devices: 6.88 us -> 3.85 us  [local(): lax.ppermute(ens_t[:, :128], SPACE, [((i + 1) % space_count, i) for i in...]
    ppermute x1, starting transfers between devices: 0.01 us -> 3.03 us  [local(): lax.ppermute(ens_t[:, -128:], SPACE, [(i, (i + 1) % space_count) for i in...]
    all_to_all x2, blocking collectives: 33.6 us -> 35.5 us  [to_all(): lax.all_to_all(jnp.broadcast_to(x[None], (count,) + x.shape), axes, 0, 0,...]
    ppermute x1, waiting for transfers between devices: 1.52 us -> 0.01 us  [local(): lax.ppermute(ens_t[:, -128:], SPACE, [(i, (i + 1) % space_count) for i in...]
  transfers between devices with their start and end apart: 2 -> 2, of which waited for: 1 -> 0; matrix products, arithmetic and copies ran while one was open for 2% -> 2% of each run, Pallas kernels for 0% -> 0%
where the time goes in v11:
time: 113 us
  blocking collectives  82 us (73%)
  Pallas kernels  19.2 us (17%)
  starting transfers between devices  6.88 us (6%)
  local copies, waits for them, and re-layouts  2.82 us (2%)
  other arithmetic  1.65 us (1%)
    all_to_all x2, blocking collectives, to_all(): lax.all_to_all(jnp.broadcast_to(x[None], (count,) + x.shape), axes, 0, 0,...  35.5 us
    all_to_all x1, blocking collectives, local(): part = jnp.sum(lax.all_to_all(part, PLANE, 0, 0, tiled=True), axis=0)  19.7 us
    all_to_all x1, blocking collectives, local(): shared = lax.all_to_all(shared, EXCHANGE, 0, 0, tiled=True)  13.5 us
    all_to_all x1, blocking collectives, local(): lax.all_to_all(transform(gram_sum, shared, rows // member_count), EXCHANG...  13.3 us
    pallas_call x1, Pallas kernels, predict(): pl.pallas_call(predict_kernel, out_shape=[jax.ShapeDtypeStruct((parts, me...  9.41 us
    pallas_call x1, Pallas kernels, transform(): pl.pallas_call(transform_kernel, out_shape=jax.ShapeDtypeStruct((sources,...  8.5 us
    ppermute x1, starting transfers between devices, local(): lax.ppermute(ens_t[:, :128], SPACE, [((i + 1) % space_count, i) for i in...  3.85 us
    ppermute x1, starting transfers between devices, local(): lax.ppermute(ens_t[:, -128:], SPACE, [(i, (i + 1) % space_count) for i in...  3.03 us
  transfers between devices with their start and end apart: 2, of which 0 were waited for; matrix products, arithmetic and copies ran while one was open for 2% of the time, Pallas kernels for 0%

profile of v11, /device:TPU:1, one launch (start us, length us, event | category | flops | bytes accessed | tf_op | source)
XLA Modules:
  0.0 112.7 jit_solution(2138420234748841177)
XLA Ops:
  0.0 0.7 fusion.2
  0.7 3.0 %collective-permute-start.1 = (bf16[16,128]{1,0:T(8,128)(2,1)S(1)}, bf16[16,128]{1,0:T(8,128)(2,1)S(1)}, u32[]{:S(2)}, u32[]{:S(2)}) collective-permute-start(bf16[16,128]{1,0:T(8,128)(2,1)S(1)} %get-tuple-element.9), channel_id=1, source_target_pairs={{0,16},{16,32},{32,48},{48,64},{64,80},{80,96},{96,112},{112,128},... | collective-permute-start | bytes 12296 | tf_op jit(solution)/shard_map/ppermute | solution.py:319
  3.7 3.9 %collective-permute-start = (bf16[16,128]{1,0:T(8,128)(2,1)S(1)}, bf16[16,128]{1,0:T(8,128)(2,1)S(1)}, u32[]{:S(2)}, u32[]{:S(2)}) collective-permute-start(bf16[16,128]{1,0:T(8,128)(2,1)S(1)} %get-tuple-element.10), channel_id=1, source_target_pairs={{16,0},{32,16},{48,32},{64,48},{80,64},{96,80},{112,96},{128,112},... | collective-permute-start | bytes 12296 | tf_op jit(solution)/shard_map/ppermute | solution.py:320
  7.6 0.7 broadcast_subtract_fusion
  8.3 0.1 copy.18
  8.4 0.8 fusion.1
  9.2 1.1 pad.4.state
  10.3 0.0 collective-permute-done.1.left_ref
  10.3 0.0 collective-permute-done.right_ref
  10.3 9.4 %shard_map.55 = (bf16[16,16,1664]{2,1,0:T(8,128)(2,1)S(1)}, f32[8,512]{1,0:T(8,128)S(1)}) custom-call(s32[1]{0:T(128)} %bitcast.place_ref, s32[64,8]{1,0:T(8,128)S(1)} %add_select_fusion.cols_ref, bf16[16,16640]{1,0:T(8,128)(2,1)S(1)} %pad.4.state, bf16[16,128]{1,0:T(8,128)(2,1)S(1)} %collective-permute-done.right_ref, ...), custom_call_target="tpu_custom_call" | custom-call | flops 268435456 | bytes 16777216 | tf_op jit(solution)/shard_map/pallas_call | solution.py:123
  19.7 13.5 %all_to_all.25.pred_ref.ens_ref = bf16[16,16,1664]{2,1,0:T(8,128)(2,1)S(1)} all-to-all(bf16[16,16,1664]{2,1,0:T(8,128)(2,1)S(1)} %get-tuple-element.8), channel_id=1, replica_groups=mesh['z'=16,'core'=2,'y'=4,'x'=4] {'x','y'}, dimensions={0} | all-to-all | bytes 1703936 | tf_op jit(solution)/shard_map/all_to_all | solution.py:328
  33.2 1.3 %shard_map.56 = f32[32,1,1152]{2,1,0:T(1,128)S(1)} custom-call(f32[8,512]{1,0:T(8,128)S(1)} %get-tuple-element.7.side_ref, bf16[16,16,1664]{2,1,0:T(8,128)(2,1)S(1)} %all_to_all.25.pred_ref.ens_ref), custom_call_target="tpu_custom_call" | custom-call | tf_op jit(solution)/shard_map/pallas_call | solution.py:179
  34.5 19.7 %all_to_all.26 = f32[32,1,1152]{2,1,0:T(1,128)S(1)} all-to-all(f32[32,1,1152]{2,1,0:T(1,128)S(1)} %shard_map.56), channel_id=1, replica_groups=mesh['z'=16,'core'=2,'y'=4,'x'=4] {'core','y','x'}, dimensions={0} | all-to-all | bytes 294912 | tf_op jit(solution)/shard_map/all_to_all | solution.py:330
  54.3 0.1 reduce_sum.18
  54.4 22.4 %all_to_all.27 = f32[16,1,1152]{2,1,0:T(1,128)S(1)} all-to-all(f32[16,1,1152]{2,1,0:T(1,128)S(1)} %broadcast_in_dim.4), channel_id=1, replica_groups=mesh['z'=16,'core'=2,'y'=4,'x'=4] {'z'}, dimensions={0} | all-to-all | bytes 147456 | tf_op jit(solution)/shard_map/all_to_all | solution.py:307
  76.9 0.1 reduce_sum.19
  76.9 0.1 broadcast_in_dim.5
  77.0 13.0 %all_to_all.28.gram_ref = f32[32,1,1152]{2,1,0:T(1,128)S(1)} all-to-all(f32[32,1,1152]{2,1,0:T(1,128)S(1)} %broadcast_in_dim.5), channel_id=1, replica_groups=mesh['z'=16,'core'=2,'y'=4,'x'=4] {'core','y','x'}, dimensions={0} | all-to-all | bytes 294912 | tf_op jit(solution)/shard_map/all_to_all | solution.py:307
  90.0 8.5 %shard_map.57 = bf16[16,16,1024]{2,1,0:T(8,128)(2,1)S(1)} custom-call(f32[32,1,1152]{2,1,0:T(1,128)S(1)} %all_to_all.28.gram_ref, bf16[16,16,1664]{2,1,0:T(8,128)(2,1)S(1)} %all_to_all.25.pred_ref.ens_ref), custom_call_target="tpu_custom_call" | custom-call | tf_op jit(solution)/shard_map/pallas_call | solution.py:298
  98.5 13.3 %all_to_all.29 = bf16[16,16,1024]{2,1,0:T(8,128)(2,1)S(1)} all-to-all(bf16[16,16,1024]{2,1,0:T(8,128)(2,1)S(1)} %shard_map.57), channel_id=1, replica_groups=mesh['z'=16,'core'=2,'y'=4,'x'=4] {'x','y'}, dimensions={0} | all-to-all | bytes 1048576 | tf_op jit(solution)/shard_map/all_to_all | solution.py:333
  111.8 0.8 copy.22
  (2 shorter events, 0.1 us)
Async XLA Ops:
  0.7 9.6 %collective-permute-start.1 = (bf16[16,128]{1,0:T(8,128)(2,1)S(1)}, bf16[16,128]{1,0:T(8,128)(2,1)S(1)}, u32[]{:S(2)}, u32[]{:S(2)}) collective-permute-start(bf16[16,128]{1,0:T(8,128)(2,1)S(1)} %get-tuple-element.9), channel_id=1, source_target_pairs={{0,16},{16,32},{32,48},{48,64},{64,80},{80,96},{96,112},{112,128},... | collective-permute-start | bytes 12296 | tf_op jit(solution)/shard_map/ppermute | solution.py:319
  3.7 6.6 %collective-permute-start = (bf16[16,128]{1,0:T(8,128)(2,1)S(1)}, bf16[16,128]{1,0:T(8,128)(2,1)S(1)}, u32[]{:S(2)}, u32[]{:S(2)}) collective-permute-start(bf16[16,128]{1,0:T(8,128)(2,1)S(1)} %get-tuple-element.10), channel_id=1, source_target_pairs={{16,0},{32,16},{48,32},{64,48},{80,64},{96,80},{112,96},{128,112},... | collective-permute-start | bytes 12296 | tf_op jit(solution)/shard_map/ppermute | solution.py:320
